TPU v7x, 128 devices: a whole 4x4x4 slice. The times are simulated.
128 devices in a mesh: px: 8 (over x, core), py: 16 (over y, z).
Axes of the slice: x: 4, y: 4, z: 4, core: 2. Of those that a mesh axis runs over, the one named last changes fastest.
Arguments:
- field: float32 [512, 512, 256], P('px', 'py'), may hold values from -6 to 6
- diffusivity: bfloat16 [512, 512, 256], P('px', 'py'), may hold values from 0.049804688 to 1
- velocity: bfloat16 [3, 512, 512, 256], P(None, 'px', 'py'), may hold values from -4 to 4
- margin: int32 [8, 2], P('px'), may hold values from 0 to 4, as said below
Outputs:
- advected: float32 [512, 512, 256], P('px', 'py')
- controls: float32 [256, 256, 128], P('px', 'py')
Inputs may be any that keep to these rules, and one draw needn't show every extreme that they name: One subdomain has an upper margin of 0 and one has a lower margin of 4.
All inputs are finite; a program needn't handle non-finite values.
Results may differ from a plain program's by a relative error of at most 0.0003.
Values may be sent and summed in bfloat16 or wider, within the bound.
No kernel may reach another device: no remote copies, remote signals or barrier semaphores. Data moves between devices by JAX's collectives and lax.ppermute only.
A program may use at most 192 MiB of HBM per device.

v0:
```python
import functools

import jax
import jax.numpy as jnp
import numpy as np
from jax import lax
from jax.experimental import pallas as pl
from jax.experimental.pallas import tpu as pltpu
from jax.sharding import PartitionSpec as P

STEPS = 4
OVMAX = 4
BX = 64
BY = 32
NZ = 256
MZ = 128
W = 4
EX = BX + 2 * W
EY = BY + 2 * W
HIGH = lax.Precision.HIGHEST


def bspline(t):
    m = np.abs(t)
    inner = (4.0 - 6.0 * m * m + 3.0 * m**3) / 6.0
    outer = np.maximum(2.0 - m, 0.0) ** 3 / 6.0
    return np.where(m < 1.0, inner, outer)


def basis(n):
    j = np.arange(n)[:, None]
    k = np.arange(n // 2)[None, :]
    return bspline((j - 2.0 * k - 0.5) / 2.0)


def fit_matrix(n):
    b = basis(n)
    return np.linalg.solve(b.T @ b, b.T)


def y_tables(count):
    total = count * BY
    s = fit_matrix(total)
    own = BY // 2
    diag = np.zeros((count, own, BY))
    up = np.zeros((count, 3, BY))
    down = np.zeros((count, 3, BY))
    couple = np.zeros((count, own, count, 3))
    for q in range(count):
        cols = s[:, q * BY : (q + 1) * BY]
        diag[q] = cols[q * own : (q + 1) * own]
        if q < count - 1:
            below = cols[(q + 1) * own :]
            u, sv, vt = np.linalg.svd(below, full_matrices=False)
            assert sv[3] < 1e-10 * sv[0]
            up[q] = vt[:3]
            left = u[:, :3] * sv[:3]
            for t in range(q + 1, count):
                couple[t, :, q] = left[(t - q - 1) * own : (t - q) * own]
        if q > 0:
            above = cols[: q * own]
            u, sv, vt = np.linalg.svd(above, full_matrices=False)
            assert sv[3] < 1e-10 * sv[0]
            down[q] = vt[:3]
            left = u[:, :3] * sv[:3]
            for t in range(q):
                couple[t, :, q] = left[t * own : (t + 1) * own]
    return [a.astype(np.float32) for a in (diag, up, down, couple.reshape(count, own, count * 3))]


def x_tables(count):
    total = count * BX
    block = BX // 2
    ctrl = total // 2
    b = basis(total)
    g = b.T @ b
    width = block + 2 * OVMAX
    gpad = np.zeros((ctrl + 16, ctrl + 16))
    gpad[8:-8, 8:-8] = g
    inverse = np.zeros((3, OVMAX + 1, OVMAX + 1, block, width))
    band = np.zeros((3, width, width + 6))
    for cls, p in enumerate((0, 1, count - 1)):
        start = p * block
        knots = start - OVMAX + np.arange(width)
        lo = start - OVMAX + 8
        full = gpad[lo : lo + width, lo : lo + width]
        band[cls] = gpad[lo : lo + width, lo - 3 : lo + width + 3]
        for m0 in range(OVMAX + 1):
            for m1 in range(OVMAX + 1):
                inside = (knots >= start - m0) & (knots < start + block + m1) & (knots >= 0) & (knots < ctrl)
                w = inside.astype(np.float64)
                mat = full * w[:, None] * w[None, :] + np.diag(1.0 - w)
                inverse[cls, m0, m1] = (np.linalg.inv(mat) * w[None, :])[OVMAX : OVMAX + block]
    bt = np.zeros((block + 4, BX))
    for r in range(block + 4):
        bt[r] = bspline((np.arange(BX) - 2.0 * (r - 2) - 0.5) / 2.0)
    return inverse.reshape(-1, block, width).astype(np.float32), band.astype(np.float32), bt.astype(np.float32)


def stencil_body(mask_ref, f_ref, k_ref, v_ref, yl_ref, yh_ref, xl_ref, xh_ref, dll_ref, dlh_ref, dhl_ref, dhh_ref,
                 fit_hi_ref, fit_lo_ref, adv_ref, zfit_ref, u_s, v0_s, v1_s, v2_s, kx_s, ky_s, kyd_s, kz_s, kzd_s, c_s):
    f32 = jnp.float32
    from_low_x = mask_ref[0]
    from_high_x = mask_ref[1]
    from_low_y = mask_ref[2]
    from_high_y = mask_ref[3]
    dest = (u_s, c_s, v0_s, v1_s, v2_s)

    def own_planes(group, carry):
        at = group * 4
        ul = yl_ref[BX + group].astype(f32) * from_low_y
        uh = yh_ref[BX + group].astype(f32) * from_high_y
        for i in range(4):
            x = at + i
            kl = yl_ref[x].astype(f32) * from_low_y
            kh = yh_ref[x].astype(f32) * from_high_y
            u_s[x + W, 0:BY] = f_ref[x]
            u_s[x + W, BY:EY] = jnp.concatenate([uh[4 * i : 4 * i + 4], ul[4 * i : 4 * i + 4]], axis=0)
            for n in range(4):
                ref = dest[1 + n]
                ref[x + W, 0:BY] = (k_ref[x] if n == 0 else v_ref[n - 1, x]).astype(f32)
                ref[x + W, BY:EY] = jnp.concatenate([kh[4 * n : 4 * n + 4], kl[4 * n : 4 * n + 4]], axis=0)
        return carry

    lax.fori_loop(0, BX // 4, own_planes, 0)
    for n in range(5):
        for base, ref, below, above, scale in (
            (0, xl_ref, dll_ref, dlh_ref, from_low_x),
            (BX + W, xh_ref, dhl_ref, dhh_ref, from_high_x),
        ):
            low = below[n].astype(f32) * (scale * from_low_y)
            high = above[n].astype(f32) * (scale * from_high_y)
            for i in range(W):
                dest[n][base + i, 0:BY] = ref[n * W + i].astype(f32) * scale
                dest[n][base + i, BY:EY] = jnp.concatenate([high[4 * i : 4 * i + 4], low[4 * i : 4 * i + 4]], axis=0)

    lane = lax.broadcasted_iota(jnp.int32, (EY, 128), 1)
    first = lane == 0
    final = lane == 127

    def z_up(a):
        lo = pltpu.roll(a[:, :128], 1, 1)
        hi = pltpu.roll(a[:, 128:], 1, 1)
        return jnp.concatenate([jnp.where(first, 0.0, lo), jnp.where(first, lo, hi)], axis=1)

    def z_down(a):
        lo = pltpu.roll(a[:, :128], 127, 1)
        hi = pltpu.roll(a[:, 128:], 127, 1)
        return jnp.concatenate([jnp.where(final, hi, lo), jnp.where(final, 0.0, hi)], axis=1)

    def coefficients(x, carry):
        k, kx_low = carry
        k_next = c_s[jnp.minimum(x + 1, EX - 1)]
        kx = 0.05 * (k + k_next)
        ky = 0.05 * (k + pltpu.roll(k, EY - 1, 0))
        kyd = pltpu.roll(ky, 1, 0)
        kz = 0.05 * (k + z_down(k))
        kzd = 0.05 * (k + z_up(k))
        kx_s[x] = kx
        ky_s[x] = ky
        kyd_s[x] = kyd
        kz_s[x] = kz
        kzd_s[x] = kzd
        c_s[x] = 1.0 - ((kx + kx_low) + (ky + kyd) + (kz + kzd))
        return k_next, kx

    lax.fori_loop(0, EX, coefficients, (c_s[0], jnp.zeros((EY, NZ), f32)))

    row = lax.broadcasted_iota(jnp.int32, (EY, NZ), 0)
    row_mask = jnp.where(row < BY, 1.0, jnp.where(row < BY + W, from_high_y, from_low_y))

    for step in range(STEPS):
        lo = step
        hi = EX - 1 - step

        def one_plane(x, carry, step=step):
            partial, up = carry
            u = u_s[x]
            w = 0.025 * u
            g0 = v0_s[x] * w
            g1 = v1_s[x] * w
            g2 = v2_s[x] * w
            done = partial + u * (kx_s[x - 1] - g0)
            prev = x - 1
            plane_mask = jnp.where(prev < W, from_low_x, jnp.where(prev >= BX + W, from_high_x, 1.0))
            u_s[prev] = done * (row_mask * plane_mask)
            up_next = u * (kx_s[x] + g0)
            total = u * c_s[x] + up
            total = total + pltpu.roll(u * (ky_s[x] + g1), 1, 0)
            total = total + pltpu.roll(u * (kyd_s[x] - g1), EY - 1, 0)
            total = total + z_up(u * (kz_s[x] + g2))
            total = total + z_down(u * (kzd_s[x] - g2))
            return total, up_next

        first_u = u_s[lo]
        first_up = first_u * (kx_s[lo] + v0_s[lo] * (0.025 * first_u))
        lax.fori_loop(lo + 1, hi + 1, one_plane, (jnp.zeros((EY, NZ), f32), first_up))

    fit_hi = fit_hi_ref[...]
    fit_lo = fit_lo_ref[...]

    def fit_planes(group, carry):
        at = group * 8
        part = u_s[pl.ds(at + W, 8), 0:BY]
        adv_ref[pl.ds(at, 8)] = part
        flat = part.reshape(8 * BY, NZ)
        flat_hi = flat.astype(jnp.bfloat16)
        flat_lo = (flat - flat_hi.astype(f32)).astype(jnp.bfloat16)
        dot = functools.partial(jnp.dot, preferred_element_type=f32)
        out = dot(flat_hi, fit_hi) + (dot(flat_hi, fit_lo) + dot(flat_lo, fit_hi))
        zfit_ref[pl.ds(at, 8)] = out.reshape(8, BY, MZ)
        return carry

    lax.fori_loop(0, BX // 8, fit_planes, 0)


def time_steps(masks, field, diffusivity, velocity, halos, fit_hi, fit_lo):
    vmem = pl.BlockSpec(memory_space=pltpu.VMEM)
    return pl.pallas_call(
        stencil_body,
        out_shape=(
            jax.ShapeDtypeStruct((BX, BY, NZ), jnp.float32),
            jax.ShapeDtypeStruct((BX, BY, MZ), jnp.float32),
        ),
        in_specs=[pl.BlockSpec(memory_space=pltpu.SMEM)] + [vmem] * 13,
        out_specs=(vmem, vmem),
        scratch_shapes=[pltpu.VMEM((EX, EY, NZ), jnp.float32)] * 10,
        compiler_params=pltpu.CompilerParams(vmem_limit_bytes=60 * 1024 * 1024),
        name="time_steps",
    )(masks, field, diffusivity, velocity, *halos, fit_hi, fit_lo)


def ring(n, d):
    return [(i, (i + d) % n) for i in range(n)]


def shift(a, axis, d):
    return lax.ppermute(a, axis, ring(lax.axis_size(axis), d))


def shift_both(a, dx, dy):
    nx = lax.axis_size("px")
    ny = lax.axis_size("py")
    pairs = [(i * ny + j, ((i + dx) % nx) * ny + (j + dy) % ny) for i in range(nx) for j in range(ny)]
    return lax.ppermute(a, ("px", "py"), pairs)


def halo_parts(field, diffusivity, velocity):
    u = field.astype(jnp.bfloat16)

    def y_face(rows):
        kv = jnp.concatenate([diffusivity[:, rows]] + [velocity[n][:, rows] for n in range(3)], axis=1)
        return jnp.concatenate([kv, u[:, rows].reshape(BX // 4, 16, NZ)], axis=0)

    def x_face(planes):
        return jnp.concatenate([u[planes], diffusivity[planes]] + [velocity[n][planes] for n in range(3)], axis=0)

    def corner(planes, rows):
        return jnp.stack(
            [a[planes, rows].reshape(16, NZ) for a in (u, diffusivity, velocity[0], velocity[1], velocity[2])]
        )

    head = slice(0, W)
    ty = slice(BY - W, BY)
    tx = slice(BX - W, BX)
    yl = shift(y_face(ty), "py", 1)
    yh = shift(y_face(head), "py", -1)
    xl = shift(x_face(tx), "px", 1)
    xh = shift(x_face(head), "px", -1)
    dll = shift_both(corner(tx, ty), 1, 1)
    dlh = shift_both(corner(tx, head), 1, -1)
    dhl = shift_both(corner(head, ty), -1, 1)
    dhh = shift_both(corner(head, head), -1, -1)
    return yl, yh, xl, xh, dll, dlh, dhl, dhh


def mm(a, b):
    return jnp.dot(a, b, precision=HIGH, preferred_element_type=jnp.float32)


def x_operator(margin, tables, p, count):
    inverse, band, bt = tables
    margins = lax.all_gather(margin[0], "px")

    def rows_of(owner):
        own = jnp.clip(owner, 0, count - 1)
        cls = jnp.where(own == 0, 0, jnp.where(own == count - 1, 2, 1))
        m = lax.dynamic_index_in_dim(margins, own, 0, keepdims=False)
        m = jnp.clip(m, 0, OVMAX)
        n = OVMAX + 1
        found = lax.dynamic_index_in_dim(inverse, (cls * n + m[0]) * n + m[1], 0, keepdims=False)
        return found * ((owner >= 0) & (owner < count)).astype(jnp.float32), cls

    inverse = jnp.asarray(inverse)
    e, cls = rows_of(p)
    e_low, _ = rows_of(p - 1)
    e_high, _ = rows_of(p + 1)
    block = BX // 2
    g = lax.dynamic_index_in_dim(jnp.asarray(band), cls, 0, keepdims=False)
    has_low = (p > 0).astype(jnp.float32)
    has_high = (p < count - 1).astype(jnp.float32)
    q = mm(e, g)
    ql = q[:, :7] * has_low
    q0 = q[:, 7 : 7 + block]
    qr = q[:, 7 + block :] * has_high
    a = 2.0 * e - mm(q0, e)
    ql_e = mm(ql, e_low[block - 7 :])
    qr_e = mm(qr, e_high[:7])
    w = a[:, 2 : block + 6]
    w = w - jnp.pad(ql_e[:, block + 2 : block + 8], ((0, 0), (0, block - 2)))
    w = w - jnp.pad(qr_e[:, 0:6], ((0, 0), (block - 2, 0)))
    bt = jnp.asarray(bt)
    full = jnp.concatenate(
        [
            mm(w, bt),
            a[:, 0:6] * has_low,
            -ql,
            a[:, block + 2 :] * has_high,
            -qr,
            -ql_e[:, 0:6] * (p > 1).astype(jnp.float32),
            -qr_e[:, block + 2 :] * (p < count - 2).astype(jnp.float32),
        ],
        axis=1,
    )
    kappa = mm(jnp.concatenate([e[block - 7 :, 2 : block + 6], e[:7, 2 : block + 6]], axis=0), bt)
    send = jnp.concatenate([bt[block - 2 :], kappa[:7], bt[:6], kappa[7:]], axis=0)
    return send, full


def per_device(field, diffusivity, velocity, margin):
    count_x = lax.axis_size("px")
    count_y = lax.axis_size("py")
    p = lax.axis_index("px")
    q = lax.axis_index("py")
    masks = jnp.stack([p > 0, p < count_x - 1, q > 0, q < count_y - 1]).astype(jnp.float32)
    s_z = fit_matrix(NZ).T.astype(np.float32)
    fit_hi = s_z.astype(jnp.bfloat16)
    fit_lo = (s_z - fit_hi.astype(np.float32)).astype(jnp.bfloat16)
    halos = halo_parts(field, diffusivity, velocity)
    send, full = x_operator(margin, x_tables(count_x), p, count_x)
    diag, up, down, couple = [
        lax.dynamic_index_in_dim(jnp.asarray(t), q, 0, keepdims=False) for t in y_tables(count_y)
    ]
    advected, zfit = time_steps(masks, field, diffusivity, velocity, halos, jnp.asarray(fit_hi), jnp.asarray(fit_lo))

    lines = zfit.reshape(BX, BY * MZ)
    out = mm(send, lines)
    from_low = shift(out[:13], "px", 1)
    from_high = shift(out[13:], "px", -1)
    from_low2 = shift(out[:6].astype(jnp.bfloat16), "px", 2)
    from_high2 = shift(out[13:19].astype(jnp.bfloat16), "px", -2)
    stacked = jnp.concatenate(
        [lines, from_low, from_high, from_low2.astype(jnp.float32), from_high2.astype(jnp.float32)], axis=0
    )
    xfit = mm(full, stacked).reshape(BX // 2, BY, MZ)

    both = jnp.einsum("cy,xyz->cxz", jnp.concatenate([up, down], axis=0), xfit, precision=HIGH)
    target = jnp.arange(count_y)[:, None, None, None]
    carries = jnp.where(target > q, both[None, :3], both[None, 3:])
    got = lax.all_to_all(carries, "py", split_axis=0, concat_axis=0, tiled=True)
    controls = jnp.einsum("my,xyz->xmz", diag, xfit, precision=HIGH)
    controls = controls + jnp.einsum(
        "mc,cxz->xmz", couple, got.reshape(count_y * 3, BX // 2, MZ), precision=HIGH
    )
    return advected, controls


def solution(mesh):
    placed = (P("px", "py", None), P("px", "py", None), P(None, "px", "py", None), P("px", None))
    return jax.shard_map(
        per_device,
        mesh=mesh,
        in_specs=placed,
        out_specs=(P("px", "py", None), P("px", "py", None)),
        check_vma=False,
    )
```

profile of v0, /device:TPU:0, one launch (start us, length us, event | category | flops | bytes accessed | tf_op | source)
XLA Modules:
  0.0 151.7 jit_solution(14242732244096495279)
XLA Ops:
  0.6 1.9 %convert_element_type.40 = bf16[64,32,256]{2,1,0:T(8,128)(2,1)S(1)} convert(f32[64,32,256]{2,1,0:T(8,128)} %f_ref.1) | non-fusion elementwise | flops 524288 | bytes 3145728 | tf_op jit(solution)/shard_map/convert_element_type | solution.py:249
  3.3 1.5 %slice_dynamic-update-slice_fusion.2 = (bf16[20,32,256]{2,1,0:T(8,128)(2,1)}, bf16[20,32,256]{2,1,0:T(8,128)(2,1)}) fusion(bf16[20,32,256]{2,1,0:T(8,128)(2,1)} %get-tuple-element.37, bf16[64,32,256]{2,1,0:T(8,128)(2,1)} %k_ref.1, bf16[20,32,256]{2,1,0:T(8,128)(2,1)} %get-tuple-element.38), kind=kLoop, calls=%fused_computation.20 | loop fusion | bytes 262144
  6.8 2.3 %collective-permute-start.3 = (bf16[20,32,256]{2,1,0:T(8,128)(2,1)}, bf16[20,32,256]{2,1,0:T(8,128)(2,1)S(1)}, u32[]{:S(2)}, u32[]{:S(2)}) collective-permute-start(bf16[20,32,256]{2,1,0:T(8,128)(2,1)} %get-tuple-element.6), channel_id=1, source_target_pairs={{0,112},{16,0},{32,16},{48,32},{64,48},{80,64},{96,80},{112,96},{1... | collective-permute-start | bytes 983048 | tf_op jit(solution)/shard_map/ppermute | solution.py:238
  9.9 1.7 %slice_bitcast_fusion.2 = (bf16[64,32,256]{2,1,0:T(8,128)(2,1)}, bf16[64,32,256]{2,1,0:T(8,128)(2,1)}, bf16[64,32,256]{2,1,0:T(8,128)(2,1)}) fusion(bf16[3,64,32,256]{3,2,1,0:T(8,128)(2,1)S(1)} %copy-done), kind=kLoop, calls=%fused_computation.7 | loop fusion | bytes 6291456 | tf_op jit(solution)/shard_map/squeeze | solution.py:252
  13.3 8.9 %collective-permute-start.7 = (bf16[5,16,256]{2,1,0:T(8,128)(2,1)S(1)}, bf16[5,16,256]{2,1,0:T(8,128)(2,1)S(1)}, u32[]{:S(2)}, u32[]{:S(2)}) collective-permute-start(bf16[5,16,256]{2,1,0:T(8,128)(2,1)S(1)} %constant_dynamic-update-slice_fusion.15), channel_id=1, source_target_pairs={{0,127},{1,112},{2,113},{3,114},{4,115},{5,116},{6,117},{7,118},{8... | collective-permute-start | bytes 122888 | tf_op jit(solution)/shard_map/ppermute | solution.py:245
  22.3 1.1 fusion.74
  23.4 1.4 fusion.71
  24.8 1.4 fusion.70
  27.2 5.4 %collective-permute-start.1 = (bf16[80,16,256]{2,1,0:T(8,128)(2,1)S(1)}, bf16[80,16,256]{2,1,0:T(8,128)(2,1)S(1)}, u32[]{:S(2)}, u32[]{:S(2)}) collective-permute-start(bf16[80,16,256]{2,1,0:T(8,128)(2,1)S(1)} %pad_maximum_fusion.1), channel_id=1, source_target_pairs={{0,15},{1,0},{2,1},{3,2},{4,3},{5,4},{6,5},{7,6},{8,7},{9,8},{10,9... | collective-permute-start | bytes 1966088 | tf_op jit(solution)/shard_map/ppermute | solution.py:238
  32.6 7.8 %all-gather = s32[8,1,2]{2,1,0:T(1,128)S(1)} all-gather(s32[1,1,2]{2,1,0:T(1,128)S(1)} %bitcast.91), channel_id=1, replica_groups=mesh['px'=8,'py'=16] {'px'}, dimensions={0}, use_global_device_ids=true | all-gather | bytes 72 | tf_op jit(solution)/shard_map/all_gather | solution.py:283
  47.1 1.0 convolution_subtract_fusion
  51.1 6.7 %collective-permute-done.6.dhl_ref = bf16[5,16,256]{2,1,0:T(8,128)(2,1)S(1)} collective-permute-done((bf16[5,16,256]{2,1,0:T(8,128)(2,1)S(1)}, bf16[5,16,256]{2,1,0:T(8,128)(2,1)S(1)}, u32[]{:S(2)}, u32[]{:S(2)}) %collective-permute-start.6) | collective-permute-done | bytes 40992 | tf_op jit(solution)/shard_map/ppermute | solution.py:245
  58.5 4.8 %collective-permute-done.5.dlh_ref = bf16[5,16,256]{2,1,0:T(8,128)(2,1)S(1)} collective-permute-done((bf16[5,16,256]{2,1,0:T(8,128)(2,1)S(1)}, bf16[5,16,256]{2,1,0:T(8,128)(2,1)S(1)}, u32[]{:S(2)}, u32[]{:S(2)}) %collective-permute-start.5) | collective-permute-done | bytes 40992 | tf_op jit(solution)/shard_map/ppermute | solution.py:245
  64.0 8.2 %collective-permute-done.4.dll_ref = bf16[5,16,256]{2,1,0:T(8,128)(2,1)S(1)} collective-permute-done((bf16[5,16,256]{2,1,0:T(8,128)(2,1)S(1)}, bf16[5,16,256]{2,1,0:T(8,128)(2,1)S(1)}, u32[]{:S(2)}, u32[]{:S(2)}) %collective-permute-start.4) | collective-permute-done | bytes 40992 | tf_op jit(solution)/shard_map/ppermute | solution.py:245
  74.0 42.6 %time_steps.1 = (f32[64,32,256]{2,1,0:T(8,128)}, f32[64,32,128]{2,1,0:T(8,128)}) custom-call(f32[4]{0:T(128)} %add_convert_fusion.mask_ref, f32[64,32,256]{2,1,0:T(8,128)} %f_ref.1, bf16[64,32,256]{2,1,0:T(8,128)(2,1)} %k_ref.1, bf16[3,64,32,256]{3,2,1,0:T(8,128)(2,1)} %v_ref.1, bf16[80,16,256]{2,1,0:T(8,128)(2,1)} %copy-done.3, ...), custom_call_target="tpu_custom_call" | custom-call | tf_op jit(solution)/shard_map/time_steps/pallas_call | solution.py:219
  116.6 2.5 %fusion.83 = (bf16[26,4096]{1,0:T(8,128)(2,1)S(1)}, f32[26,4096]{1,0:T(8,128)S(1)}) fusion(f32[8,8,32,128]{3,2,1,0:T(8,128)} %bitcast.87, f32[7,64]{1,0:T(8,128)S(1)} %get-tuple-element.66, f32[6,64]{1,0:T(8,128)S(1)} %copy-done.11, f32[7,64]{1,0:T(8,128)S(1)} %get-tuple-element.65, f32[6,64]{1,0:T(8,128)S(1)} %copy-done.12), kind=kOutput, calls=%fused_computation.138 | convolution fusion | flops 81900416 | bytes 1694208 | tf_op jit(solution)/shard_map/dot_general | solution.py:278
  119.8 2.0 %collective-permute-start.10 = (bf16[6,4096]{1,0:T(8,128)(2,1)S(1)}, bf16[6,4096]{1,0:T(8,128)(2,1)S(1)}, u32[]{:S(2)}, u32[]{:S(2)}) collective-permute-start(bf16[6,4096]{1,0:T(8,128)(2,1)S(1)} %get-tuple-element.52), channel_id=1, source_target_pairs={{0,32},{16,48},{32,64},{48,80},{64,96},{80,112},{96,0},{112,16},{1... | collective-permute-start | bytes 147464 | tf_op jit(solution)/shard_map/ppermute | solution.py:238
  122.5 2.0 %collective-permute-done.11 = bf16[6,4096]{1,0:T(8,128)(2,1)S(1)} collective-permute-done((bf16[6,4096]{1,0:T(8,128)(2,1)S(1)}, bf16[6,4096]{1,0:T(8,128)(2,1)S(1)}, u32[]{:S(2)}, u32[]{:S(2)}) %collective-permute-start.11) | collective-permute-done | bytes 49184 | tf_op jit(solution)/shard_map/ppermute | solution.py:238
  124.5 1.5 %collective-permute-done.10 = bf16[6,4096]{1,0:T(8,128)(2,1)S(1)} collective-permute-done((bf16[6,4096]{1,0:T(8,128)(2,1)S(1)}, bf16[6,4096]{1,0:T(8,128)(2,1)S(1)}, u32[]{:S(2)}, u32[]{:S(2)}) %collective-permute-start.10) | collective-permute-done | bytes 49184 | tf_op jit(solution)/shard_map/ppermute | solution.py:238
  129.0 1.0 broadcast_select_fusion
  130.0 3.6 %all-to-all-start = ((f32[16,3,32,128]{3,2,1,0:T(8,128)}), f32[16,3,32,128]{3,2,1,0:T(8,128)S(1)}, u32[]{:S(2)}, u32[]{:S(2)}) async-start(f32[16,3,32,128]{3,2,1,0:T(8,128)} %broadcast_select_fusion), calls=%async_computation | async-start | bytes 1572864 | tf_op jit(solution)/shard_map/all_to_all | solution.py:360
  133.6 1.1 fusion.30
  134.7 14.6 %all-to-all-done = f32[16,3,32,128]{3,2,1,0:T(8,128)S(1)} async-done(((f32[16,3,32,128]{3,2,1,0:T(8,128)}), f32[16,3,32,128]{3,2,1,0:T(8,128)S(1)}, u32[]{:S(2)}, u32[]{:S(2)}) %all-to-all-start) | async-done | bytes 786464 | tf_op jit(solution)/shard_map/all_to_all | solution.py:360
  149.3 2.4 %fusion = f32[32,16,128]{2,1,0:T(8,128)} fusion(f32[32,128,16]{1,2,0:T(8,128)S(1)} %fusion.30, f32[48,32,128]{2,1,0:T(8,128)S(1)} %bitcast.90, f32[16,16,48]{2,1,0:T(8,128)} %constant.97.clone, s32[]{:T(128)S(6)} %select_n.58), kind=kOutput, calls=%fused_computation.2 | convolution fusion | flops 37814272 | bytes 1318916 | tf_op jit(solution)/shard_map/mc,cxz->xmz/dot_general | solution.py:362
  (124 shorter events, 19.1 us)
Async XLA Ops:
  0.6 4.2 %copy-start = (bf16[3,64,32,256]{3,2,1,0:T(8,128)(2,1)S(1)}, bf16[3,64,32,256]{3,2,1,0:T(8,128)(2,1)}, u32[]{:S(2)}) copy-start(bf16[3,64,32,256]{3,2,1,0:T(8,128)(2,1)} %v_ref.1) | copy-start | bytes 9437188
  2.5 7.3 %copy-start.2 = (bf16[64,32,256]{2,1,0:T(8,128)(2,1)}, bf16[64,32,256]{2,1,0:T(8,128)(2,1)S(1)}, u32[]{:S(2)}) copy-start(bf16[64,32,256]{2,1,0:T(8,128)(2,1)S(1)} %convert_element_type.40) | copy-start | bytes 3145732
  6.8 65.4 %collective-permute-start.3 = (bf16[20,32,256]{2,1,0:T(8,128)(2,1)}, bf16[20,32,256]{2,1,0:T(8,128)(2,1)S(1)}, u32[]{:S(2)}, u32[]{:S(2)}) collective-permute-start(bf16[20,32,256]{2,1,0:T(8,128)(2,1)} %get-tuple-element.6), channel_id=1, source_target_pairs={{0,112},{16,0},{32,16},{48,32},{64,48},{80,64},{96,80},{112,96},{1... | collective-permute-start | bytes 983048 | tf_op jit(solution)/shard_map/ppermute | solution.py:238
  9.0 63.2 %collective-permute-start.2 = (bf16[20,32,256]{2,1,0:T(8,128)(2,1)}, bf16[20,32,256]{2,1,0:T(8,128)(2,1)}, u32[]{:S(2)}, u32[]{:S(2)}) collective-permute-start(bf16[20,32,256]{2,1,0:T(8,128)(2,1)} %get-tuple-element.7), channel_id=1, source_target_pairs={{0,16},{16,32},{32,48},{48,64},{64,80},{80,96},{96,112},{112,0},{1... | collective-permute-start | bytes 983048 | tf_op jit(solution)/shard_map/ppermute | solution.py:238
  13.3 37.6 %collective-permute-start.7 = (bf16[5,16,256]{2,1,0:T(8,128)(2,1)S(1)}, bf16[5,16,256]{2,1,0:T(8,128)(2,1)S(1)}, u32[]{:S(2)}, u32[]{:S(2)}) collective-permute-start(bf16[5,16,256]{2,1,0:T(8,128)(2,1)S(1)} %constant_dynamic-update-slice_fusion.15), channel_id=1, source_target_pairs={{0,127},{1,112},{2,113},{3,114},{4,115},{5,116},{6,117},{7,118},{8... | collective-permute-start | bytes 122888 | tf_op jit(solution)/shard_map/ppermute | solution.py:245
  26.3 6.4 %copy-start.13 = (s32[1,2]{1,0:T(1,128)S(1)}, s32[1,2]{1,0:T(1,128)}, u32[]{:S(2)}) copy-start(s32[1,2]{1,0:T(1,128)} %param.16) | copy-start | bytes 28
  26.7 23.8 %copy-start.6 = (f32[36,64]{1,0:T(8,128)S(1)}, f32[36,64]{1,0:T(8,128)}, u32[]{:S(2)}) copy-start(f32[36,64]{1,0:T(8,128)} %constant.93.clone) | copy-start | bytes 27652
  26.7 45.5 %collective-permute-start = (bf16[80,16,256]{2,1,0:T(8,128)(2,1)S(1)}, bf16[80,16,256]{2,1,0:T(8,128)(2,1)S(1)}, u32[]{:S(2)}, u32[]{:S(2)}) collective-permute-start(bf16[80,16,256]{2,1,0:T(8,128)(2,1)S(1)} %pad_maximum_fusion), channel_id=1, source_target_pairs={{0,1},{1,2},{2,3},{3,4},{4,5},{5,6},{6,7},{7,8},{8,9},{9,10},{10,1... | collective-permute-start | bytes 1966088 | tf_op jit(solution)/shard_map/ppermute | solution.py:238
  27.2 45.0 %collective-permute-start.1 = (bf16[80,16,256]{2,1,0:T(8,128)(2,1)S(1)}, bf16[80,16,256]{2,1,0:T(8,128)(2,1)S(1)}, u32[]{:S(2)}, u32[]{:S(2)}) collective-permute-start(bf16[80,16,256]{2,1,0:T(8,128)(2,1)S(1)} %pad_maximum_fusion.1), channel_id=1, source_target_pairs={{0,15},{1,0},{2,1},{3,2},{4,3},{5,4},{6,5},{7,6},{8,7},{9,8},{10,9... | collective-permute-start | bytes 1966088 | tf_op jit(solution)/shard_map/ppermute | solution.py:238
  51.0 21.3 %copy-start.7 = (bf16[5,16,256]{2,1,0:T(8,128)(2,1)}, bf16[5,16,256]{2,1,0:T(8,128)(2,1)S(1)}, u32[]{:S(2)}) copy-start(bf16[5,16,256]{2,1,0:T(8,128)(2,1)S(1)} %collective-permute-done.7.dhh_ref) | copy-start | bytes 122884
  51.0 6.8 %collective-permute-start.6 = (bf16[5,16,256]{2,1,0:T(8,128)(2,1)S(1)}, bf16[5,16,256]{2,1,0:T(8,128)(2,1)S(1)}, u32[]{:S(2)}, u32[]{:S(2)}) collective-permute-start(bf16[5,16,256]{2,1,0:T(8,128)(2,1)S(1)} %constant_dynamic-update-slice_fusion.10), channel_id=1, source_target_pairs={{0,113},{1,114},{2,115},{3,116},{4,117},{5,118},{6,119},{7,120},{8... | collective-permute-start | bytes 122888 | tf_op jit(solution)/shard_map/ppermute | solution.py:245
  57.8 14.5 %copy-start.8 = (bf16[5,16,256]{2,1,0:T(8,128)(2,1)}, bf16[5,16,256]{2,1,0:T(8,128)(2,1)S(1)}, u32[]{:S(2)}) copy-start(bf16[5,16,256]{2,1,0:T(8,128)(2,1)S(1)} %collective-permute-done.6.dhl_ref) | copy-start | bytes 122884
  57.8 5.5 %collective-permute-start.5 = (bf16[5,16,256]{2,1,0:T(8,128)(2,1)S(1)}, bf16[5,16,256]{2,1,0:T(8,128)(2,1)S(1)}, u32[]{:S(2)}, u32[]{:S(2)}) collective-permute-start(bf16[5,16,256]{2,1,0:T(8,128)(2,1)S(1)} %constant_dynamic-update-slice_fusion.5), channel_id=1, source_target_pairs={{0,31},{1,16},{2,17},{3,18},{4,19},{5,20},{6,21},{7,22},{8,23},{9,... | collective-permute-start | bytes 122888 | tf_op jit(solution)/shard_map/ppermute | solution.py:245
  63.3 8.9 %copy-start.9 = (bf16[5,16,256]{2,1,0:T(8,128)(2,1)}, bf16[5,16,256]{2,1,0:T(8,128)(2,1)S(1)}, u32[]{:S(2)}) copy-start(bf16[5,16,256]{2,1,0:T(8,128)(2,1)S(1)} %collective-permute-done.5.dlh_ref) | copy-start | bytes 122884
  63.3 8.9 %collective-permute-start.4 = (bf16[5,16,256]{2,1,0:T(8,128)(2,1)S(1)}, bf16[5,16,256]{2,1,0:T(8,128)(2,1)S(1)}, u32[]{:S(2)}, u32[]{:S(2)}) collective-permute-start(bf16[5,16,256]{2,1,0:T(8,128)(2,1)S(1)} %constant_dynamic-update-slice_fusion), channel_id=1, source_target_pairs={{0,17},{1,18},{2,19},{3,20},{4,21},{5,22},{6,23},{7,24},{8,25},{9,... | collective-permute-start | bytes 122888 | tf_op jit(solution)/shard_map/ppermute | solution.py:245
  64.0 52.6 %copy-start.11 = (f32[6,64]{1,0:T(8,128)S(1)}, f32[6,64]{1,0:T(8,128)}, u32[]{:S(2)}) copy-start(f32[6,64]{1,0:T(8,128)} %constant.106) | copy-start | bytes 4612
  64.0 52.6 %copy-start.12 = (f32[6,64]{1,0:T(8,128)S(1)}, f32[6,64]{1,0:T(8,128)}, u32[]{:S(2)}) copy-start(f32[6,64]{1,0:T(8,128)} %constant.105) | copy-start | bytes 4612
  72.2 0.9 copy-start.3
  116.6 5.3 %copy-start.1 = (f32[64,32,128]{2,1,0:T(8,128)S(1)}, f32[64,32,128]{2,1,0:T(8,128)}, u32[]{:S(2)}) copy-start(f32[64,32,128]{2,1,0:T(8,128)} %get-tuple-element.5) | copy-start | bytes 3145732
  119.2 6.9 %collective-permute-start.9 = (f32[13,4096]{1,0:T(8,128)S(1)}, f32[13,4096]{1,0:T(8,128)S(1)}, u32[]{:S(2)}, u32[]{:S(2)}) collective-permute-start(f32[13,4096]{1,0:T(8,128)S(1)} %get-tuple-element.49), channel_id=1, source_target_pairs={{0,112},{16,0},{32,16},{48,32},{64,48},{80,64},{96,80},{112,96},{1... | collective-permute-start | bytes 638984 | tf_op jit(solution)/shard_map/ppermute | solution.py:238
  119.2 7.7 %collective-permute-start.8 = (f32[13,4096]{1,0:T(8,128)S(1)}, f32[13,4096]{1,0:T(8,128)S(1)}, u32[]{:S(2)}, u32[]{:S(2)}) collective-permute-start(f32[13,4096]{1,0:T(8,128)S(1)} %get-tuple-element.50), channel_id=1, source_target_pairs={{0,16},{16,32},{32,48},{48,64},{64,80},{80,96},{96,112},{112,0},{1... | collective-permute-start | bytes 638984 | tf_op jit(solution)/shard_map/ppermute | solution.py:238
  119.7 4.8 %collective-permute-start.11 = (bf16[6,4096]{1,0:T(8,128)(2,1)S(1)}, bf16[6,4096]{1,0:T(8,128)(2,1)S(1)}, u32[]{:S(2)}, u32[]{:S(2)}) collective-permute-start(bf16[6,4096]{1,0:T(8,128)(2,1)S(1)} %get-tuple-element.51), channel_id=1, source_target_pairs={{0,96},{16,112},{32,0},{48,16},{64,32},{80,48},{96,64},{112,80},{1... | collective-permute-start | bytes 147464 | tf_op jit(solution)/shard_map/ppermute | solution.py:238
  119.8 6.3 %collective-permute-start.10 = (bf16[6,4096]{1,0:T(8,128)(2,1)S(1)}, bf16[6,4096]{1,0:T(8,128)(2,1)S(1)}, u32[]{:S(2)}, u32[]{:S(2)}) collective-permute-start(bf16[6,4096]{1,0:T(8,128)(2,1)S(1)} %get-tuple-element.52), channel_id=1, source_target_pairs={{0,32},{16,48},{32,64},{48,80},{64,96},{80,112},{96,0},{112,16},{1... | collective-permute-start | bytes 147464 | tf_op jit(solution)/shard_map/ppermute | solution.py:238
  130.0 19.3 %all-to-all-start = ((f32[16,3,32,128]{3,2,1,0:T(8,128)}), f32[16,3,32,128]{3,2,1,0:T(8,128)S(1)}, u32[]{:S(2)}, u32[]{:S(2)}) async-start(f32[16,3,32,128]{3,2,1,0:T(8,128)} %broadcast_select_fusion), calls=%async_computation | async-start | bytes 1572864 | tf_op jit(solution)/shard_map/all_to_all | solution.py:360
  (3 other events, 2.2 us)
where the time goes:
time: 153 us; the launch traced here: 152 us
  Pallas kernels  42.6 us (28%)
  waiting for transfers between devices  38.7 us (25%)
  starting transfers between devices  23 us (15%)
  local copies, waits for them, and re-layouts  17.9 us (12%)
  matrix products  11.3 us (7%)
  blocking collectives  7.76 us (5%)
  other arithmetic  5.43 us (4%)
  between operations  5.09 us (3%)
    pallas_call x1, Pallas kernels, time_steps(): pl.pallas_call(stencil_body, out_shape=(jax.ShapeDtypeStruct((BX, BY, NZ)...  42.6 us
    ppermute x4, waiting for transfers between devices, shift_both(): return lax.ppermute(a, ('px', 'py'), pairs)  19.7 us
    all_to_all x1, waiting for transfers between devices, per_device(): got = lax.all_to_all(carries, 'py', split_axis=0, concat_axis=0, tiled=True)  14.6 us
    ppermute x8, starting transfers between devices, shift(): return lax.ppermute(a, axis, ring(lax.axis_size(axis), d))  10.4 us
    ppermute x4, starting transfers between devices, shift_both(): return lax.ppermute(a, ('px', 'py'), pairs)  9.03 us
    all_gather x1, blocking collectives, x_operator(): margins = lax.all_gather(margin[0], 'px')  7.76 us
    dot_general x8, matrix products, mm(): return jnp.dot(a, b, precision=HIGH, preferred_element_type=jnp.float32)  7.42 us
    unnamed x50, local copies, waits for them, and re-layouts  6.08 us
  transfers between devices with their start and end apart: 13, of which 7 were waited for; matrix products, arithmetic and copies ran while one was open for 12% of the time, Pallas kernels for 0%

commit v1 on v0

--- a/solution.py
+++ b/solution.py
@@ -65,7 +65,7 @@
             left = u[:, :3] * sv[:3]
             for t in range(q):
                 couple[t, :, q] = left[t * own : (t + 1) * own]
-    return [a.astype(np.float32) for a in (diag, up, down, couple.reshape(count, own, count * 3))]
+    return [a.astype(np.float32) for a in (diag, up, down, np.concatenate([couple, couple[..., :1]], axis=3).reshape(count, own, count * 4))]
 
 
 def x_tables(count):
@@ -73,28 +73,46 @@
     block = BX // 2
     ctrl = total // 2
     b = basis(total)
-    g = b.T @ b
     width = block + 2 * OVMAX
     gpad = np.zeros((ctrl + 16, ctrl + 16))
-    gpad[8:-8, 8:-8] = g
-    inverse = np.zeros((3, OVMAX + 1, OVMAX + 1, block, width))
-    band = np.zeros((3, width, width + 6))
+    gpad[8:-8, 8:-8] = b.T @ b
+    bt = bspline((np.arange(BX)[None] - 2.0 * (np.arange(block + 4)[:, None] - 2) - 0.5) / 2.0)
+    base, send, near = [], [], []
     for cls, p in enumerate((0, 1, count - 1)):
+        has_low = float(cls != 0)
+        has_high = float(cls != 2)
         start = p * block
         knots = start - OVMAX + np.arange(width)
         lo = start - OVMAX + 8
         full = gpad[lo : lo + width, lo : lo + width]
-        band[cls] = gpad[lo : lo + width, lo - 3 : lo + width + 3]
+        band = gpad[lo : lo + width, lo - 3 : lo + width + 3]
         for m0 in range(OVMAX + 1):
             for m1 in range(OVMAX + 1):
                 inside = (knots >= start - m0) & (knots < start + block + m1) & (knots >= 0) & (knots < ctrl)
                 w = inside.astype(np.float64)
                 mat = full * w[:, None] * w[None, :] + np.diag(1.0 - w)
-                inverse[cls, m0, m1] = (np.linalg.inv(mat) * w[None, :])[OVMAX : OVMAX + block]
-    bt = np.zeros((block + 4, BX))
-    for r in range(block + 4):
-        bt[r] = bspline((np.arange(BX) - 2.0 * (r - 2) - 0.5) / 2.0)
-    return inverse.reshape(-1, block, width).astype(np.float32), band.astype(np.float32), bt.astype(np.float32)
+                e = (np.linalg.inv(mat) * w[None, :])[OVMAX : OVMAX + block]
+                q = e @ band
+                ql = q[:, :7] * has_low
+                qr = q[:, 7 + block :] * has_high
+                two = 2.0 * e - q[:, 7 : 7 + block] @ e
+                low = two[:, 0:6] * has_low
+                high = two[:, block + 2 :] * has_high
+                base.append(np.concatenate([two[:, 2 : block + 6] @ bt, low, -ql, high, -qr], axis=1))
+                send.append(
+                    np.concatenate(
+                        [bt[block - 2 :], e[block - 7 :, 2 : block + 6] @ bt, bt[:6], e[:7, 2 : block + 6] @ bt]
+                    )
+                )
+                zero = np.zeros((7, 6))
+                as_low = np.concatenate(
+                    [e[block - 7 :, block + 2 :] @ bt[0:6], np.zeros((7, 26)), e[block - 7 :, 0:6] * has_low, zero], axis=1
+                )
+                as_high = np.concatenate(
+                    [e[:7, 0:6] @ bt[block - 2 :], np.zeros((7, 26)), zero, e[:7, block + 2 :] * has_high], axis=1
+                )
+                near.append(np.stack([as_low, as_high]))
+    return [np.stack(t).astype(np.float32) for t in (base, send, near)]
 
 
 def stencil_body(mask_ref, f_ref, k_ref, v_ref, yl_ref, yh_ref, xl_ref, xh_ref, dll_ref, dlh_ref, dhl_ref, dhh_ref,
@@ -108,14 +126,16 @@
 
     def own_planes(group, carry):
         at = group * 4
-        ul = yl_ref[BX + group].astype(f32) * from_low_y
-        uh = yh_ref[BX + group].astype(f32) * from_high_y
+        ul = yl_ref[group, 4].astype(f32) * from_low_y
+        uh = yh_ref[group, 4].astype(f32) * from_high_y
+        gap = jnp.zeros((4, NZ), f32)
         for i in range(4):
             x = at + i
-            kl = yl_ref[x].astype(f32) * from_low_y
-            kh = yh_ref[x].astype(f32) * from_high_y
+            kl = yl_ref[group, i].astype(f32) * from_low_y
+            kh = yh_ref[group, i].astype(f32) * from_high_y
             u_s[x + W, 0:BY] = f_ref[x]
-            u_s[x + W, BY:EY] = jnp.concatenate([uh[4 * i : 4 * i + 4], ul[4 * i : 4 * i + 4]], axis=0)
+            rest = jnp.concatenate([kh[7:8], kh[15:16], gap, kl[12:13], kl[4:5]], axis=0)
+            u_s[x + W, BY:EY] = rest + jnp.concatenate([uh[4 * i : 4 * i + 4], ul[4 * i : 4 * i + 4]], axis=0)
             for n in range(4):
                 ref = dest[1 + n]
                 ref[x + W, 0:BY] = (k_ref[x] if n == 0 else v_ref[n - 1, x]).astype(f32)
@@ -124,14 +144,17 @@
 
     lax.fori_loop(0, BX // 4, own_planes, 0)
     for n in range(5):
-        for base, ref, below, above, scale in (
-            (0, xl_ref, dll_ref, dlh_ref, from_low_x),
-            (BX + W, xh_ref, dhl_ref, dhh_ref, from_high_x),
+        for base, ref, below, above, scale, near, outer in (
+            (0, xl_ref, dll_ref, dlh_ref, from_low_x, (W - 1, W - 2), 0),
+            (BX + W, xh_ref, dhl_ref, dhh_ref, from_high_x, (0, 1), W - 1),
         ):
             low = below[n].astype(f32) * (scale * from_low_y)
             high = above[n].astype(f32) * (scale * from_high_y)
             for i in range(W):
-                dest[n][base + i, 0:BY] = ref[n * W + i].astype(f32) * scale
+                value = ref[n * W + i].astype(f32)
+                if n == 0 and i in near:
+                    value = value + ref[(3 + near.index(i)) * W + outer].astype(f32)
+                dest[n][base + i, 0:BY] = value * scale
                 dest[n][base + i, BY:EY] = jnp.concatenate([high[4 * i : 4 * i + 4], low[4 * i : 4 * i + 4]], axis=0)
 
     lane = lax.broadcasted_iota(jnp.int32, (EY, 128), 1)
@@ -164,7 +187,7 @@
         c_s[x] = 1.0 - ((kx + kx_low) + (ky + kyd) + (kz + kzd))
         return k_next, kx
 
-    lax.fori_loop(0, EX, coefficients, (c_s[0], jnp.zeros((EY, NZ), f32)))
+    lax.fori_loop(0, EX, coefficients, (c_s[0], jnp.zeros((EY, NZ), f32)), unroll=4)
 
     row = lax.broadcasted_iota(jnp.int32, (EY, NZ), 0)
     row_mask = jnp.where(row < BY, 1.0, jnp.where(row < BY + W, from_high_y, from_low_y))
@@ -194,7 +217,7 @@
 
         first_u = u_s[lo]
         first_up = first_u * (kx_s[lo] + v0_s[lo] * (0.025 * first_u))
-        lax.fori_loop(lo + 1, hi + 1, one_plane, (jnp.zeros((EY, NZ), f32), first_up))
+        lax.fori_loop(lo + 1, hi + 1, one_plane, (jnp.zeros((EY, NZ), f32), first_up), unroll=4)
 
     fit_hi = fit_hi_ref[...]
     fit_lo = fit_lo_ref[...]
@@ -211,7 +234,7 @@
         zfit_ref[pl.ds(at, 8)] = out.reshape(8, BY, MZ)
         return carry
 
-    lax.fori_loop(0, BX // 8, fit_planes, 0)
+    lax.fori_loop(0, BX // 8, fit_planes, 0, unroll=2)
 
 
 def time_steps(masks, field, diffusivity, velocity, halos, fit_hi, fit_lo):
@@ -245,86 +268,121 @@
     return lax.ppermute(a, ("px", "py"), pairs)
 
 
-def halo_parts(field, diffusivity, velocity):
-    u = field.astype(jnp.bfloat16)
-
-    def y_face(rows):
-        kv = jnp.concatenate([diffusivity[:, rows]] + [velocity[n][:, rows] for n in range(3)], axis=1)
-        return jnp.concatenate([kv, u[:, rows].reshape(BX // 4, 16, NZ)], axis=0)
-
-    def x_face(planes):
-        return jnp.concatenate([u[planes], diffusivity[planes]] + [velocity[n][planes] for n in range(3)], axis=0)
-
-    def corner(planes, rows):
-        return jnp.stack(
-            [a[planes, rows].reshape(16, NZ) for a in (u, diffusivity, velocity[0], velocity[1], velocity[2])]
-        )
-
-    head = slice(0, W)
-    ty = slice(BY - W, BY)
-    tx = slice(BX - W, BX)
-    yl = shift(y_face(ty), "py", 1)
-    yh = shift(y_face(head), "py", -1)
-    xl = shift(x_face(tx), "px", 1)
-    xh = shift(x_face(head), "px", -1)
-    dll = shift_both(corner(tx, ty), 1, 1)
-    dlh = shift_both(corner(tx, head), 1, -1)
-    dhl = shift_both(corner(head, ty), -1, 1)
-    dhh = shift_both(corner(head, head), -1, -1)
-    return yl, yh, xl, xh, dll, dlh, dhl, dhh
+def pack_body(margin_ref, f_ref, k_ref, v_ref, ylo_ref, yhi_ref, xlo_ref, xhi_ref, ll_ref, lh_ref, hl_ref, hh_ref):
+    f32 = jnp.float32
+    bf16 = jnp.bfloat16
+    step = pl.program_id(0)
+    t = BY - W
+
+    def rest(u):
+        return u - u.astype(bf16).astype(f32)
+
+    for g in range(PACK // 4):
+        tails, heads = [], []
+        for i in range(4):
+            x = 4 * g + i
+            u = f_ref[x]
+            tails.append(u[t:])
+            heads.append(u[:W])
+            ur_t = rest(u[t - 4 :])
+            ur_h = rest(u[:8])
+            k, v0, v1, v2 = [r.astype(f32) for r in (k_ref[x], v_ref[0, x], v_ref[1, x], v_ref[2, x])]
+            ylo_ref[g, i] = jnp.concatenate(
+                [k[t:], ur_t[7:8], v0[t + 1 :], v1[t:], ur_t[6:7], v2[t + 1 :]], axis=0
+            ).astype(bf16)
+            yhi_ref[g, i] = jnp.concatenate(
+                [k[:W], v0[: W - 1], ur_h[0:1], v1[:W], v2[: W - 1], ur_h[1:2]], axis=0
+            ).astype(bf16)
+        ylo_ref[g, 4] = jnp.concatenate(tails, axis=0).astype(bf16)
+        yhi_ref[g, 4] = jnp.concatenate(heads, axis=0).astype(bf16)
+
+    def x_side(at, out, near, outer, low, high):
+        for i in range(W):
+            out[i] = f_ref[at + i].astype(bf16)
+            out[W + i] = k_ref[at + i]
+            out[2 * W + i] = v_ref[0, at + i]
+            if i == outer:
+                out[3 * W + i] = rest(f_ref[at + near[0]]).astype(bf16)
+                out[4 * W + i] = rest(f_ref[at + near[1]]).astype(bf16)
+            else:
+                out[3 * W + i] = v_ref[1, at + i]
+                out[4 * W + i] = v_ref[2, at + i]
+        half = jnp.zeros((16, NZ), f32)
+        out[5 * W] = jnp.concatenate([half + margin_ref[0, 0].astype(f32), half + margin_ref[0, 1].astype(f32)], axis=0).astype(bf16)
+        for n in range(5):
+            planes = [
+                (f_ref[at + i] if n == 0 else k_ref[at + i] if n == 1 else v_ref[n - 2, at + i]).astype(f32)
+                for i in range(W)
+            ]
+            low[n] = jnp.concatenate([a[t:] for a in planes], axis=0).astype(bf16)
+            high[n] = jnp.concatenate([a[:W] for a in planes], axis=0).astype(bf16)
+
+    @pl.when(step == 0)
+    def _():
+        x_side(0, xhi_ref, (0, 1), W - 1, hl_ref, hh_ref)
+
+    @pl.when(step == BX // PACK - 1)
+    def _():
+        x_side(PACK - W, xlo_ref, (W - 1, W - 2), 0, ll_ref, lh_ref)
+
+
+PACK = 16
+
+
+def halo_parts(field, diffusivity, velocity, margin):
+    bf16 = jnp.bfloat16
+    y_shape = (BX // 4, 5, 16, NZ)
+    y_spec = pl.BlockSpec((PACK // 4, 5, 16, NZ), lambda g: (g, 0, 0, 0))
+    x_shape = (5 * W + 1, BY, NZ)
+    x_spec = pl.BlockSpec(x_shape, lambda g: (0, 0, 0))
+    c_shape = (5, 16, NZ)
+    c_spec = pl.BlockSpec(c_shape, lambda g: (0, 0, 0))
+    planes = pl.BlockSpec((PACK, BY, NZ), lambda g: (g, 0, 0))
+    ylo, yhi, xlo, xhi, ll, lh, hl, hh = pl.pallas_call(
+        pack_body,
+        grid=(BX // PACK,),
+        out_shape=[jax.ShapeDtypeStruct(s, bf16) for s in [y_shape] * 2 + [x_shape] * 2 + [c_shape] * 4],
+        in_specs=[
+            pl.BlockSpec(memory_space=pltpu.SMEM),
+            planes,
+            planes,
+            pl.BlockSpec((3, PACK, BY, NZ), lambda g: (0, g, 0, 0)),
+        ],
+        out_specs=[y_spec] * 2 + [x_spec] * 2 + [c_spec] * 4,
+        compiler_params=pltpu.CompilerParams(vmem_limit_bytes=40 * 1024 * 1024),
+        name="pack_faces",
+    )(margin, field, diffusivity, velocity)
+    return (
+        shift(ylo, "py", 1),
+        shift(yhi, "py", -1),
+        shift(xlo, "px", 1),
+        shift(xhi, "px", -1),
+        shift_both(ll, 1, 1),
+        shift_both(lh, 1, -1),
+        shift_both(hl, -1, 1),
+        shift_both(hh, -1, -1),
+    )
 
 
 def mm(a, b):
     return jnp.dot(a, b, precision=HIGH, preferred_element_type=jnp.float32)
 
 
-def x_operator(margin, tables, p, count):
-    inverse, band, bt = tables
-    margins = lax.all_gather(margin[0], "px")
-
-    def rows_of(owner):
-        own = jnp.clip(owner, 0, count - 1)
-        cls = jnp.where(own == 0, 0, jnp.where(own == count - 1, 2, 1))
-        m = lax.dynamic_index_in_dim(margins, own, 0, keepdims=False)
-        m = jnp.clip(m, 0, OVMAX)
-        n = OVMAX + 1
-        found = lax.dynamic_index_in_dim(inverse, (cls * n + m[0]) * n + m[1], 0, keepdims=False)
-        return found * ((owner >= 0) & (owner < count)).astype(jnp.float32), cls
-
-    inverse = jnp.asarray(inverse)
-    e, cls = rows_of(p)
-    e_low, _ = rows_of(p - 1)
-    e_high, _ = rows_of(p + 1)
-    block = BX // 2
-    g = lax.dynamic_index_in_dim(jnp.asarray(band), cls, 0, keepdims=False)
-    has_low = (p > 0).astype(jnp.float32)
-    has_high = (p < count - 1).astype(jnp.float32)
-    q = mm(e, g)
-    ql = q[:, :7] * has_low
-    q0 = q[:, 7 : 7 + block]
-    qr = q[:, 7 + block :] * has_high
-    a = 2.0 * e - mm(q0, e)
-    ql_e = mm(ql, e_low[block - 7 :])
-    qr_e = mm(qr, e_high[:7])
-    w = a[:, 2 : block + 6]
-    w = w - jnp.pad(ql_e[:, block + 2 : block + 8], ((0, 0), (0, block - 2)))
-    w = w - jnp.pad(qr_e[:, 0:6], ((0, 0), (block - 2, 0)))
-    bt = jnp.asarray(bt)
-    full = jnp.concatenate(
-        [
-            mm(w, bt),
-            a[:, 0:6] * has_low,
-            -ql,
-            a[:, block + 2 :] * has_high,
-            -qr,
-            -ql_e[:, 0:6] * (p > 1).astype(jnp.float32),
-            -qr_e[:, block + 2 :] * (p < count - 2).astype(jnp.float32),
-        ],
-        axis=1,
-    )
-    kappa = mm(jnp.concatenate([e[block - 7 :, 2 : block + 6], e[:7, 2 : block + 6]], axis=0), bt)
-    send = jnp.concatenate([bt[block - 2 :], kappa[:7], bt[:6], kappa[7:]], axis=0)
-    return send, full
+def table_row(table, margins, owner, count):
+    own = jnp.clip(owner, 0, count - 1)
+    cls = jnp.where(own == 0, 0, jnp.where(own == count - 1, 2, 1))
+    n = OVMAX + 1
+    m = jnp.clip(margins, 0, OVMAX)
+    return lax.dynamic_index_in_dim(jnp.asarray(table), (cls * n + m[0]) * n + m[1], 0, keepdims=False)
+
+
+def x_operator(margin, low_margin, high_margin, tables, p, count):
+    base, send, near = tables
+    own = table_row(base, margin, p, count)
+    pad = jnp.pad(own, ((0, 0), (0, 12)))
+    as_low = table_row(near, low_margin, p - 1, count)[0]
+    as_high = table_row(near, high_margin, p + 1, count)[1]
+    return pad + mm(own[:, BX + 6 : BX + 13], as_low) + mm(own[:, BX + 19 : BX + 26], as_high)
 
 
 def per_device(field, diffusivity, velocity, margin):
@@ -336,8 +394,11 @@
     s_z = fit_matrix(NZ).T.astype(np.float32)
     fit_hi = s_z.astype(jnp.bfloat16)
     fit_lo = (s_z - fit_hi.astype(np.float32)).astype(jnp.bfloat16)
-    halos = halo_parts(field, diffusivity, velocity)
-    send, full = x_operator(margin, x_tables(count_x), p, count_x)
+    halos = halo_parts(field, diffusivity, velocity, margin)
+    tables = x_tables(count_x)
+    send = table_row(tables[1], margin[0], p, count_x)
+    low_margin, high_margin = [h[5 * W, 0:32:16, 0].astype(jnp.int32) for h in (halos[2], halos[3])]
+    full = x_operator(margin[0], low_margin, high_margin, tables, p, count_x)
     diag, up, down, couple = [
         lax.dynamic_index_in_dim(jnp.asarray(t), q, 0, keepdims=False) for t in y_tables(count_y)
     ]
@@ -355,12 +416,18 @@
     xfit = mm(full, stacked).reshape(BX // 2, BY, MZ)
 
     both = jnp.einsum("cy,xyz->cxz", jnp.concatenate([up, down], axis=0), xfit, precision=HIGH)
+    head = lax.reduce_precision(both, 8, 7)
+    rest = both - head
     target = jnp.arange(count_y)[:, None, None, None]
-    carries = jnp.where(target > q, both[None, :3], both[None, 3:])
+    carries = jnp.where(
+        target > q,
+        jnp.concatenate([head[:3], rest[:1]], axis=0)[None],
+        jnp.concatenate([head[3:], rest[3:4]], axis=0)[None],
+    ).astype(jnp.bfloat16)
     got = lax.all_to_all(carries, "py", split_axis=0, concat_axis=0, tiled=True)
     controls = jnp.einsum("my,xyz->xmz", diag, xfit, precision=HIGH)
     controls = controls + jnp.einsum(
-        "mc,cxz->xmz", couple, got.reshape(count_y * 3, BX // 2, MZ), precision=HIGH
+        "mc,cxz->xmz", couple, got.astype(jnp.float32).reshape(count_y * 4, BX // 2, MZ), precision=HIGH
     )
     return advected, controls
 

time: 153 us -> 105 us (0.69)
  waiting for transfers between devices: 38.7 us -> 10.3 us
  Pallas kernels: 42.6 us -> 28.8 us
  starting transfers between devices: 23 us -> 34.3 us
  blocking collectives: 7.76 us -> 0 us
  local copies, waits for them, and re-layouts: 17.9 us -> 14.7 us
  other arithmetic: 5.43 us -> 2.38 us
  matrix products: 11.3 us -> 8.46 us
    ppermute x4, waiting for transfers between devices: 19.7 us -> 0.01 us  [shift_both(): return lax.ppermute(a, ('px', 'py'), pairs)]
    pallas_call x1, Pallas kernels: 42.6 us -> 27.4 us  [time_steps(): pl.pallas_call(stencil_body, out_shape=(jax.ShapeDtypeStruct((BX, BY, NZ)...]
    all_gather x1 -> x0, blocking collectives: 7.76 us -> none  [x_operator(): margins = lax.all_gather(margin[0], 'px')]
    ppermute x8, starting transfers between devices: 10.4 us -> 15.9 us  [shift(): return lax.ppermute(a, axis, ring(lax.axis_size(axis), d))]
    all_to_all x1, waiting for transfers between devices: 14.6 us -> 9.53 us  [per_device(): got = lax.all_to_all(carries, 'py', split_axis=0, concat_axis=0, tiled=True)]
    slice x14 -> x7, local copies, waits for them, and re-layouts: 7.71 us -> 3.2 us  [the longest x3 1.7 us: table_row(): m[1]]
    ppermute x8, waiting for transfers between devices: 4.39 us -> 0.74 us  [shift(): return lax.ppermute(a, axis, ring(lax.axis_size(axis), d))]
    ppermute x4, starting transfers between devices: 9.03 us -> 12.4 us  [shift_both(): return lax.ppermute(a, ('px', 'py'), pairs)]
  transfers between devices with their start and end apart: 13 -> 13, of which waited for: 7 -> 2; matrix products, arithmetic and copies ran while one was open for 12% -> 10% of each run, Pallas kernels for 0% -> 0%
where the time goes in v1:
time: 105 us; the launch traced here: 104 us
  starting transfers between devices  34.3 us (33%)
  Pallas kernels  28.8 us (27%)
  local copies, waits for them, and re-layouts  14.7 us (14%)
  waiting for transfers between devices  10.3 us (10%)
  matrix products  8.46 us (8%)
  between operations  4.79 us (5%)
  other arithmetic  2.38 us (2%)
    pallas_call x1, Pallas kernels, time_steps(): pl.pallas_call(stencil_body, out_shape=(jax.ShapeDtypeStruct((BX, BY, NZ)...  27.4 us
    ppermute x8, starting transfers between devices, shift(): return lax.ppermute(a, axis, ring(lax.axis_size(axis), d))  15.9 us
    ppermute x4, starting transfers between devices, shift_both(): return lax.ppermute(a, ('px', 'py'), pairs)  12.4 us
    all_to_all x1, waiting for transfers between devices, per_device(): got = lax.all_to_all(carries, 'py', split_axis=0, concat_axis=0, tiled=True)  9.53 us
    unnamed x30, local copies, waits for them, and re-layouts  7.76 us
    all_to_all x1, starting transfers between devices, per_device(): got = lax.all_to_all(carries, 'py', split_axis=0, concat_axis=0, tiled=True)  6.01 us
    dot_general x4, matrix products, mm(): return jnp.dot(a, b, precision=HIGH, preferred_element_type=jnp.float32)  5.26 us
  transfers between devices with their start and end apart: 13, of which 2 were waited for; matrix products, arithmetic and copies ran while one was open for 10% of the time, Pallas kernels for 0%

profile of v1, /device:TPU:0, one launch (start us, length us, event | category | flops | bytes accessed | tf_op | source)
XLA Modules:
  0.0 103.7 jit_solution(13418301539617274505)
XLA Ops:
  0.6 1.9 %copy-done = bf16[3,64,32,256]{3,2,1,0:T(8,128)(2,1)S(1)} copy-done((bf16[3,64,32,256]{3,2,1,0:T(8,128)(2,1)S(1)}, bf16[3,64,32,256]{3,2,1,0:T(8,128)(2,1)}, u32[]{:S(2)}) %copy-start) | copy-done | bytes 3145752
  2.5 1.6 %copy-done.1 = f32[64,32,256]{2,1,0:T(8,128)S(1)} copy-done((f32[64,32,256]{2,1,0:T(8,128)S(1)}, f32[64,32,256]{2,1,0:T(8,128)}, u32[]{:S(2)}) %copy-start.1) | copy-done | bytes 2097176
  4.1 1.2 %copy-done.2 = bf16[64,32,256]{2,1,0:T(8,128)(2,1)S(1)} copy-done((bf16[64,32,256]{2,1,0:T(8,128)(2,1)S(1)}, bf16[64,32,256]{2,1,0:T(8,128)(2,1)}, u32[]{:S(2)}) %copy-start.2) | copy-done | bytes 1048600
  6.0 1.5 %pack_faces.1 = (bf16[16,5,16,256]{3,2,1,0:T(8,128)(2,1)S(1)}, bf16[16,5,16,256]{3,2,1,0:T(8,128)(2,1)S(1)}, bf16[21,32,256]{2,1,0:T(8,128)(2,1)S(1)}, bf16[21,3...) custom-call(s32[1,2]{1,0:T(1,128)S(1)} %copy-done.3, ...), custom_call_target="tpu_custom_call" | custom-call | tf_op jit(solution)/shard_map/pack_faces/pallas_call | solution.py:341
  7.5 2.1 %collective-permute-start = (bf16[16,5,16,256]{3,2,1,0:T(8,128)(2,1)S(1)}, bf16[16,5,16,256]{3,2,1,0:T(8,128)(2,1)S(1)}, u32[]{:S(2)}, u32[]{:S(2)}) collective-permute-start(bf16[16,5,16,256]{3,2,1,0:T(8,128)(2,1)S(1)} %get-tuple-element.12), channel_id=1, source_target_pairs={{0,1},{1,2},{2,3},{3,4},{4,5},{5,6},{6,7},{7,8},{8,9},{9,10},{10,1... | collective-permute-start | bytes 1966088 | tf_op jit(solution)/shard_map/ppermute | solution.py:261
  9.6 4.7 %collective-permute-start.1 = (bf16[16,5,16,256]{3,2,1,0:T(8,128)(2,1)S(1)}, bf16[16,5,16,256]{3,2,1,0:T(8,128)(2,1)S(1)}, u32[]{:S(2)}, u32[]{:S(2)}) collective-permute-start(bf16[16,5,16,256]{3,2,1,0:T(8,128)(2,1)S(1)} %get-tuple-element.13), channel_id=1, source_target_pairs={{0,15},{1,0},{2,1},{3,2},{4,3},{5,4},{6,5},{7,6},{8,7},{9,8},{10,9... | collective-permute-start | bytes 1966088 | tf_op jit(solution)/shard_map/ppermute | solution.py:261
  14.2 3.0 %collective-permute-start.3 = (bf16[21,32,256]{2,1,0:T(8,128)(2,1)S(1)}, bf16[21,32,256]{2,1,0:T(8,128)(2,1)}, u32[]{:S(2)}, u32[]{:S(2)}) collective-permute-start(bf16[21,32,256]{2,1,0:T(8,128)(2,1)S(1)} %get-tuple-element.15), channel_id=1, source_target_pairs={{0,112},{16,0},{32,16},{48,32},{64,48},{80,64},{96,80},{112,96},{1... | collective-permute-start | bytes 1032200 | tf_op jit(solution)/shard_map/ppermute | solution.py:261
  20.3 1.3 %dynamic-slice_bitcast_fusion.5 = (f32[3,32]{1,0:T(4,128)}, f32[3,32]{1,0:T(4,128)}) fusion(f32[16,3,32]{2,1,0:T(4,128)} %constant.80.clone, s32[]{:T(128)S(6)} %select_n.57, f32[16,3,32]{2,1,0:T(4,128)} %constant.79.clone), kind=kLoop, calls=%fused_computation.27 | loop fusion | bytes 1540 | tf_op jit(solution)/shard_map/jit(dynamic_index_in_dim)/squeeze | solution.py:403
  22.3 4.8 %collective-permute-start.5 = (bf16[5,16,256]{2,1,0:T(8,128)(2,1)S(1)}, bf16[5,16,256]{2,1,0:T(8,128)(2,1)S(1)}, u32[]{:S(2)}, u32[]{:S(2)}) collective-permute-start(bf16[5,16,256]{2,1,0:T(8,128)(2,1)S(1)} %get-tuple-element.17), channel_id=1, source_target_pairs={{0,31},{1,16},{2,17},{3,18},{4,19},{5,20},{6,21},{7,22},{8,23},{9,... | collective-permute-start | bytes 122888 | tf_op jit(solution)/shard_map/ppermute | solution.py:268
  30.5 0.9 convolution_add_fusion.2
  31.4 7.5 %collective-permute-start.7 = (bf16[5,16,256]{2,1,0:T(8,128)(2,1)S(1)}, bf16[5,16,256]{2,1,0:T(8,128)(2,1)S(1)}, u32[]{:S(2)}, u32[]{:S(2)}) collective-permute-start(bf16[5,16,256]{2,1,0:T(8,128)(2,1)S(1)} %get-tuple-element.19), channel_id=1, source_target_pairs={{0,127},{1,112},{2,113},{3,114},{4,115},{5,116},{6,117},{7,118},{8... | collective-permute-start | bytes 122888 | tf_op jit(solution)/shard_map/ppermute | solution.py:268
  41.6 0.8 copy-done.6
  42.5 27.4 %time_steps.1 = (f32[64,32,256]{2,1,0:T(8,128)}, f32[64,32,128]{2,1,0:T(8,128)}) custom-call(f32[4]{0:T(128)} %add_convert_fusion.mask_ref, f32[64,32,256]{2,1,0:T(8,128)} %f_ref.3, bf16[64,32,256]{2,1,0:T(8,128)(2,1)} %k_ref.3, bf16[3,64,32,256]{3,2,1,0:T(8,128)(2,1)} %v_ref.3, bf16[16,5,16,256]{3,2,1,0:T(8,128)(2,1)} %copy-done.5, ...), custom_call_target="tpu_custom_call" | custom-call | tf_op jit(solution)/shard_map/time_steps/pallas_call | solution.py:242
  69.8 2.5 %fusion.28 = (bf16[26,4096]{1,0:T(8,128)(2,1)S(1)}, f32[26,4096]{1,0:T(8,128)S(1)}) fusion(f32[8,8,32,128]{3,2,1,0:T(8,128)} %bitcast.60, f32[75,26,64]{2,1,0:T(8,128)} %constant.75.clone, s32[]{:T(128)S(6)} %select_n.50), kind=kOutput, calls=%fused_computation.48 | convolution fusion | flops 81895424 | bytes 1703940 | tf_op jit(solution)/shard_map/dot_general | solution.py:368
  72.4 2.9 %collective-permute-start.9 = (f32[13,4096]{1,0:T(8,128)S(1)}, f32[13,4096]{1,0:T(8,128)S(1)}, u32[]{:S(2)}, u32[]{:S(2)}) collective-permute-start(f32[13,4096]{1,0:T(8,128)S(1)} %get-tuple-element.22), channel_id=1, source_target_pairs={{0,112},{16,0},{32,16},{48,32},{64,48},{80,64},{96,80},{112,96},{1... | collective-permute-start | bytes 638984 | tf_op jit(solution)/shard_map/ppermute | solution.py:261
  75.5 3.2 %collective-permute-start.11 = (bf16[6,4096]{1,0:T(8,128)(2,1)S(1)}, bf16[6,4096]{1,0:T(8,128)(2,1)}, u32[]{:S(2)}, u32[]{:S(2)}) collective-permute-start(bf16[6,4096]{1,0:T(8,128)(2,1)S(1)} %get-tuple-element.24), channel_id=1, source_target_pairs={{0,96},{16,112},{32,0},{48,16},{64,32},{80,48},{96,64},{112,80},{1... | collective-permute-start | bytes 147464 | tf_op jit(solution)/shard_map/ppermute | solution.py:261
  78.7 0.9 convolution_add_fusion.1
  81.0 1.4 %concatenate.12 = f32[102,4096]{1,0:T(8,128)S(1)} concatenate(f32[64,4096]{1,0:T(8,128)S(1)} %bitcast.62, f32[13,4096]{1,0:T(8,128)S(1)} %collective-permute-done.8, f32[13,4096]{1,0:T(8,128)S(1)} %collective-permute-done.9, bf16[6,4096]{1,0:T(8,128)(2,1)S(1)} %collective-permute-done.10, bf16[6,4096]{1,0:T(8,128)(2,1)} %collective-permute-done.11), dimensions={0} | concatenate | bytes 3244032 | tf_op jit(solution)/shard_map/concatenate | solution.py:413
  82.4 0.9 convolution_bitcast_fusion
  84.0 1.0 %select_convert_fusion = bf16[16,4,32,128]{3,1,2,0:T(4,128)(2,1)} fusion(bf16[4,32,128]{2,0,1:T(4,128)(2,1)S(1)} %pad_maximum_fusion.1, bf16[4,32,128]{2,0,1:T(4,128)(2,1)S(1)} %pad_maximum_fusion, pred[16]{0:T(512)(128)(4,1)S(1)} %copy-done.13), kind=kLoop, calls=%fused_computation.6 | loop fusion | flops 262144 | bytes 589840 | tf_op jit(solution)/shard_map/convert_element_type | solution.py:426
  85.1 6.0 %all-to-all-start = ((bf16[16,4,32,128]{3,1,2,0:T(4,128)(2,1)}), bf16[16,4,32,128]{3,1,2,0:T(4,128)(2,1)S(1)}, u32[]{:S(2)}, u32[]{:S(2)}) async-start(bf16[16,4,32,128]{3,1,2,0:T(4,128)(2,1)} %select_convert_fusion), calls=%async_computation | async-start | bytes 1048576 | tf_op jit(solution)/shard_map/all_to_all | solution.py:427
  91.1 1.1 %fusion.7 = f32[32,128,16]{1,2,0:T(8,128)S(1)} fusion(f32[32,32,128]{2,1,0:T(8,128)S(1)} %bitcast.59, f32[16,16,32]{2,1,0:T(8,128)} %constant.78.clone, s32[]{:T(128)S(6)} %select_n.57), kind=kOutput, calls=%fused_computation.17 | convolution fusion | flops 25165824 | bytes 794628 | tf_op jit(solution)/shard_map/my,xyz->xmz/dot_general | solution.py:428
  92.2 9.5 %all-to-all-done = bf16[16,4,32,128]{3,1,2,0:T(4,128)(2,1)S(1)} async-done(((bf16[16,4,32,128]{3,1,2,0:T(4,128)(2,1)}), bf16[16,4,32,128]{3,1,2,0:T(4,128)(2,1)S(1)}, u32[]{:S(2)}, u32[]{:S(2)}) %all-to-all-start) | async-done | bytes 524320 | tf_op jit(solution)/shard_map/all_to_all | solution.py:427
  102.0 1.7 %fusion = f32[32,16,128]{2,1,0:T(8,128)} fusion(f32[32,128,16]{1,2,0:T(8,128)S(1)} %fusion.7, bf16[64,32,128]{2,0,1:T(8,128)(2,1)S(1)} %bitcast.63, f32[16,16,64]{2,1,0:T(8,128)} %constant.81.clone, s32[]{:T(128)S(6)} %select_n.57), kind=kOutput, calls=%fused_computation.2 | convolution fusion | flops 50397184 | bytes 1056772 | tf_op jit(solution)/shard_map/mc,cxz->xmz/dot_general | solution.py:429
  (61 shorter events, 9.1 us)
Async XLA Ops:
  0.6 1.9 %copy-start = (bf16[3,64,32,256]{3,2,1,0:T(8,128)(2,1)S(1)}, bf16[3,64,32,256]{3,2,1,0:T(8,128)(2,1)}, u32[]{:S(2)}) copy-start(bf16[3,64,32,256]{3,2,1,0:T(8,128)(2,1)} %v_ref.3) | copy-start | bytes 9437188
  2.5 1.6 %copy-start.1 = (f32[64,32,256]{2,1,0:T(8,128)S(1)}, f32[64,32,256]{2,1,0:T(8,128)}, u32[]{:S(2)}) copy-start(f32[64,32,256]{2,1,0:T(8,128)} %f_ref.3) | copy-start | bytes 6291460
  4.1 1.2 %copy-start.2 = (bf16[64,32,256]{2,1,0:T(8,128)(2,1)S(1)}, bf16[64,32,256]{2,1,0:T(8,128)(2,1)}, u32[]{:S(2)}) copy-start(bf16[64,32,256]{2,1,0:T(8,128)(2,1)} %k_ref.3) | copy-start | bytes 3145732
  5.3 0.7 copy-start.3
  7.5 33.3 %collective-permute-start = (bf16[16,5,16,256]{3,2,1,0:T(8,128)(2,1)S(1)}, bf16[16,5,16,256]{3,2,1,0:T(8,128)(2,1)S(1)}, u32[]{:S(2)}, u32[]{:S(2)}) collective-permute-start(bf16[16,5,16,256]{3,2,1,0:T(8,128)(2,1)S(1)} %get-tuple-element.12), channel_id=1, source_target_pairs={{0,1},{1,2},{2,3},{3,4},{4,5},{5,6},{6,7},{7,8},{8,9},{9,10},{10,1... | collective-permute-start | bytes 1966088 | tf_op jit(solution)/shard_map/ppermute | solution.py:261
  9.6 31.2 %collective-permute-start.1 = (bf16[16,5,16,256]{3,2,1,0:T(8,128)(2,1)S(1)}, bf16[16,5,16,256]{3,2,1,0:T(8,128)(2,1)S(1)}, u32[]{:S(2)}, u32[]{:S(2)}) collective-permute-start(bf16[16,5,16,256]{3,2,1,0:T(8,128)(2,1)S(1)} %get-tuple-element.13), channel_id=1, source_target_pairs={{0,15},{1,0},{2,1},{3,2},{4,3},{5,4},{6,5},{7,6},{8,7},{9,8},{10,9... | collective-permute-start | bytes 1966088 | tf_op jit(solution)/shard_map/ppermute | solution.py:261
  14.2 13.6 %collective-permute-start.2 = (bf16[21,32,256]{2,1,0:T(8,128)(2,1)S(1)}, bf16[21,32,256]{2,1,0:T(8,128)(2,1)}, u32[]{:S(2)}, u32[]{:S(2)}) collective-permute-start(bf16[21,32,256]{2,1,0:T(8,128)(2,1)S(1)} %get-tuple-element.14), channel_id=1, source_target_pairs={{0,16},{16,32},{32,48},{48,64},{64,80},{80,96},{96,112},{112,0},{1... | collective-permute-start | bytes 1032200 | tf_op jit(solution)/shard_map/ppermute | solution.py:261
  14.2 8.1 %collective-permute-start.3 = (bf16[21,32,256]{2,1,0:T(8,128)(2,1)S(1)}, bf16[21,32,256]{2,1,0:T(8,128)(2,1)}, u32[]{:S(2)}, u32[]{:S(2)}) collective-permute-start(bf16[21,32,256]{2,1,0:T(8,128)(2,1)S(1)} %get-tuple-element.15), channel_id=1, source_target_pairs={{0,112},{16,0},{32,16},{48,32},{64,48},{80,64},{96,80},{112,96},{1... | collective-permute-start | bytes 1032200 | tf_op jit(solution)/shard_map/ppermute | solution.py:261
  17.2 14.2 %collective-permute-start.4 = (bf16[5,16,256]{2,1,0:T(8,128)(2,1)S(1)}, bf16[5,16,256]{2,1,0:T(8,128)(2,1)S(1)}, u32[]{:S(2)}, u32[]{:S(2)}) collective-permute-start(bf16[5,16,256]{2,1,0:T(8,128)(2,1)S(1)} %get-tuple-element.16), channel_id=1, source_target_pairs={{0,17},{1,18},{2,19},{3,20},{4,21},{5,22},{6,23},{7,24},{8,25},{9,... | collective-permute-start | bytes 122888 | tf_op jit(solution)/shard_map/ppermute | solution.py:268
  22.3 18.4 %collective-permute-start.5 = (bf16[5,16,256]{2,1,0:T(8,128)(2,1)S(1)}, bf16[5,16,256]{2,1,0:T(8,128)(2,1)S(1)}, u32[]{:S(2)}, u32[]{:S(2)}) collective-permute-start(bf16[5,16,256]{2,1,0:T(8,128)(2,1)S(1)} %get-tuple-element.17), channel_id=1, source_target_pairs={{0,31},{1,16},{2,17},{3,18},{4,19},{5,20},{6,21},{7,22},{8,23},{9,... | collective-permute-start | bytes 122888 | tf_op jit(solution)/shard_map/ppermute | solution.py:268
  27.8 12.9 %collective-permute-start.6 = (bf16[5,16,256]{2,1,0:T(8,128)(2,1)S(1)}, bf16[5,16,256]{2,1,0:T(8,128)(2,1)S(1)}, u32[]{:S(2)}, u32[]{:S(2)}) collective-permute-start(bf16[5,16,256]{2,1,0:T(8,128)(2,1)S(1)} %get-tuple-element.18), channel_id=1, source_target_pairs={{0,113},{1,114},{2,115},{3,116},{4,117},{5,118},{6,119},{7,120},{8... | collective-permute-start | bytes 122888 | tf_op jit(solution)/shard_map/ppermute | solution.py:268
  31.4 9.4 %copy-start.7 = (bf16[5,16,256]{2,1,0:T(8,128)(2,1)}, bf16[5,16,256]{2,1,0:T(8,128)(2,1)S(1)}, u32[]{:S(2)}) copy-start(bf16[5,16,256]{2,1,0:T(8,128)(2,1)S(1)} %collective-permute-done.4.dll_ref) | copy-start | bytes 122884
  31.4 9.3 %collective-permute-start.7 = (bf16[5,16,256]{2,1,0:T(8,128)(2,1)S(1)}, bf16[5,16,256]{2,1,0:T(8,128)(2,1)S(1)}, u32[]{:S(2)}, u32[]{:S(2)}) collective-permute-start(bf16[5,16,256]{2,1,0:T(8,128)(2,1)S(1)} %get-tuple-element.19), channel_id=1, source_target_pairs={{0,127},{1,112},{2,113},{3,114},{4,115},{5,116},{6,117},{7,118},{8... | collective-permute-start | bytes 122888 | tf_op jit(solution)/shard_map/ppermute | solution.py:268
  40.8 0.9 copy-start.5
  41.6 0.8 copy-start.6
  69.8 9.8 %copy-start.4 = (f32[64,32,128]{2,1,0:T(8,128)S(1)}, f32[64,32,128]{2,1,0:T(8,128)}, u32[]{:S(2)}) copy-start(f32[64,32,128]{2,1,0:T(8,128)} %get-tuple-element.21) | copy-start | bytes 3145732
  72.4 8.5 %collective-permute-start.8 = (f32[13,4096]{1,0:T(8,128)S(1)}, f32[13,4096]{1,0:T(8,128)S(1)}, u32[]{:S(2)}, u32[]{:S(2)}) collective-permute-start(f32[13,4096]{1,0:T(8,128)S(1)} %get-tuple-element.23), channel_id=1, source_target_pairs={{0,16},{16,32},{32,48},{48,64},{64,80},{80,96},{96,112},{112,0},{1... | collective-permute-start | bytes 638984 | tf_op jit(solution)/shard_map/ppermute | solution.py:261
  72.4 8.5 %collective-permute-start.9 = (f32[13,4096]{1,0:T(8,128)S(1)}, f32[13,4096]{1,0:T(8,128)S(1)}, u32[]{:S(2)}, u32[]{:S(2)}) collective-permute-start(f32[13,4096]{1,0:T(8,128)S(1)} %get-tuple-element.22), channel_id=1, source_target_pairs={{0,112},{16,0},{32,16},{48,32},{64,48},{80,64},{96,80},{112,96},{1... | collective-permute-start | bytes 638984 | tf_op jit(solution)/shard_map/ppermute | solution.py:261
  75.4 5.5 %collective-permute-start.10 = (bf16[6,4096]{1,0:T(8,128)(2,1)S(1)}, bf16[6,4096]{1,0:T(8,128)(2,1)S(1)}, u32[]{:S(2)}, u32[]{:S(2)}) collective-permute-start(bf16[6,4096]{1,0:T(8,128)(2,1)S(1)} %get-tuple-element.25), channel_id=1, source_target_pairs={{0,32},{16,48},{32,64},{48,80},{64,96},{80,112},{96,0},{112,16},{1... | collective-permute-start | bytes 147464 | tf_op jit(solution)/shard_map/ppermute | solution.py:261
  75.5 5.5 %collective-permute-start.11 = (bf16[6,4096]{1,0:T(8,128)(2,1)S(1)}, bf16[6,4096]{1,0:T(8,128)(2,1)}, u32[]{:S(2)}, u32[]{:S(2)}) collective-permute-start(bf16[6,4096]{1,0:T(8,128)(2,1)S(1)} %get-tuple-element.24), channel_id=1, source_target_pairs={{0,96},{16,112},{32,0},{48,16},{64,32},{80,48},{96,64},{112,80},{1... | collective-permute-start | bytes 147464 | tf_op jit(solution)/shard_map/ppermute | solution.py:261
  82.4 1.1 %copy-start.11 = (f32[3,32]{1,0:T(4,128)S(1)}, f32[3,32]{1,0:T(4,128)}, u32[]{:S(2)}) copy-start(f32[3,32]{1,0:T(4,128)} %get-tuple-element.42) | copy-start | bytes 1156
  82.4 1.1 %copy-start.12 = (f32[3,32]{1,0:T(4,128)S(1)}, f32[3,32]{1,0:T(4,128)}, u32[]{:S(2)}) copy-start(f32[3,32]{1,0:T(4,128)} %get-tuple-element.43) | copy-start | bytes 1156
  82.4 1.6 %copy-start.13 = (pred[16]{0:T(512)(128)(4,1)S(1)}, pred[16]{0:T(512)(128)(4,1)}, u32[]{:S(2)}) copy-start(pred[16]{0:T(512)(128)(4,1)} %iota_compare_fusion) | copy-start | bytes 52
  85.1 16.7 %all-to-all-start = ((bf16[16,4,32,128]{3,1,2,0:T(4,128)(2,1)}), bf16[16,4,32,128]{3,1,2,0:T(4,128)(2,1)S(1)}, u32[]{:S(2)}, u32[]{:S(2)}) async-start(bf16[16,4,32,128]{3,1,2,0:T(4,128)(2,1)} %select_convert_fusion), calls=%async_computation | async-start | bytes 1048576 | tf_op jit(solution)/shard_map/all_to_all | solution.py:427
  (3 other events, 1.9 us)

commit v2 on v1

--- a/solution.py
+++ b/solution.py
@@ -115,8 +115,8 @@
     return [np.stack(t).astype(np.float32) for t in (base, send, near)]
 
 
-def stencil_body(mask_ref, f_ref, k_ref, v_ref, yl_ref, yh_ref, xl_ref, xh_ref, dll_ref, dlh_ref, dhl_ref, dhh_ref,
-                 fit_hi_ref, fit_lo_ref, adv_ref, zfit_ref, u_s, v0_s, v1_s, v2_s, kx_s, ky_s, kyd_s, kz_s, kzd_s, c_s):
+def stencil_body(mask_ref, f_ref, k_ref, v_ref, yl_ref, yh_ref, xl_ref, xh_ref, cl_ref, ch_ref, send_ref,
+                 fit_hi_ref, fit_lo_ref, adv_ref, zfit_ref, out_ref, u_s, v0_s, v1_s, v2_s, kx_s, ky_s, kyd_s, kz_s, kzd_s, c_s):
     f32 = jnp.float32
     from_low_x = mask_ref[0]
     from_high_x = mask_ref[1]
@@ -144,12 +144,12 @@
 
     lax.fori_loop(0, BX // 4, own_planes, 0)
     for n in range(5):
-        for base, ref, below, above, scale, near, outer in (
-            (0, xl_ref, dll_ref, dlh_ref, from_low_x, (W - 1, W - 2), 0),
-            (BX + W, xh_ref, dhl_ref, dhh_ref, from_high_x, (0, 1), W - 1),
+        for base, ref, corner, scale, near, outer in (
+            (0, xl_ref, 0, from_low_x, (W - 1, W - 2), 0),
+            (BX + W, xh_ref, 5, from_high_x, (0, 1), W - 1),
         ):
-            low = below[n].astype(f32) * (scale * from_low_y)
-            high = above[n].astype(f32) * (scale * from_high_y)
+            low = cl_ref[corner + n].astype(f32) * (scale * from_low_y)
+            high = ch_ref[corner + n].astype(f32) * (scale * from_high_y)
             for i in range(W):
                 value = ref[n * W + i].astype(f32)
                 if n == 0 and i in near:
@@ -236,21 +236,43 @@
 
     lax.fori_loop(0, BX // 8, fit_planes, 0, unroll=2)
 
-
-def time_steps(masks, field, diffusivity, velocity, halos, fit_hi, fit_lo):
+    half = OUT // 2
+    for base, cells in ((0, range(BX - 11, BX)), (half, range(11))):
+        rows = [jnp.zeros((BY, MZ), f32)] * 6
+        for x in cells:
+            plane = zfit_ref[x]
+            rows = [a + send_ref[base + r, x] * plane for r, a in enumerate(rows)]
+        for r in range(6):
+            out_ref[base + r] = rows[r]
+
+        def sweep(x, rows, base=base):
+            plane = zfit_ref[x]
+            return tuple(a + send_ref[base + 6 + r, x] * plane for r, a in enumerate(rows))
+
+        rows = lax.fori_loop(0, BX, sweep, (jnp.zeros((BY, MZ), f32),) * 7, unroll=8)
+        for r in range(7):
+            out_ref[base + 6 + r] = rows[r]
+
+
+OUT = 26
+
+
+def time_steps(masks, field, diffusivity, velocity, halos, send, fit_hi, fit_lo):
     vmem = pl.BlockSpec(memory_space=pltpu.VMEM)
+    smem = pl.BlockSpec(memory_space=pltpu.SMEM)
     return pl.pallas_call(
         stencil_body,
         out_shape=(
             jax.ShapeDtypeStruct((BX, BY, NZ), jnp.float32),
             jax.ShapeDtypeStruct((BX, BY, MZ), jnp.float32),
+            jax.ShapeDtypeStruct((OUT, BY, MZ), jnp.float32),
         ),
-        in_specs=[pl.BlockSpec(memory_space=pltpu.SMEM)] + [vmem] * 13,
-        out_specs=(vmem, vmem),
+        in_specs=[smem] + [vmem] * 9 + [smem] + [vmem] * 2,
+        out_specs=(vmem, vmem, vmem),
         scratch_shapes=[pltpu.VMEM((EX, EY, NZ), jnp.float32)] * 10,
-        compiler_params=pltpu.CompilerParams(vmem_limit_bytes=60 * 1024 * 1024),
+        compiler_params=pltpu.CompilerParams(vmem_limit_bytes=STEP_VMEM * 1024 * 1024),
         name="time_steps",
-    )(masks, field, diffusivity, velocity, *halos, fit_hi, fit_lo)
+    )(masks, field, diffusivity, velocity, *halos, send, fit_hi, fit_lo)
 
 
 def ring(n, d):
@@ -261,23 +283,27 @@
     return lax.ppermute(a, axis, ring(lax.axis_size(axis), d))
 
 
-def shift_both(a, dx, dy):
-    nx = lax.axis_size("px")
-    ny = lax.axis_size("py")
-    pairs = [(i * ny + j, ((i + dx) % nx) * ny + (j + dy) % ny) for i in range(nx) for j in range(ny)]
-    return lax.ppermute(a, ("px", "py"), pairs)
-
-
-def pack_body(margin_ref, f_ref, k_ref, v_ref, ylo_ref, yhi_ref, xlo_ref, xhi_ref, ll_ref, lh_ref, hl_ref, hh_ref):
+def pack_body(margin_ref, f_hbm, k_hbm, v_hbm, ylo_ref, yhi_ref, xlo_ref, xhi_ref, f_ref, k_ref, v_ref, sems):
     f32 = jnp.float32
     bf16 = jnp.bfloat16
-    step = pl.program_id(0)
     t = BY - W
+    copies = []
+    for c in range(BX // PACK):
+        part = pl.ds(c * PACK, PACK)
+        copies.append(
+            [
+                pltpu.make_async_copy(f_hbm.at[part], f_ref.at[part], sems.at[0, c]),
+                pltpu.make_async_copy(k_hbm.at[part], k_ref.at[part], sems.at[1, c]),
+                pltpu.make_async_copy(v_hbm.at[:, part], v_ref.at[:, part], sems.at[2, c]),
+            ]
+        )
+        for copy in copies[-1]:
+            copy.start()
 
     def rest(u):
         return u - u.astype(bf16).astype(f32)
 
-    for g in range(PACK // 4):
+    def faces(g, carry):
         tails, heads = [], []
         for i in range(4):
             x = 4 * g + i
@@ -295,8 +321,9 @@
             ).astype(bf16)
         ylo_ref[g, 4] = jnp.concatenate(tails, axis=0).astype(bf16)
         yhi_ref[g, 4] = jnp.concatenate(heads, axis=0).astype(bf16)
-
-    def x_side(at, out, near, outer, low, high):
+        return carry
+
+    def x_side(at, out, near, outer):
         for i in range(W):
             out[i] = f_ref[at + i].astype(bf16)
             out[W + i] = k_ref[at + i]
@@ -309,59 +336,64 @@
                 out[4 * W + i] = v_ref[2, at + i]
         half = jnp.zeros((16, NZ), f32)
         out[5 * W] = jnp.concatenate([half + margin_ref[0, 0].astype(f32), half + margin_ref[0, 1].astype(f32)], axis=0).astype(bf16)
+
+    for c in range(BX // PACK):
+        for copy in copies[c]:
+            copy.wait()
+        lax.fori_loop(c * PACK // 4, (c + 1) * PACK // 4, faces, 0)
+        if c == 0:
+            x_side(0, xhi_ref, (0, 1), W - 1)
+    x_side(BX - W, xlo_ref, (W - 1, W - 2), 0)
+
+
+def corner_body(xl_ref, xh_ref, up_ref, down_ref):
+    f32 = jnp.float32
+    for side, ref in enumerate((xl_ref, xh_ref)):
         for n in range(5):
-            planes = [
-                (f_ref[at + i] if n == 0 else k_ref[at + i] if n == 1 else v_ref[n - 2, at + i]).astype(f32)
-                for i in range(W)
-            ]
-            low[n] = jnp.concatenate([a[t:] for a in planes], axis=0).astype(bf16)
-            high[n] = jnp.concatenate([a[:W] for a in planes], axis=0).astype(bf16)
-
-    @pl.when(step == 0)
-    def _():
-        x_side(0, xhi_ref, (0, 1), W - 1, hl_ref, hh_ref)
-
-    @pl.when(step == BX // PACK - 1)
-    def _():
-        x_side(PACK - W, xlo_ref, (W - 1, W - 2), 0, ll_ref, lh_ref)
+            planes = [ref[n * W + i].astype(f32) for i in range(W)]
+            up_ref[side * 5 + n] = jnp.concatenate([a[BY - W :] for a in planes], axis=0).astype(jnp.bfloat16)
+            down_ref[side * 5 + n] = jnp.concatenate([a[:W] for a in planes], axis=0).astype(jnp.bfloat16)
 
 
 PACK = 16
+PACK_VMEM = 61
+STEP_VMEM = 48
 
 
 def halo_parts(field, diffusivity, velocity, margin):
     bf16 = jnp.bfloat16
     y_shape = (BX // 4, 5, 16, NZ)
-    y_spec = pl.BlockSpec((PACK // 4, 5, 16, NZ), lambda g: (g, 0, 0, 0))
     x_shape = (5 * W + 1, BY, NZ)
-    x_spec = pl.BlockSpec(x_shape, lambda g: (0, 0, 0))
-    c_shape = (5, 16, NZ)
-    c_spec = pl.BlockSpec(c_shape, lambda g: (0, 0, 0))
-    planes = pl.BlockSpec((PACK, BY, NZ), lambda g: (g, 0, 0))
-    ylo, yhi, xlo, xhi, ll, lh, hl, hh = pl.pallas_call(
+    c_shape = (10, 16, NZ)
+    vmem = pl.BlockSpec(memory_space=pltpu.VMEM)
+    hbm = pl.BlockSpec(memory_space=pltpu.HBM)
+    ylo, yhi, xlo, xhi = pl.pallas_call(
         pack_body,
-        grid=(BX // PACK,),
-        out_shape=[jax.ShapeDtypeStruct(s, bf16) for s in [y_shape] * 2 + [x_shape] * 2 + [c_shape] * 4],
-        in_specs=[
-            pl.BlockSpec(memory_space=pltpu.SMEM),
-            planes,
-            planes,
-            pl.BlockSpec((3, PACK, BY, NZ), lambda g: (0, g, 0, 0)),
+        out_shape=[jax.ShapeDtypeStruct(s, bf16) for s in [y_shape] * 2 + [x_shape] * 2],
+        in_specs=[pl.BlockSpec(memory_space=pltpu.SMEM), hbm, hbm, hbm],
+        out_specs=[vmem] * 4,
+        scratch_shapes=[
+            pltpu.VMEM((BX, BY, NZ), jnp.float32),
+            pltpu.VMEM((BX, BY, NZ), bf16),
+            pltpu.VMEM((3, BX, BY, NZ), bf16),
+            pltpu.SemaphoreType.DMA((3, BX // PACK)),
         ],
-        out_specs=[y_spec] * 2 + [x_spec] * 2 + [c_spec] * 4,
-        compiler_params=pltpu.CompilerParams(vmem_limit_bytes=40 * 1024 * 1024),
+        compiler_params=pltpu.CompilerParams(vmem_limit_bytes=PACK_VMEM * 1024 * 1024),
         name="pack_faces",
     )(margin, field, diffusivity, velocity)
-    return (
-        shift(ylo, "py", 1),
-        shift(yhi, "py", -1),
-        shift(xlo, "px", 1),
-        shift(xhi, "px", -1),
-        shift_both(ll, 1, 1),
-        shift_both(lh, 1, -1),
-        shift_both(hl, -1, 1),
-        shift_both(hh, -1, -1),
-    )
+    xl = shift(xlo, "px", 1)
+    xh = shift(xhi, "px", -1)
+    yl = shift(ylo, "py", 1)
+    yh = shift(yhi, "py", -1)
+    c_up, c_down = pl.pallas_call(
+        corner_body,
+        out_shape=[jax.ShapeDtypeStruct(c_shape, bf16)] * 2,
+        in_specs=[vmem] * 2,
+        out_specs=[vmem] * 2,
+        compiler_params=pltpu.CompilerParams(vmem_limit_bytes=4 * 1024 * 1024),
+        name="pack_corners",
+    )(xl, xh)
+    return yl, yh, xl, xh, shift(c_up, "py", 1), shift(c_down, "py", -1)
 
 
 def mm(a, b):
@@ -402,18 +434,18 @@
     diag, up, down, couple = [
         lax.dynamic_index_in_dim(jnp.asarray(t), q, 0, keepdims=False) for t in y_tables(count_y)
     ]
-    advected, zfit = time_steps(masks, field, diffusivity, velocity, halos, jnp.asarray(fit_hi), jnp.asarray(fit_lo))
-
-    lines = zfit.reshape(BX, BY * MZ)
-    out = mm(send, lines)
+    advected, zfit, out = time_steps(
+        masks, field, diffusivity, velocity, halos, send, jnp.asarray(fit_hi), jnp.asarray(fit_lo)
+    )
+
     from_low = shift(out[:13], "px", 1)
     from_high = shift(out[13:], "px", -1)
     from_low2 = shift(out[:6].astype(jnp.bfloat16), "px", 2)
     from_high2 = shift(out[13:19].astype(jnp.bfloat16), "px", -2)
     stacked = jnp.concatenate(
-        [lines, from_low, from_high, from_low2.astype(jnp.float32), from_high2.astype(jnp.float32)], axis=0
+        [zfit, from_low, from_high, from_low2.astype(jnp.float32), from_high2.astype(jnp.float32)], axis=0
     )
-    xfit = mm(full, stacked).reshape(BX // 2, BY, MZ)
+    xfit = jnp.einsum("kx,xyz->kyz", full, stacked, precision=HIGH)
 
     both = jnp.einsum("cy,xyz->cxz", jnp.concatenate([up, down], axis=0), xfit, precision=HIGH)
     head = lax.reduce_precision(both, 8, 7)

time: 105 us -> 93.5 us (0.89)
  local copies, waits for them, and re-layouts: 14.7 us -> 5.04 us
  starting transfers between devices: 34.3 us -> 27.3 us
  Pallas kernels: 28.8 us -> 33 us
  waiting for transfers between devices: 10.3 us -> 13.5 us
    ppermute x4 -> x0, starting transfers between devices: 12.4 us -> none  [shift_both(): return lax.ppermute(a, ('px', 'py'), pairs)]
    unnamed x30 -> x17, local copies, waits for them, and re-layouts: 7.76 us -> 0.14 us
    ppermute x8 -> x10, starting transfers between devices: 15.9 us -> 20.6 us  [shift(): return lax.ppermute(a, axis, ring(lax.axis_size(axis), d))]
    pallas_call x1 -> x2, Pallas kernels: 1.48 us -> 5.17 us  [the longest x1 5.12 us: halo_parts(): pl.pallas_call(pack_body, out_shape=[jax.ShapeDtypeStruct(s, bf16) for s...]
    dot_general x4 -> x2, matrix products: 5.26 us -> 1.79 us  [mm(): return jnp.dot(a, b, precision=HIGH, preferred_element_type=jnp.float32)]
    ppermute x8 -> x10, waiting for transfers between devices: 0.74 us -> 3.88 us  [shift(): return lax.ppermute(a, axis, ring(lax.axis_size(axis), d))]
    dot_general x0 -> x1, matrix products: none -> 1.89 us  [per_device(): xfit = jnp.einsum('kx,xyz->kyz', full, stacked, precision=HIGH)]
    concatenate x1 -> x0, local copies, waits for them, and re-layouts: 1.42 us -> none  [per_device(): jnp.concatenate([lines, from_low, from_high, from_low2.astype(jnp.float32...]
  transfers between devices with their start and end apart: 13 -> 11, of which waited for: 2 -> 4; matrix products, arithmetic and copies ran while one was open for 10% -> 9% of each run, Pallas kernels for 0% -> 0%
where the time goes in v2:
time: 93.5 us; the launch traced here: 92.8 us
  Pallas kernels  33 us (35%)
  starting transfers between devices  27.3 us (29%)
  waiting for transfers between devices  13.5 us (14%)
  matrix products  7.46 us (8%)
  local copies, waits for them, and re-layouts  5.04 us (5%)
  between operations  4.69 us (5%)
  other arithmetic  1.85 us (2%)
    pallas_call x1, Pallas kernels, time_steps(): pl.pallas_call(stencil_body, out_shape=(jax.ShapeDtypeStruct((BX, BY, NZ)...  27.8 us
    ppermute x10, starting transfers between devices, shift(): return lax.ppermute(a, axis, ring(lax.axis_size(axis), d))  20.6 us
    all_to_all x1, waiting for transfers between devices, per_device(): got = lax.all_to_all(carries, 'py', split_axis=0, concat_axis=0, tiled=True)  9.59 us
    all_to_all x1, starting transfers between devices, per_device(): got = lax.all_to_all(carries, 'py', split_axis=0, concat_axis=0, tiled=True)  6.71 us
    pallas_call x1, Pallas kernels, halo_parts(): pl.pallas_call(pack_body, out_shape=[jax.ShapeDtypeStruct(s, bf16) for s...  5.12 us
    ppermute x10, waiting for transfers between devices, shift(): return lax.ppermute(a, axis, ring(lax.axis_size(axis), d))  3.88 us
    dot_general x1, matrix products, per_device(): xfit = jnp.einsum('kx,xyz->kyz', full, stacked, precision=HIGH)  1.89 us
  transfers between devices with their start and end apart: 11, of which 4 were waited for; matrix products, arithmetic and copies ran while one was open for 9% of the time, Pallas kernels for 0%

profile of v2, /device:TPU:0, one launch (start us, length us, event | category | flops | bytes accessed | tf_op | source)
XLA Modules:
  0.0 92.8 jit_solution(2765645311225718540)
XLA Ops:
  0.7 5.1 %pack_faces.1 = (bf16[16,5,16,256]{3,2,1,0:T(8,128)(2,1)}, bf16[16,5,16,256]{3,2,1,0:T(8,128)(2,1)}, bf16[21,32,256]{2,1,0:T(8,128)(2,1)}, bf16[21,32,256]{2,1,0:T(8,128)(2,1)}) custom-call(s32[1,2]{1,0:T(1,128)} %margin_ref.1, f32[64,32,256]{2,1,0:T(8,128)} %f_ref.1, bf16[64,32,256]{2,1,0:T(8,128)(2,1)} %k_ref.1, bf16[3,64,32,256]{3,2,1,0:T(8,128)(2,1)} %v_ref.1), custom_call_target="tpu_custom_call" | custom-call | tf_op jit(solution)/shard_map/pack_faces/pallas_call | solution.py:370
  5.8 2.9 %collective-permute-start.3 = (bf16[21,32,256]{2,1,0:T(8,128)(2,1)}, bf16[21,32,256]{2,1,0:T(8,128)(2,1)S(1)}, u32[]{:S(2)}, u32[]{:S(2)}) collective-permute-start(bf16[21,32,256]{2,1,0:T(8,128)(2,1)} %get-tuple-element.14), channel_id=1, source_target_pairs={{0,112},{16,0},{32,16},{48,32},{64,48},{80,64},{96,80},{112,96},{1... | collective-permute-start | bytes 1032200 | tf_op jit(solution)/shard_map/ppermute | solution.py:283
  8.8 2.0 %collective-permute-start = (bf16[16,5,16,256]{3,2,1,0:T(8,128)(2,1)}, bf16[16,5,16,256]{3,2,1,0:T(8,128)(2,1)S(1)}, u32[]{:S(2)}, u32[]{:S(2)}) collective-permute-start(bf16[16,5,16,256]{3,2,1,0:T(8,128)(2,1)} %get-tuple-element.11), channel_id=1, source_target_pairs={{0,1},{1,2},{2,3},{3,4},{4,5},{5,6},{6,7},{7,8},{8,9},{9,10},{10,1... | collective-permute-start | bytes 1966088 | tf_op jit(solution)/shard_map/ppermute | solution.py:283
  10.8 4.6 %collective-permute-start.1 = (bf16[16,5,16,256]{3,2,1,0:T(8,128)(2,1)}, bf16[16,5,16,256]{3,2,1,0:T(8,128)(2,1)S(1)}, u32[]{:S(2)}, u32[]{:S(2)}) collective-permute-start(bf16[16,5,16,256]{3,2,1,0:T(8,128)(2,1)} %get-tuple-element.12), channel_id=1, source_target_pairs={{0,15},{1,0},{2,1},{3,2},{4,3},{5,4},{6,5},{7,6},{8,7},{9,8},{10,9... | collective-permute-start | bytes 1966088 | tf_op jit(solution)/shard_map/ppermute | solution.py:283
  15.9 0.6 fusion.28
  17.8 1.3 %dynamic-slice_bitcast_fusion.6 = (f32[3,32]{1,0:T(4,128)}, f32[3,32]{1,0:T(4,128)}) fusion(f32[16,3,32]{2,1,0:T(4,128)} %constant.80.clone, s32[]{:T(128)S(6)} %select_n.57, f32[16,3,32]{2,1,0:T(4,128)} %constant.79.clone), kind=kLoop, calls=%fused_computation.33 | loop fusion | bytes 1540 | tf_op jit(solution)/shard_map/jit(dynamic_index_in_dim)/squeeze | solution.py:435
  19.1 0.7 dynamic-slice_bitcast_fusion
  19.9 0.7 dynamic-slice_bitcast_fusion.1.send_ref
  24.5 5.3 %collective-permute-start.5 = (bf16[10,16,256]{2,1,0:T(8,128)(2,1)S(1)}, bf16[10,16,256]{2,1,0:T(8,128)(2,1)S(1)}, u32[]{:S(2)}, u32[]{:S(2)}) collective-permute-start(bf16[10,16,256]{2,1,0:T(8,128)(2,1)S(1)} %get-tuple-element.16), channel_id=1, source_target_pairs={{0,15},{1,0},{2,1},{3,2},{4,3},{5,4},{6,5},{7,6},{8,7},{9,8},{10,9... | collective-permute-start | bytes 245768 | tf_op jit(solution)/shard_map/ppermute | solution.py:283
  29.8 0.9 convolution_add_fusion.2
  30.7 0.9 fusion.3
  31.6 0.6 collective-permute-done.4.cl_ref
  32.3 27.8 %time_steps.1 = (f32[64,32,256]{2,1,0:T(8,128)}, f32[64,32,128]{2,1,0:T(8,128)S(1)}, f32[26,32,128]{2,1,0:T(8,128)S(1)}) custom-call(f32[4]{0:T(128)S(1)} %add_convert_fusion.mask_ref, f32[64,32,256]{2,1,0:T(8,128)} %f_ref.1, bf16[64,32,256]{2,1,0:T(8,128)(2,1)S(1)} %copy-done, bf16[3,64,32,256]{3,2,1,0:T(8,128)(2,1)} %v_ref.1, ...), custom_call_target="tpu_custom_call" | custom-call | tf_op jit(solution)/shard_map/time_steps/pallas_call | solution.py:263
  60.2 1.6 %collective-permute-start.9 = (bf16[6,32,128]{2,1,0:T(8,128)(2,1)S(1)}, bf16[6,32,128]{2,1,0:T(8,128)(2,1)S(1)}, u32[]{:S(2)}, u32[]{:S(2)}) collective-permute-start(bf16[6,32,128]{2,1,0:T(8,128)(2,1)S(1)} %get-tuple-element.22), channel_id=1, source_target_pairs={{0,96},{16,112},{32,0},{48,16},{64,32},{80,48},{96,64},{112,80},{1... | collective-permute-start | bytes 147464 | tf_op jit(solution)/shard_map/ppermute | solution.py:283
  62.3 3.6 %collective-permute-start.7 = (f32[13,32,128]{2,1,0:T(8,128)S(1)}, f32[13,32,128]{2,1,0:T(8,128)S(1)}, u32[]{:S(2)}, u32[]{:S(2)}) collective-permute-start(f32[13,32,128]{2,1,0:T(8,128)S(1)} %get-tuple-element.20), channel_id=1, source_target_pairs={{0,112},{16,0},{32,16},{48,32},{64,48},{80,64},{96,80},{112,96},{1... | collective-permute-start | bytes 638984 | tf_op jit(solution)/shard_map/ppermute | solution.py:283
  66.0 0.7 collective-permute-done.6
  66.7 2.6 %collective-permute-done.7 = f32[13,32,128]{2,1,0:T(8,128)S(1)} collective-permute-done((f32[13,32,128]{2,1,0:T(8,128)S(1)}, f32[13,32,128]{2,1,0:T(8,128)S(1)}, u32[]{:S(2)}, u32[]{:S(2)}) %collective-permute-start.7) | collective-permute-done | bytes 213024 | tf_op jit(solution)/shard_map/ppermute | solution.py:283
  69.3 1.9 %fusion = f32[32,32,128]{2,0,1:T(8,128)S(1)} fusion(f32[32,102,1]{1,0,2:T(8,128)S(1)} %fusion.3, f32[102,32,128]{2,1,0:T(8,128)S(1)} %convert_dynamic-update-slice_fusion), kind=kOutput, calls=%fused_computation | convolution fusion | flops 160432128 | bytes 2208512 | tf_op jit(solution)/shard_map/kx,xyz->kyz/dot_general | solution.py:448
  71.2 0.6 fusion.23
  72.1 1.1 %select_convert_fusion = bf16[16,4,32,128]{3,1,2,0:T(4,128)(2,1)} fusion(bf16[4,32,128]{2,0,1:T(4,128)(2,1)S(1)} %pad_maximum_fusion.1, bf16[4,32,128]{2,0,1:T(4,128)(2,1)S(1)} %pad_maximum_fusion, pred[16]{0:T(512)(128)(4,1)S(1)} %copy-done.6), kind=kLoop, calls=%fused_computation.7 | loop fusion | flops 262144 | bytes 589840 | tf_op jit(solution)/shard_map/convert_element_type | solution.py:458
  73.1 6.7 %all-to-all-start = ((bf16[16,4,32,128]{3,1,2,0:T(4,128)(2,1)}), bf16[16,4,32,128]{3,1,2,0:T(4,128)(2,1)S(1)}, u32[]{:S(2)}, u32[]{:S(2)}) async-start(bf16[16,4,32,128]{3,1,2,0:T(4,128)(2,1)} %select_convert_fusion), calls=%async_computation | async-start | bytes 1048576 | tf_op jit(solution)/shard_map/all_to_all | solution.py:459
  79.8 1.4 %fusion.6 = f32[32,128,16]{1,2,0:T(8,128)S(1)} fusion(f32[32,32,128]{2,0,1:T(8,128)S(1)} %fusion, f32[16,16,32]{2,1,0:T(8,128)} %constant.78.clone, s32[]{:T(128)S(6)} %select_n.57), kind=kOutput, calls=%fused_computation.10 | convolution fusion | flops 25165824 | bytes 794628 | tf_op jit(solution)/shard_map/my,xyz->xmz/dot_general | solution.py:460
  81.2 9.6 %all-to-all-done = bf16[16,4,32,128]{3,1,2,0:T(4,128)(2,1)S(1)} async-done(((bf16[16,4,32,128]{3,1,2,0:T(4,128)(2,1)}), bf16[16,4,32,128]{3,1,2,0:T(4,128)(2,1)S(1)}, u32[]{:S(2)}, u32[]{:S(2)}) %all-to-all-start) | async-done | bytes 524320 | tf_op jit(solution)/shard_map/all_to_all | solution.py:459
  91.1 1.7 %fusion.2 = f32[32,16,128]{2,1,0:T(8,128)} fusion(f32[32,128,16]{1,2,0:T(8,128)S(1)} %fusion.6, bf16[64,32,128]{2,0,1:T(8,128)(2,1)S(1)} %bitcast.44, f32[16,16,64]{2,1,0:T(8,128)} %constant.81.clone, s32[]{:T(128)S(6)} %select_n.57), kind=kOutput, calls=%fused_computation.3 | convolution fusion | flops 50397184 | bytes 1056772 | tf_op jit(solution)/shard_map/mc,cxz->xmz/dot_general | solution.py:461
  (47 shorter events, 3.2 us)
Async XLA Ops:
  0.6 31.6 %copy-start.1 = (bf16[256,128]{1,0:T(8,128)(2,1)S(1)}, bf16[256,128]{1,0:T(8,128)(2,1)}, u32[]{:S(2)}) copy-start(bf16[256,128]{1,0:T(8,128)(2,1)} %constant.83.clone.fit_lo_ref) | copy-start | bytes 196612
  0.6 31.6 %copy-start.2 = (bf16[256,128]{1,0:T(8,128)(2,1)S(1)}, bf16[256,128]{1,0:T(8,128)(2,1)}, u32[]{:S(2)}) copy-start(bf16[256,128]{1,0:T(8,128)(2,1)} %constant.82.clone.fit_hi_ref) | copy-start | bytes 196612
  0.7 14.7 %copy-start.5 = (s32[1,2]{1,0:T(1,128)S(1)}, s32[1,2]{1,0:T(1,128)}, u32[]{:S(2)}) copy-start(s32[1,2]{1,0:T(1,128)} %margin_ref.1) | copy-start | bytes 28
  0.7 31.6 %copy-start = (bf16[64,32,256]{2,1,0:T(8,128)(2,1)S(1)}, bf16[64,32,256]{2,1,0:T(8,128)(2,1)}, u32[]{:S(2)}) copy-start(bf16[64,32,256]{2,1,0:T(8,128)(2,1)} %k_ref.1) | copy-start | bytes 3145732
  5.8 14.8 %collective-permute-start.2 = (bf16[21,32,256]{2,1,0:T(8,128)(2,1)}, bf16[21,32,256]{2,1,0:T(8,128)(2,1)S(1)}, u32[]{:S(2)}, u32[]{:S(2)}) collective-permute-start(bf16[21,32,256]{2,1,0:T(8,128)(2,1)} %get-tuple-element.13), channel_id=1, source_target_pairs={{0,16},{16,32},{32,48},{48,64},{64,80},{80,96},{96,112},{112,0},{1... | collective-permute-start | bytes 1032200 | tf_op jit(solution)/shard_map/ppermute | solution.py:283
  5.8 14.8 %collective-permute-start.3 = (bf16[21,32,256]{2,1,0:T(8,128)(2,1)}, bf16[21,32,256]{2,1,0:T(8,128)(2,1)S(1)}, u32[]{:S(2)}, u32[]{:S(2)}) collective-permute-start(bf16[21,32,256]{2,1,0:T(8,128)(2,1)} %get-tuple-element.14), channel_id=1, source_target_pairs={{0,112},{16,0},{32,16},{48,32},{64,48},{80,64},{96,80},{112,96},{1... | collective-permute-start | bytes 1032200 | tf_op jit(solution)/shard_map/ppermute | solution.py:283
  8.8 23.4 %collective-permute-start = (bf16[16,5,16,256]{3,2,1,0:T(8,128)(2,1)}, bf16[16,5,16,256]{3,2,1,0:T(8,128)(2,1)S(1)}, u32[]{:S(2)}, u32[]{:S(2)}) collective-permute-start(bf16[16,5,16,256]{3,2,1,0:T(8,128)(2,1)} %get-tuple-element.11), channel_id=1, source_target_pairs={{0,1},{1,2},{2,3},{3,4},{4,5},{5,6},{6,7},{7,8},{8,9},{9,10},{10,1... | collective-permute-start | bytes 1966088 | tf_op jit(solution)/shard_map/ppermute | solution.py:283
  10.8 21.4 %collective-permute-start.1 = (bf16[16,5,16,256]{3,2,1,0:T(8,128)(2,1)}, bf16[16,5,16,256]{3,2,1,0:T(8,128)(2,1)S(1)}, u32[]{:S(2)}, u32[]{:S(2)}) collective-permute-start(bf16[16,5,16,256]{3,2,1,0:T(8,128)(2,1)} %get-tuple-element.12), channel_id=1, source_target_pairs={{0,15},{1,0},{2,1},{3,2},{4,3},{5,4},{6,5},{7,6},{8,7},{9,8},{10,9... | collective-permute-start | bytes 1966088 | tf_op jit(solution)/shard_map/ppermute | solution.py:283
  24.4 7.8 %collective-permute-start.4 = (bf16[10,16,256]{2,1,0:T(8,128)(2,1)S(1)}, bf16[10,16,256]{2,1,0:T(8,128)(2,1)S(1)}, u32[]{:S(2)}, u32[]{:S(2)}) collective-permute-start(bf16[10,16,256]{2,1,0:T(8,128)(2,1)S(1)} %get-tuple-element.15), channel_id=1, source_target_pairs={{0,1},{1,2},{2,3},{3,4},{4,5},{5,6},{6,7},{7,8},{8,9},{9,10},{10,1... | collective-permute-start | bytes 245768 | tf_op jit(solution)/shard_map/ppermute | solution.py:283
  24.5 7.8 %collective-permute-start.5 = (bf16[10,16,256]{2,1,0:T(8,128)(2,1)S(1)}, bf16[10,16,256]{2,1,0:T(8,128)(2,1)S(1)}, u32[]{:S(2)}, u32[]{:S(2)}) collective-permute-start(bf16[10,16,256]{2,1,0:T(8,128)(2,1)S(1)} %get-tuple-element.16), channel_id=1, source_target_pairs={{0,15},{1,0},{2,1},{3,2},{4,3},{5,4},{6,5},{7,6},{8,7},{9,8},{10,9... | collective-permute-start | bytes 245768 | tf_op jit(solution)/shard_map/ppermute | solution.py:283
  60.1 6.5 %collective-permute-start.6 = (f32[13,32,128]{2,1,0:T(8,128)S(1)}, f32[13,32,128]{2,1,0:T(8,128)S(1)}, u32[]{:S(2)}, u32[]{:S(2)}) collective-permute-start(f32[13,32,128]{2,1,0:T(8,128)S(1)} %get-tuple-element.21), channel_id=1, source_target_pairs={{0,16},{16,32},{32,48},{48,64},{64,80},{80,96},{96,112},{112,0},{1... | collective-permute-start | bytes 638984 | tf_op jit(solution)/shard_map/ppermute | solution.py:283
  60.2 9.1 %collective-permute-start.9 = (bf16[6,32,128]{2,1,0:T(8,128)(2,1)S(1)}, bf16[6,32,128]{2,1,0:T(8,128)(2,1)S(1)}, u32[]{:S(2)}, u32[]{:S(2)}) collective-permute-start(bf16[6,32,128]{2,1,0:T(8,128)(2,1)S(1)} %get-tuple-element.22), channel_id=1, source_target_pairs={{0,96},{16,112},{32,0},{48,16},{64,32},{80,48},{96,64},{112,80},{1... | collective-permute-start | bytes 147464 | tf_op jit(solution)/shard_map/ppermute | solution.py:283
  61.8 7.4 %collective-permute-start.8 = (bf16[6,32,128]{2,1,0:T(8,128)(2,1)S(1)}, bf16[6,32,128]{2,1,0:T(8,128)(2,1)S(1)}, u32[]{:S(2)}, u32[]{:S(2)}) collective-permute-start(bf16[6,32,128]{2,1,0:T(8,128)(2,1)S(1)} %get-tuple-element.23), channel_id=1, source_target_pairs={{0,32},{16,48},{32,64},{48,80},{64,96},{80,112},{96,0},{112,16},{1... | collective-permute-start | bytes 147464 | tf_op jit(solution)/shard_map/ppermute | solution.py:283
  62.3 6.9 %collective-permute-start.7 = (f32[13,32,128]{2,1,0:T(8,128)S(1)}, f32[13,32,128]{2,1,0:T(8,128)S(1)}, u32[]{:S(2)}, u32[]{:S(2)}) collective-permute-start(f32[13,32,128]{2,1,0:T(8,128)S(1)} %get-tuple-element.20), channel_id=1, source_target_pairs={{0,112},{16,0},{32,16},{48,32},{64,48},{80,64},{96,80},{112,96},{1... | collective-permute-start | bytes 638984 | tf_op jit(solution)/shard_map/ppermute | solution.py:283
  65.9 5.3 %copy-start.3 = (f32[3,32]{1,0:T(4,128)S(1)}, f32[3,32]{1,0:T(4,128)}, u32[]{:S(2)}) copy-start(f32[3,32]{1,0:T(4,128)} %get-tuple-element.38) | copy-start | bytes 1156
  65.9 5.3 %copy-start.4 = (f32[3,32]{1,0:T(4,128)S(1)}, f32[3,32]{1,0:T(4,128)}, u32[]{:S(2)}) copy-start(f32[3,32]{1,0:T(4,128)} %get-tuple-element.39) | copy-start | bytes 1156
  69.3 2.7 %copy-start.6 = (pred[16]{0:T(512)(128)(4,1)S(1)}, pred[16]{0:T(512)(128)(4,1)}, u32[]{:S(2)}) copy-start(pred[16]{0:T(512)(128)(4,1)} %iota_compare_fusion) | copy-start | bytes 52
  73.1 17.7 %all-to-all-start = ((bf16[16,4,32,128]{3,1,2,0:T(4,128)(2,1)}), bf16[16,4,32,128]{3,1,2,0:T(4,128)(2,1)S(1)}, u32[]{:S(2)}, u32[]{:S(2)}) async-start(bf16[16,4,32,128]{3,1,2,0:T(4,128)(2,1)} %select_convert_fusion), calls=%async_computation | async-start | bytes 1048576 | tf_op jit(solution)/shard_map/all_to_all | solution.py:459

commit v3 on v2

v3 whole, which is shorter than its diff:
```python
import functools

import jax
import jax.numpy as jnp
import numpy as np
from jax import lax
from jax.experimental import pallas as pl
from jax.experimental.pallas import tpu as pltpu
from jax.sharding import PartitionSpec as P

STEPS = 4
OVMAX = 4
BX = 64
BY = 32
NZ = 256
MZ = 128
W = 4
EX = BX + 2 * W
EY = BY + 2 * W
YR = BY // 2 + 6
LINES = YR * 128


PACK = 16
PACK_VMEM = 12
STEP_VMEM = 16


def bspline(t):
    m = np.abs(t)
    inner = (4.0 - 6.0 * m * m + 3.0 * m**3) / 6.0
    outer = np.maximum(2.0 - m, 0.0) ** 3 / 6.0
    return np.where(m < 1.0, inner, outer)


def basis(n):
    j = np.arange(n)[:, None]
    k = np.arange(n // 2)[None, :]
    return bspline((j - 2.0 * k - 0.5) / 2.0)


def fit_matrix(n):
    b = basis(n)
    return np.linalg.solve(b.T @ b, b.T)


def split(a):
    a = a.astype(np.float32)
    hi = a.astype(jnp.bfloat16)
    return hi, (a - hi.astype(np.float32)).astype(jnp.bfloat16)


def y_tables(count):
    total = count * BY
    s = fit_matrix(total)
    own = BY // 2
    rows = np.zeros((count, YR, BY))
    couple = np.zeros((count, own, count, 4))
    for q in range(count):
        cols = s[:, q * BY : (q + 1) * BY]
        rows[q, :own] = cols[q * own : (q + 1) * own]
        for at, far, targets in ((own, cols[(q + 1) * own :], range(q + 1, count)), (own + 3, cols[: q * own], range(q))):
            if len(targets) == 0:
                continue
            u, sv, vt = np.linalg.svd(far, full_matrices=False)
            assert sv[3] < 1e-10 * sv[0]
            rows[q, at : at + 3] = vt[:3]
            left = (u[:, :3] * sv[:3]).reshape(len(targets), own, 3)
            for i, t in enumerate(targets):
                couple[t, :, q, :3] = left[i]
                couple[t, :, q, 3] = left[i, :, 0]
    table = np.einsum("qry,xw->qrxwy", rows, np.eye(8)).reshape(count, YR * 8, 8 * BY)
    return np.stack(split(table), axis=1), couple.reshape(count, own, count * 4).astype(np.float32)


def x_tables(count):
    total = count * BX
    block = BX // 2
    ctrl = total // 2
    b = basis(total)
    width = block + 2 * OVMAX
    gpad = np.zeros((ctrl + 16, ctrl + 16))
    gpad[8:-8, 8:-8] = b.T @ b
    bt = bspline((np.arange(BX)[None] - 2.0 * (np.arange(block + 4)[:, None] - 2) - 0.5) / 2.0)
    base, send, near = [], [], []
    for cls, p in enumerate((0, 1, count - 1)):
        has_low = float(cls != 0)
        has_high = float(cls != 2)
        start = p * block
        knots = start - OVMAX + np.arange(width)
        lo = start - OVMAX + 8
        full = gpad[lo : lo + width, lo : lo + width]
        band = gpad[lo : lo + width, lo - 3 : lo + width + 3]
        for m0 in range(OVMAX + 1):
            for m1 in range(OVMAX + 1):
                inside = (knots >= start - m0) & (knots < start + block + m1) & (knots >= 0) & (knots < ctrl)
                w = inside.astype(np.float64)
                mat = full * w[:, None] * w[None, :] + np.diag(1.0 - w)
                e = (np.linalg.inv(mat) * w[None, :])[OVMAX : OVMAX + block]
                q = e @ band
                ql = q[:, :7] * has_low
                qr = q[:, 7 + block :] * has_high
                two = 2.0 * e - q[:, 7 : 7 + block] @ e
                low = two[:, 0:6] * has_low
                high = two[:, block + 2 :] * has_high
                gap3 = np.zeros((block, 3))
                gap32 = np.zeros((block, 32))
                base.append(np.concatenate([two[:, 2 : block + 6] @ bt, low, -ql, gap3, high, -qr, gap3, gap32], axis=1))
                pad = np.zeros((3, BX))
                send.append(
                    np.concatenate(
                        [bt[block - 2 :], e[block - 7 :, 2 : block + 6] @ bt, pad, bt[:6], e[:7, 2 : block + 6] @ bt, pad]
                    )
                )
                both = np.zeros((2, 8, 128))
                both[0, :7, :BX] = e[block - 7 :, block + 2 :] @ bt[0:6]
                both[0, :7, 96:102] = e[block - 7 :, 0:6] * has_low
                both[1, :7, :BX] = e[:7, 0:6] @ bt[block - 2 :]
                both[1, :7, 112:118] = e[:7, block + 2 :] * has_high
                near.append(both)
    return [np.stack(t).astype(np.float32) for t in (base, send, near)]


def z_shifts(rows):
    lane = lax.broadcasted_iota(jnp.int32, (rows, 128), 1)
    first = lane == 0
    final = lane == 127

    def z_up(a):
        lo = pltpu.roll(a[:, :128], 1, 1)
        hi = pltpu.roll(a[:, 128:], 1, 1)
        return jnp.concatenate([jnp.where(first, 0.0, lo), jnp.where(first, lo, hi)], axis=1)

    def z_down(a):
        lo = pltpu.roll(a[:, :128], 127, 1)
        hi = pltpu.roll(a[:, 128:], 127, 1)
        return jnp.concatenate([jnp.where(final, hi, lo), jnp.where(final, 0.0, hi)], axis=1)

    return z_up, z_down


def own_rows(k, kx_low, kx, refs, x):
    kx_s, ky_s, kyd_s, kz_s, kzd_s, c_s = refs
    z_up, z_down = z_shifts(BY)
    row = lax.broadcasted_iota(jnp.int32, (BY, NZ), 0)
    own = slice(0, BY)
    ky = jnp.where(row < BY - 1, 0.05 * (k + pltpu.roll(k, BY - 1, 0)), 0.0)
    kyd = pltpu.roll(ky, 1, 0)
    kz = 0.05 * (k + z_down(k))
    kzd = 0.05 * (k + z_up(k))
    kx_s[x, own] = kx
    ky_s[x, own] = ky
    kyd_s[x, own] = kyd
    kz_s[x, own] = kz
    kzd_s[x, own] = kzd
    c_s[x, own] = 1.0 - ((kx + kx_low) + (ky + kyd) + (kz + kzd))


def load(sources, targets, sems):
    copies = []
    for c in range(BX // PACK):
        part = pl.ds(c * PACK, PACK)
        copies.append([])
        for n, (src, dst) in enumerate(zip(sources, targets)):
            at = (slice(None), part) if len(src.shape) == 4 else (part,)
            copies[-1].append(pltpu.make_async_copy(src.at[at], dst.at[at], sems.at[n, c]))
            copies[-1][-1].start()
    return copies


def own_body(f_hbm, k_hbm, v_hbm, after_ref, u_s, v0_s, v1_s, v2_s, kx_s, ky_s, kyd_s, kz_s, kzd_s, c_s, edge_s, end_ref,
             f_ref, k_ref, v_ref, sems):
    f32 = jnp.float32
    for part in load((f_hbm, k_hbm, v_hbm), (f_ref, k_ref, v_ref), sems):
        for copy in part:
            copy.wait()
    refs = (kx_s, ky_s, kyd_s, kz_s, kzd_s, c_s)

    def plane(x, carry):
        k, kx_low = carry
        k_next = k_ref[jnp.minimum(x + 1, BX - 1)].astype(f32)
        kx = jnp.where(x < BX - 1, 0.05, 0.0) * (k + k_next)
        u_s[x + W, 0:BY] = f_ref[x]
        for n, ref in enumerate((v0_s, v1_s, v2_s)):
            ref[x + W, 0:BY] = v_ref[n, x].astype(f32)
        edge_s[x + W, 0:8] = k[0:8]
        edge_s[x + W, 8:16] = k[BY - 8 :]
        own_rows(k, kx_low, kx, refs, x + W)
        return k_next, kx

    lax.fori_loop(0, BX, plane, (k_ref[0].astype(f32), jnp.zeros((BY, NZ), f32)), unroll=4)
    end_ref[0] = k_ref[0].astype(f32)
    end_ref[1] = k_ref[BX - 1].astype(f32)


def dot3(a, b):
    dot = functools.partial(jnp.dot, preferred_element_type=jnp.float32)
    return dot(a[0], b[0]) + (dot(a[0], b[1]) + dot(a[1], b[0]))


def halves(a):
    hi = a.astype(jnp.bfloat16)
    return hi, (a - hi.astype(jnp.float32)).astype(jnp.bfloat16)


def place_of(owner, count, m0, m1):
    own = jnp.clip(owner, 0, count - 1)
    cls = jnp.where(own == 0, 0, jnp.where(own == count - 1, 2, 1))
    n = OVMAX + 1
    return (cls * n + jnp.clip(m0, 0, OVMAX)) * n + jnp.clip(m1, 0, OVMAX)


def stencil_body(count_x, count_y, margin_ref, yl_ref, yh_ref, xl_ref, xh_ref, cl_ref, ch_ref, fit_ref, base_hbm, send_hbm,
                 near_hbm, ytab_hbm, end_ref, *rest_refs):
    f32 = jnp.float32
    outs = rest_refs[KEPT:]
    adv_ref, zt_ref, lo_ref, hi_ref, lo2_ref, hi2_ref, full_ref = outs[:7]
    u_s, v0_s, v1_s, v2_s, kx_s, ky_s, kyd_s, kz_s, kzd_s, c_s, edge_s = outs[7 : 7 + KEPT]
    kh_s, kp_s, base_s, send_s, near_s, ytab_s, sems = outs[7 + KEPT :]
    p = lax.axis_index("px")
    q = lax.axis_index("py")

    def margins(ref):
        part = ref[5 * W].astype(f32)
        return [jnp.max(a).astype(jnp.int32) for a in (part[0:8], part[16:24])]

    mine = place_of(p, count_x, margin_ref[0, 0], margin_ref[0, 1])
    low = place_of(p - 1, count_x, *margins(xl_ref))
    high = place_of(p + 1, count_x, *margins(xh_ref))
    copies = [
        pltpu.make_async_copy(base_hbm.at[mine], base_s, sems.at[0]),
        pltpu.make_async_copy(send_hbm.at[mine], send_s, sems.at[1]),
        pltpu.make_async_copy(near_hbm.at[low, 0], near_s.at[0], sems.at[2]),
        pltpu.make_async_copy(near_hbm.at[high, 1], near_s.at[1], sems.at[3]),
        pltpu.make_async_copy(ytab_hbm.at[q], ytab_s, sems.at[4]),
    ]
    for copy in copies:
        copy.start()
    refs = (kx_s, ky_s, kyd_s, kz_s, kzd_s, c_s)
    from_low_x = jnp.where(p > 0, 1.0, 0.0)
    from_high_x = jnp.where(p < count_x - 1, 1.0, 0.0)
    from_low_y = jnp.where(q > 0, 1.0, 0.0)
    from_high_y = jnp.where(q < count_y - 1, 1.0, 0.0)
    beyond = slice(BY, EY)

    def halo_rows(group, carry):
        at = group * 4
        ul = yl_ref[group, 4].astype(f32) * from_low_y
        uh = yh_ref[group, 4].astype(f32) * from_high_y
        gap = jnp.zeros((4, NZ), f32)
        for i in range(4):
            x = at + i + W
            kl = yl_ref[group, i].astype(f32) * from_low_y
            kh = yh_ref[group, i].astype(f32) * from_high_y
            rest = jnp.concatenate([kh[7:8], kh[15:16], gap, kl[12:13], kl[4:5]], axis=0)
            u_s[x, beyond] = rest + jnp.concatenate([uh[4 * i : 4 * i + 4], ul[4 * i : 4 * i + 4]], axis=0)
            kh_s[x] = jnp.concatenate([kh[0:4], kl[0:4]], axis=0)
            for n, ref in enumerate((v0_s, v1_s, v2_s)):
                m = 4 * n + 4
                ref[x, beyond] = jnp.concatenate([kh[m : m + 4], kl[m : m + 4]], axis=0)
        return carry

    lax.fori_loop(0, BX // 4, halo_rows, 0)
    dest = (u_s, None, v0_s, v1_s, v2_s)
    for n in range(5):
        for base, ref, corner, scale, near, outer in (
            (0, xl_ref, 0, from_low_x, (W - 1, W - 2), 0),
            (BX + W, xh_ref, 5, from_high_x, (0, 1), W - 1),
        ):
            low = cl_ref[corner + n].astype(f32) * (scale * from_low_y)
            high = ch_ref[corner + n].astype(f32) * (scale * from_high_y)
            for i in range(W):
                value = ref[n * W + i].astype(f32)
                if n == 0 and i in near:
                    value = value + ref[(3 + near.index(i)) * W + outer].astype(f32)
                value = value * scale
                tile = jnp.concatenate([high[4 * i : 4 * i + 4], low[4 * i : 4 * i + 4]], axis=0)
                if n == 1:
                    kp_s[base % BX + i] = value
                    kh_s[base + i] = tile
                    edge_s[base + i, 0:8] = value[0:8]
                    edge_s[base + i, 8:16] = value[BY - 8 :]
                else:
                    dest[n][base + i, 0:BY] = value
                    dest[n][base + i, beyond] = tile

    kx_low = jnp.zeros((BY, NZ), f32)
    for i in range(W):
        k = kp_s[i]
        kx = 0.05 * (k + (kp_s[i + 1] if i < W - 1 else end_ref[0]))
        own_rows(k, kx_low, kx, refs, i)
        kx_low = kx
    c_s[W, 0:BY] = c_s[W, 0:BY] - kx_low
    kx_low = 0.05 * (end_ref[1] + kp_s[W])
    kx_s[BX + W - 1, 0:BY] = kx_low
    c_s[BX + W - 1, 0:BY] = c_s[BX + W - 1, 0:BY] - kx_low
    for i in range(W):
        k = kp_s[W + i]
        kx = 0.05 * (k + kp_s[min(W + i + 1, 2 * W - 1)])
        own_rows(k, kx_low, kx, refs, BX + W + i)
        kx_low = kx

    sub = lax.broadcasted_iota(jnp.int32, (8, NZ), 0)
    zt_up, zt_down = z_shifts(8)

    def halo_coefficients(x, carry):
        k, kx_low = carry
        k_next = kh_s[jnp.minimum(x + 1, EX - 1)]
        kx = 0.05 * (k + k_next)
        up = 0.05 * (edge_s[x, 8:16] + pltpu.roll(k, 7, 0))
        down = 0.05 * (edge_s[x, 0:8] + pltpu.roll(k, 1, 0))
        up = jnp.where(sub == 7, up, 0.0)
        down = jnp.where(sub == 0, down, 0.0)
        ky = jnp.where(sub == 7, pltpu.roll(down, 7, 0), 0.05 * (k + pltpu.roll(k, 7, 0)))
        kyd = jnp.where(sub == 0, pltpu.roll(up, 1, 0), pltpu.roll(ky, 1, 0))
        kz = 0.05 * (k + zt_down(k))
        kzd = 0.05 * (k + zt_up(k))
        kx_s[x, beyond] = kx
        ky_s[x, beyond] = ky
        kyd_s[x, beyond] = kyd
        kz_s[x, beyond] = kz
        kzd_s[x, beyond] = kzd
        c_s[x, beyond] = 1.0 - ((kx + kx_low) + (ky + kyd) + (kz + kzd))
        ky_s[x, BY - 8 : BY] = ky_s[x, BY - 8 : BY] + up
        kyd_s[x, 0:8] = kyd_s[x, 0:8] + down
        c_s[x, 0:8] = c_s[x, 0:8] - down
        c_s[x, BY - 8 : BY] = c_s[x, BY - 8 : BY] - up
        return k_next, kx

    lax.fori_loop(0, EX, halo_coefficients, (kh_s[0], jnp.zeros((8, NZ), f32)), unroll=4)
    z_up, z_down = z_shifts(EY)

    row = lax.broadcasted_iota(jnp.int32, (EY, NZ), 0)
    row_mask = jnp.where(row < BY, 1.0, jnp.where(row < BY + W, from_high_y, from_low_y))

    for step in range(STEPS):
        lo = step
        hi = EX - 1 - step

        def one_plane(x, carry, step=step):
            partial, up = carry
            u = u_s[x]
            w = 0.025 * u
            g0 = v0_s[x] * w
            g1 = v1_s[x] * w
            g2 = v2_s[x] * w
            done = partial + u * (kx_s[x - 1] - g0)
            prev = x - 1
            plane_mask = jnp.where(prev < W, from_low_x, jnp.where(prev >= BX + W, from_high_x, 1.0))
            u_s[prev] = done * (row_mask * plane_mask)
            up_next = u * (kx_s[x] + g0)
            total = u * c_s[x] + up
            total = total + pltpu.roll(u * (ky_s[x] + g1), 1, 0)
            total = total + pltpu.roll(u * (kyd_s[x] - g1), EY - 1, 0)
            total = total + z_up(u * (kz_s[x] + g2))
            total = total + z_down(u * (kzd_s[x] - g2))
            return total, up_next

        first_u = u_s[lo]
        first_up = first_u * (kx_s[lo] + v0_s[lo] * (0.025 * first_u))
        lax.fori_loop(lo + 1, hi + 1, one_plane, (jnp.zeros((EY, NZ), f32), first_up), unroll=4)

    for copy in copies:
        copy.wait()
    fit = (fit_ref[0], fit_ref[1])
    ytab = (ytab_s[0], ytab_s[1])

    def fit_planes(group, carry):
        at = pl.multiple_of(group * 8, 8)
        part = u_s[pl.ds(at + W, 8), 0:BY]
        adv_ref[pl.ds(at, 8)] = part
        rows = dot3(ytab, halves(part.reshape(8 * BY, NZ)))
        rows = dot3(halves(rows), fit)
        for r in range(YR):
            zt_ref[r, pl.ds(at, 8)] = rows[8 * r : 8 * r + 8]
        return carry

    lax.fori_loop(0, BX // 8, fit_planes, 0, unroll=2)

    send = halves(send_s[...])
    for r in range(0, YR, 2):
        lines = slice(r * MZ, (r + 2) * MZ)
        rows = dot3(send, halves(jnp.concatenate([zt_ref[r], zt_ref[r + 1]], axis=1)))
        lo_ref[:, lines] = rows[0:16]
        hi_ref[:, lines] = rows[16:32]
        lo2_ref[:, lines] = rows[0:16].astype(jnp.bfloat16)
        hi2_ref[:, lines] = rows[16:32].astype(jnp.bfloat16)
    base = base_s[...]
    full = base
    for j in range(7):
        full = full + base[:, 70 + j : 71 + j] * near_s[0, j : j + 1, :]
        full = full + base[:, 86 + j : 87 + j] * near_s[1, j : j + 1, :]
    full_ref[...] = full


def combine_body(zt_ref, lo_ref, hi_ref, lo2_ref, hi2_ref, full_ref, own_ref, carry_ref):
    f32 = jnp.float32
    q = lax.axis_index("py")
    full = halves(full_ref[...])
    carries = []
    for r in range(0, YR, 2):
        lines = slice(r * MZ, (r + 2) * MZ)
        rows = jnp.concatenate(
            [jnp.concatenate([zt_ref[r], zt_ref[r + 1]], axis=1), lo_ref[:, lines], hi_ref[:, lines]]
            + [ref[:, lines].astype(f32) for ref in (lo2_ref, hi2_ref)],
            axis=0,
        )
        out = dot3(full, halves(rows))
        for i in range(2):
            part = out[:, i * MZ : (i + 1) * MZ]
            if r + i < BY // 2:
                own_ref[r + i] = part
            else:
                carries.append(part)

    def coded(part):
        head = part[0].astype(jnp.bfloat16)
        rest = (part[0] - head.astype(f32)).astype(jnp.bfloat16)
        return jnp.concatenate([head, part[1].astype(jnp.bfloat16), part[2].astype(jnp.bfloat16), rest], axis=0)

    up = coded(carries[:3])
    down = coded(carries[3:])
    for t in range(carry_ref.shape[0]):

        @pl.when(t > q)
        def _():
            carry_ref[t] = up

        @pl.when(t <= q)
        def _():
            carry_ref[t] = down


def couple_body(own_ref, got_ref, couple_hbm, out_ref, couple_s, sem):
    f32 = jnp.float32
    q = lax.axis_index("py")
    copy = pltpu.make_async_copy(couple_hbm.at[q], couple_s, sem)
    copy.start()
    copy.wait()
    block = BX // 2
    for base in range(0, BY // 2, 8):

        def one(t, acc, base=base):
            for c in range(4):
                part = got_ref[t, c * block : (c + 1) * block].astype(f32)
                acc = tuple(a + couple_s[base + m, t * 4 + c] * part for m, a in enumerate(acc))
            return acc

        acc = lax.fori_loop(0, got_ref.shape[0], one, tuple(own_ref[base + m] for m in range(8)), unroll=2)
        for m in range(8):
            out_ref[:, base + m, :] = acc[m]


KEPT = 11


def in_hbm(a):
    return pltpu.with_memory_space_constraint(a, pltpu.HBM)


def own_coefficients(field, diffusivity, velocity, after):
    vmem = pl.BlockSpec(memory_space=pltpu.VMEM)
    f32 = jnp.float32
    return pl.pallas_call(
        own_body,
        out_shape=[pltpu.VMEM((EX, EY, NZ), f32)] * (KEPT - 1)
        + [pltpu.VMEM((EX, 16, NZ), f32), pltpu.VMEM((2, BY, NZ), f32)],
        in_specs=[pl.BlockSpec(memory_space=pltpu.HBM)] * 3 + [pl.BlockSpec(memory_space=pl.ANY)],
        out_specs=[vmem] * (KEPT + 1),
        scratch_shapes=[pltpu.VMEM(a.shape, a.dtype) for a in (field, diffusivity, velocity)]
        + [pltpu.SemaphoreType.DMA((3, BX // PACK))],
        compiler_params=pltpu.CompilerParams(vmem_limit_bytes=12 * 1024 * 1024),
        name="own_coefficients",
    )(*[in_hbm(a) for a in (field, diffusivity, velocity)], after)


def time_steps(counts, margin, halos, fit, tables, end, kept):
    vmem = pl.BlockSpec(memory_space=pltpu.VMEM)
    smem = pl.BlockSpec(memory_space=pltpu.SMEM)
    hbm = pl.BlockSpec(memory_space=pltpu.HBM)
    f32 = jnp.float32
    bf16 = jnp.bfloat16
    shapes = [((BX, BY, NZ), f32), ((YR, BX, MZ), f32)] + [((16, LINES), f32)] * 2 + [((16, LINES), bf16)] * 2
    shapes += [((BX // 2, 128), f32)]
    return pl.pallas_call(
        functools.partial(stencil_body, *counts),
        out_shape=[jax.ShapeDtypeStruct(s, t) for s, t in shapes] + [pltpu.VMEM(a.shape, f32) for a in kept],
        in_specs=[smem] + [vmem] * 7 + [hbm] * 4 + [vmem] * (1 + KEPT),
        out_specs=[vmem] * (7 + KEPT),
        input_output_aliases={13 + i: 7 + i for i in range(KEPT)},
        scratch_shapes=[
            pltpu.VMEM((EX, 8, NZ), f32),
            pltpu.VMEM((2 * W, BY, NZ), f32),
            pltpu.VMEM((BX // 2, 128), f32),
            pltpu.VMEM((BX // 2, BX), f32),
            pltpu.VMEM((2, 8, 128), f32),
            pltpu.VMEM((2, YR * 8, 8 * BY), bf16),
            pltpu.SemaphoreType.DMA((5,)),
        ],
        compiler_params=pltpu.CompilerParams(vmem_limit_bytes=STEP_VMEM * 1024 * 1024),
        name="time_steps",
    )(margin, *halos, fit, *[in_hbm(t) for t in tables], end, *kept)[:7]


def combine(count_y, rows):
    vmem = pl.BlockSpec(memory_space=pltpu.VMEM)
    return pl.pallas_call(
        combine_body,
        out_shape=[
            jax.ShapeDtypeStruct((BY // 2, BX // 2, MZ), jnp.float32),
            jax.ShapeDtypeStruct((count_y, 2 * BX, MZ), jnp.bfloat16),
        ],
        in_specs=[vmem] * 6,
        out_specs=[vmem] * 2,
        compiler_params=pltpu.CompilerParams(vmem_limit_bytes=12 * 1024 * 1024),
        name="combine",
    )(*rows)


def add_carries(own, got, couple):
    vmem = pl.BlockSpec(memory_space=pltpu.VMEM)
    return pl.pallas_call(
        couple_body,
        out_shape=jax.ShapeDtypeStruct((BX // 2, BY // 2, MZ), jnp.float32),
        in_specs=[vmem, vmem, pl.BlockSpec(memory_space=pltpu.HBM)],
        out_specs=vmem,
        scratch_shapes=[pltpu.SMEM(couple.shape[1:], jnp.float32), pltpu.SemaphoreType.DMA(())],
        compiler_params=pltpu.CompilerParams(vmem_limit_bytes=8 * 1024 * 1024),
        name="add_carries",
    )(own, got, in_hbm(couple))


def ring(n, d):
    return [(i, (i + d) % n) for i in range(n)]


def shift(a, axis, d):
    return lax.ppermute(a, axis, ring(lax.axis_size(axis), d))


def pack_body(margin_ref, f_hbm, k_hbm, v_hbm, ylo_ref, yhi_ref, xlo_ref, xhi_ref, f_ref, k_ref, v_ref, sems):
    f32 = jnp.float32
    bf16 = jnp.bfloat16
    t = BY - W
    copies = load((f_hbm, k_hbm, v_hbm), (f_ref, k_ref, v_ref), sems)

    def rest(u):
        return u - u.astype(bf16).astype(f32)

    def faces(g, carry):
        tails, heads = [], []
        for i in range(4):
            x = 4 * g + i
            u = f_ref[x]
            tails.append(u[t:])
            heads.append(u[:W])
            ur_t = rest(u[t - 4 :])
            ur_h = rest(u[:8])
            k, v0, v1, v2 = [r.astype(f32) for r in (k_ref[x], v_ref[0, x], v_ref[1, x], v_ref[2, x])]
            ylo_ref[g, i] = jnp.concatenate(
                [k[t:], ur_t[7:8], v0[t + 1 :], v1[t:], ur_t[6:7], v2[t + 1 :]], axis=0
            ).astype(bf16)
            yhi_ref[g, i] = jnp.concatenate(
                [k[:W], v0[: W - 1], ur_h[0:1], v1[:W], v2[: W - 1], ur_h[1:2]], axis=0
            ).astype(bf16)
        ylo_ref[g, 4] = jnp.concatenate(tails, axis=0).astype(bf16)
        yhi_ref[g, 4] = jnp.concatenate(heads, axis=0).astype(bf16)
        return carry

    def x_side(at, out, near, outer):
        for i in range(W):
            out[i] = f_ref[at + i].astype(bf16)
            out[W + i] = k_ref[at + i]
            out[2 * W + i] = v_ref[0, at + i]
            if i == outer:
                out[3 * W + i] = rest(f_ref[at + near[0]]).astype(bf16)
                out[4 * W + i] = rest(f_ref[at + near[1]]).astype(bf16)
            else:
                out[3 * W + i] = v_ref[1, at + i]
                out[4 * W + i] = v_ref[2, at + i]
        half = jnp.zeros((16, NZ), f32)
        out[5 * W] = jnp.concatenate([half + margin_ref[0, 0].astype(f32), half + margin_ref[0, 1].astype(f32)], axis=0).astype(bf16)

    for c in range(BX // PACK):
        for copy in copies[c]:
            copy.wait()
        lax.fori_loop(c * PACK // 4, (c + 1) * PACK // 4, faces, 0)
        if c == 0:
            x_side(0, xhi_ref, (0, 1), W - 1)
    x_side(BX - W, xlo_ref, (W - 1, W - 2), 0)


def corner_body(xl_ref, xh_ref, up_ref, down_ref):
    f32 = jnp.float32
    for side, ref in enumerate((xl_ref, xh_ref)):
        for n in range(5):
            planes = [ref[n * W + i].astype(f32) for i in range(W)]
            up_ref[side * 5 + n] = jnp.concatenate([a[BY - W :] for a in planes], axis=0).astype(jnp.bfloat16)
            down_ref[side * 5 + n] = jnp.concatenate([a[:W] for a in planes], axis=0).astype(jnp.bfloat16)


def halo_parts(field, diffusivity, velocity, margin):
    bf16 = jnp.bfloat16
    y_shape = (BX // 4, 5, 16, NZ)
    x_shape = (5 * W + 1, BY, NZ)
    c_shape = (10, 16, NZ)
    vmem = pl.BlockSpec(memory_space=pltpu.VMEM)
    hbm = pl.BlockSpec(memory_space=pltpu.HBM)
    ylo, yhi, xlo, xhi = pl.pallas_call(
        pack_body,
        out_shape=[jax.ShapeDtypeStruct(s, bf16) for s in [y_shape] * 2 + [x_shape] * 2],
        in_specs=[pl.BlockSpec(memory_space=pltpu.SMEM), hbm, hbm, hbm],
        out_specs=[vmem] * 4,
        scratch_shapes=[pltpu.VMEM(a.shape, a.dtype) for a in (field, diffusivity, velocity)]
        + [pltpu.SemaphoreType.DMA((3, BX // PACK))],
        compiler_params=pltpu.CompilerParams(vmem_limit_bytes=PACK_VMEM * 1024 * 1024),
        name="pack_faces",
    )(margin, *[in_hbm(a) for a in (field, diffusivity, velocity)])
    xl = shift(xlo, "px", 1)
    xh = shift(xhi, "px", -1)
    yl = shift(ylo, "py", 1)
    yh = shift(yhi, "py", -1)
    c_up, c_down = pl.pallas_call(
        corner_body,
        out_shape=[jax.ShapeDtypeStruct(c_shape, bf16)] * 2,
        in_specs=[vmem] * 2,
        out_specs=[vmem] * 2,
        compiler_params=pltpu.CompilerParams(vmem_limit_bytes=4 * 1024 * 1024),
        name="pack_corners",
    )(xl, xh)
    halos = (yl, yh, xl, xh, shift(c_up, "py", 1), shift(c_down, "py", -1))
    return halos, own_coefficients(field, diffusivity, velocity, ylo)


def per_device(field, diffusivity, velocity, margin):
    count_x = lax.axis_size("px")
    count_y = lax.axis_size("py")
    fit = jnp.asarray(np.stack(split(fit_matrix(NZ).T)))
    ytab, couple = y_tables(count_y)
    tables = [jnp.asarray(t) for t in x_tables(count_x) + [ytab]]
    halos, kept = halo_parts(field, diffusivity, velocity, margin)
    advected, zt, lo, hi, lo2, hi2, full = time_steps(
        (count_x, count_y), margin, halos, fit, tables, kept[KEPT], kept[:KEPT]
    )
    rows = (zt, shift(lo, "px", 1), shift(hi, "px", -1), shift(lo2, "px", 2), shift(hi2, "px", -2), full)
    own, carries = combine(count_y, rows)
    got = lax.all_to_all(carries, "py", split_axis=0, concat_axis=0, tiled=True)
    return advected, add_carries(own, got, jnp.asarray(couple))


def solution(mesh):
    placed = (P("px", "py", None), P("px", "py", None), P(None, "px", "py", None), P("px", None))
    return jax.shard_map(
        per_device,
        mesh=mesh,
        in_specs=placed,
        out_specs=(P("px", "py", None), P("px", "py", None)),
        check_vma=False,
    )
```

time: 93.5 us -> 83.2 us (0.89)
  blocking collectives: 0 us -> 13.3 us
  matrix products: 7.46 us -> 0 us
  starting transfers between devices: 27.3 us -> 21.3 us
  local copies, waits for them, and re-layouts: 5.04 us -> 0.66 us
  between operations: 4.69 us -> 0.74 us
  Pallas kernels: 33 us -> 36.8 us
  waiting for transfers between devices: 13.5 us -> 10.1 us
  other arithmetic: 1.85 us -> 0 us
    all_to_all x0 -> x1, blocking collectives: none -> 13.3 us  [per_device(): got = lax.all_to_all(carries, 'py', split_axis=0, concat_axis=0, tiled=True)]
    all_to_all x1 -> x0, waiting for transfers between devices: 9.59 us -> none  [per_device(): got = lax.all_to_all(carries, 'py', split_axis=0, concat_axis=0, tiled=True)]
    dot_general x6 -> x0, matrix products: 7.46 us -> none  [the longest x1 1.89 us: per_device(): xfit = jnp.einsum('kx,xyz->kyz', full, stacked, precision=HIGH)]
    all_to_all x1 -> x0, starting transfers between devices: 6.71 us -> none  [per_device(): got = lax.all_to_all(carries, 'py', split_axis=0, concat_axis=0, tiled=True)]
    ppermute x10, waiting for transfers between devices: 3.88 us -> 10.1 us  [shift(): return lax.ppermute(a, axis, ring(lax.axis_size(axis), d))]
    pallas_call x1 -> x4, Pallas kernels: 27.8 us -> 33.1 us  [the longest x1 24.2 us: time_steps(): pl.pallas_call(functools.partial(stencil_body, *counts), out_shape=[jax.S...]
    squeeze x3 -> x0, local copies, waits for them, and re-layouts: 2.74 us -> none  [the longest x2 1.44 us: table_row(): lax.dynamic_index_in_dim(jnp.asarray(table), (cls * n + m[0]) * n + m[1],...]
    slice x9 -> x0, local copies, waits for them, and re-layouts: 1.9 us -> none  [the longest x3 1.75 us: table_row(): m[1]]
  transfers between devices with their start and end apart: 11 -> 10, of which waited for: 4 -> 3; matrix products, arithmetic and copies ran while one was open for 9% -> 0% of each run, Pallas kernels for 0% -> 6%
where the time goes in v3:
time: 83.2 us; the launch traced here: 82.9 us
  Pallas kernels  36.8 us (44%)
  starting transfers between devices  21.3 us (26%)
  blocking collectives  13.3 us (16%)
  waiting for transfers between devices  10.1 us (12%)
    pallas_call x1, Pallas kernels, time_steps(): pl.pallas_call(functools.partial(stencil_body, *counts), out_shape=[jax.S...  24.2 us
    ppermute x10, starting transfers between devices, shift(): return lax.ppermute(a, axis, ring(lax.axis_size(axis), d))  21.3 us
    all_to_all x1, blocking collectives, per_device(): got = lax.all_to_all(carries, 'py', split_axis=0, concat_axis=0, tiled=True)  13.3 us
    ppermute x10, waiting for transfers between devices, shift(): return lax.ppermute(a, axis, ring(lax.axis_size(axis), d))  10.1 us
    pallas_call x1, Pallas kernels, own_coefficients(): pl.pallas_call(own_body, out_shape=[pltpu.VMEM((EX, EY, NZ), f32)] * (KEP...  5.15 us
    pallas_call x1, Pallas kernels, halo_parts(): pl.pallas_call(pack_body, out_shape=[jax.ShapeDtypeStruct(s, bf16) for s...  3.61 us
    pallas_call x1, Pallas kernels, add_carries(): pl.pallas_call(couple_body, out_shape=jax.ShapeDtypeStruct((BX // 2, BY /...  3.15 us
  transfers between devices with their start and end apart: 10, of which 3 were waited for; matrix products, arithmetic and copies ran while one was open for 0% of the time, Pallas kernels for 6%

profile of v3, /device:TPU:0, one launch (start us, length us, event | category | flops | bytes accessed | tf_op | source)
XLA Modules:
  0.0 82.9 jit_solution(13124774832048689477)
XLA Ops:
  0.6 0.0 copy-start.1
  0.6 0.6 copy-done.1
  1.3 3.6 %pack_faces.1 = (bf16[16,5,16,256]{3,2,1,0:T(8,128)(2,1)S(1)}, bf16[16,5,16,256]{3,2,1,0:T(8,128)(2,1)S(1)}, bf16[21,32,256]{2,1,0:T(8,128)(2,1)S(1)}, bf16[21,32,256]{2,1,0:T(8,128)(2,1)S(1)}) custom-call(s32[1,2]{1,0:T(1,128)S(1)} %copy-done.1, f32[64,32,256]{2,1,0:T(8,128)} %f_hbm.3, bf16[64,32,256]{2,1,0:T(8,128)(2,1)} %k_hbm.3, ...), custom_call_target="tpu_custom_call" | custom-call | tf_op jit(solution)/shard_map/pack_faces/pallas_call | solution.py:609
  4.9 6.6 %collective-permute-start.1 = (bf16[16,5,16,256]{3,2,1,0:T(8,128)(2,1)S(1)}, bf16[16,5,16,256]{3,2,1,0:T(8,128)(2,1)S(1)}, u32[]{:S(2)}, u32[]{:S(2)}) collective-permute-start(bf16[16,5,16,256]{3,2,1,0:T(8,128)(2,1)S(1)} %get-tuple-element.30), channel_id=1, source_target_pairs={{0,15},{1,0},{2,1},{3,2},{4,3},{5,4},{6,5},{7,6},{8,7},{9,8},{10,9... | collective-permute-start | bytes 1966088 | tf_op jit(solution)/shard_map/ppermute | solution.py:538
  11.5 0.0 collective-permute-start
  11.6 3.0 %collective-permute-start.3 = (bf16[21,32,256]{2,1,0:T(8,128)(2,1)S(1)}, bf16[21,32,256]{2,1,0:T(8,128)(2,1)S(1)}, u32[]{:S(2)}, u32[]{:S(2)}) collective-permute-start(bf16[21,32,256]{2,1,0:T(8,128)(2,1)S(1)} %get-tuple-element.32), channel_id=1, source_target_pairs={{0,112},{16,0},{32,16},{48,32},{64,48},{80,64},{96,80},{112,96},{1... | collective-permute-start | bytes 1032200 | tf_op jit(solution)/shard_map/ppermute | solution.py:538
  14.5 4.9 %collective-permute-done.2.xl_ref = bf16[21,32,256]{2,1,0:T(8,128)(2,1)S(1)} collective-permute-done((bf16[21,32,256]{2,1,0:T(8,128)(2,1)S(1)}, bf16[21,32,256]{2,1,0:T(8,128)(2,1)S(1)}, u32[]{:S(2)}, u32[]{:S(2)}) %collective-permute-start.2) | collective-permute-done | bytes 344096 | tf_op jit(solution)/shard_map/ppermute | solution.py:538
  19.4 0.1 pack_corners.1
  19.5 0.1 collective-permute-start.4
  19.6 0.0 copy-start
  19.6 0.0 copy-start.2
  19.6 5.4 %collective-permute-start.5 = (bf16[10,16,256]{2,1,0:T(8,128)(2,1)S(1)}, bf16[10,16,256]{2,1,0:T(8,128)(2,1)S(1)}, u32[]{:S(2)}, u32[]{:S(2)}) collective-permute-start(bf16[10,16,256]{2,1,0:T(8,128)(2,1)S(1)} %get-tuple-element.34), channel_id=1, source_target_pairs={{0,15},{1,0},{2,1},{3,2},{4,3},{5,4},{6,5},{7,6},{8,7},{9,8},{10,9... | collective-permute-start | bytes 245768 | tf_op jit(solution)/shard_map/ppermute | solution.py:538
  25.0 5.2 %own_coefficients.1 = (f32[72,40,256]{2,1,0:T(8,128)S(1)}, f32[72,40,256]{2,1,0:T(8,128)S(1)}, f32[72,40,256]{2,1,0:T(8,128)S(1)}, f32[72,40,256]{2,1,0:T(8,128)...) custom-call(f32[64,32,256]{2,1,0:T(8,128)} %f_hbm.3, ...), custom_call_target="tpu_custom_call" | custom-call | tf_op jit(solution)/shard_map/own_coefficients/pallas_call | solution.py:464
  30.2 2.6 %collective-permute-done.4.cl_ref = bf16[10,16,256]{2,1,0:T(8,128)(2,1)S(1)} collective-permute-done((bf16[10,16,256]{2,1,0:T(8,128)(2,1)S(1)}, bf16[10,16,256]{2,1,0:T(8,128)(2,1)S(1)}, u32[]{:S(2)}, u32[]{:S(2)}) %collective-permute-start.4) | collective-permute-done | bytes 81952 | tf_op jit(solution)/shard_map/ppermute | solution.py:538
  32.8 0.0 collective-permute-done.5.ch_ref
  32.8 24.2 %time_steps.1 = (f32[64,32,256]{2,1,0:T(8,128)}, f32[22,64,128]{2,1,0:T(8,128)S(1)}, f32[16,2816]{1,0:T(8,128)S(1)}, f32[16,2816]{1,0:T(8,128)S(1)}, bf16[16,281...) custom-call(s32[1,2]{1,0:T(1,128)S(1)} %copy-done.2, ...), custom_call_target="tpu_custom_call", output_to_operand_aliasing={{7}: (13, {}), {8}: (14, {}), {9}: (15, {}), {10}: (16, {})... | custom-call | tf_op jit(solution)/shard_map/time_steps/pallas_call | solution.py:485
  57.1 0.0 collective-permute-start.6
  57.1 2.9 %collective-permute-start.7 = (f32[16,2816]{1,0:T(8,128)S(1)}, f32[16,2816]{1,0:T(8,128)S(1)}, u32[]{:S(2)}, u32[]{:S(2)}) collective-permute-start(f32[16,2816]{1,0:T(8,128)S(1)} %get-tuple-element.50), channel_id=1, source_target_pairs={{0,112},{16,0},{32,16},{48,32},{64,48},{80,64},{96,80},{112,96},{1... | collective-permute-start | bytes 540680 | tf_op jit(solution)/shard_map/ppermute | solution.py:538
  60.1 0.3 collective-permute-start.8
  60.3 3.0 %collective-permute-start.9 = (bf16[16,2816]{1,0:T(8,128)(2,1)S(1)}, bf16[16,2816]{1,0:T(8,128)(2,1)S(1)}, u32[]{:S(2)}, u32[]{:S(2)}) collective-permute-start(bf16[16,2816]{1,0:T(8,128)(2,1)S(1)} %get-tuple-element.52), channel_id=1, source_target_pairs={{0,96},{16,112},{32,0},{48,16},{64,32},{80,48},{96,64},{112,80},{1... | collective-permute-start | bytes 270344 | tf_op jit(solution)/shard_map/ppermute | solution.py:538
  63.3 2.5 %collective-permute-done.8.lo2_ref = bf16[16,2816]{1,0:T(8,128)(2,1)S(1)} collective-permute-done((bf16[16,2816]{1,0:T(8,128)(2,1)S(1)}, bf16[16,2816]{1,0:T(8,128)(2,1)S(1)}, u32[]{:S(2)}, u32[]{:S(2)}) %collective-permute-start.8) | collective-permute-done | bytes 90144 | tf_op jit(solution)/shard_map/ppermute | solution.py:538
  65.8 0.6 combine.1
  66.4 13.3 %all_to_all.5.got_ref = bf16[16,128,128]{2,1,0:T(8,128)(2,1)S(1)} all-to-all(bf16[16,128,128]{2,1,0:T(8,128)(2,1)S(1)} %get-tuple-element.55), channel_id=1, replica_groups=mesh['px'=8,'py'=16] {'py'}, dimensions={0} | all-to-all | bytes 1048576 | tf_op jit(solution)/shard_map/all_to_all | solution.py:647
  79.7 3.1 %add_carries.1 = f32[32,16,128]{2,1,0:T(8,128)} custom-call(f32[16,32,128]{2,1,0:T(8,128)S(1)} %get-tuple-element.54.own_ref, bf16[16,128,128]{2,1,0:T(8,128)(2,1)S(1)} %all_to_all.5.got_ref, f32[16,16,64]{2,1,0:T(8,128)} %constant.17.clone.couple_hbm), custom_call_target="tpu_custom_call" | custom-call | tf_op jit(solution)/shard_map/add_carries/pallas_call | solution.py:522
  (9 shorter events, 0.0 us)
Async XLA Ops:
  0.6 0.7 copy-start.1
  4.9 27.9 %collective-permute-start.1 = (bf16[16,5,16,256]{3,2,1,0:T(8,128)(2,1)S(1)}, bf16[16,5,16,256]{3,2,1,0:T(8,128)(2,1)S(1)}, u32[]{:S(2)}, u32[]{:S(2)}) collective-permute-start(bf16[16,5,16,256]{3,2,1,0:T(8,128)(2,1)S(1)} %get-tuple-element.30), channel_id=1, source_target_pairs={{0,15},{1,0},{2,1},{3,2},{4,3},{5,4},{6,5},{7,6},{8,7},{9,8},{10,9... | collective-permute-start | bytes 1966088 | tf_op jit(solution)/shard_map/ppermute | solution.py:538
  11.5 21.3 %collective-permute-start = (bf16[16,5,16,256]{3,2,1,0:T(8,128)(2,1)S(1)}, bf16[16,5,16,256]{3,2,1,0:T(8,128)(2,1)S(1)}, u32[]{:S(2)}, u32[]{:S(2)}) collective-permute-start(bf16[16,5,16,256]{3,2,1,0:T(8,128)(2,1)S(1)} %get-tuple-element.29.after_ref), channel_id=1, source_target_pairs={{0,1},{1,2},{2,3},{3,4},{4,5},{5,6},{6,7},{7,8},{8,9},{9,10},{10,1... | collective-permute-start | bytes 1966088 | tf_op jit(solution)/shard_map/ppermute | solution.py:538
  11.6 7.9 %collective-permute-start.2 = (bf16[21,32,256]{2,1,0:T(8,128)(2,1)S(1)}, bf16[21,32,256]{2,1,0:T(8,128)(2,1)S(1)}, u32[]{:S(2)}, u32[]{:S(2)}) collective-permute-start(bf16[21,32,256]{2,1,0:T(8,128)(2,1)S(1)} %get-tuple-element.31), channel_id=1, source_target_pairs={{0,16},{16,32},{32,48},{48,64},{64,80},{80,96},{96,112},{112,0},{1... | collective-permute-start | bytes 1032200 | tf_op jit(solution)/shard_map/ppermute | solution.py:538
  11.6 7.9 %collective-permute-start.3 = (bf16[21,32,256]{2,1,0:T(8,128)(2,1)S(1)}, bf16[21,32,256]{2,1,0:T(8,128)(2,1)S(1)}, u32[]{:S(2)}, u32[]{:S(2)}) collective-permute-start(bf16[21,32,256]{2,1,0:T(8,128)(2,1)S(1)} %get-tuple-element.32), channel_id=1, source_target_pairs={{0,112},{16,0},{32,16},{48,32},{64,48},{80,64},{96,80},{112,96},{1... | collective-permute-start | bytes 1032200 | tf_op jit(solution)/shard_map/ppermute | solution.py:538
  19.5 13.3 %collective-permute-start.4 = (bf16[10,16,256]{2,1,0:T(8,128)(2,1)S(1)}, bf16[10,16,256]{2,1,0:T(8,128)(2,1)S(1)}, u32[]{:S(2)}, u32[]{:S(2)}) collective-permute-start(bf16[10,16,256]{2,1,0:T(8,128)(2,1)S(1)} %get-tuple-element.33), channel_id=1, source_target_pairs={{0,1},{1,2},{2,3},{3,4},{4,5},{5,6},{6,7},{7,8},{8,9},{9,10},{10,1... | collective-permute-start | bytes 245768 | tf_op jit(solution)/shard_map/ppermute | solution.py:538
  19.6 13.3 %copy-start = (bf16[2,256,128]{2,1,0:T(8,128)(2,1)S(1)}, bf16[2,256,128]{2,1,0:T(8,128)(2,1)}, u32[]{:S(2)}) copy-start(bf16[2,256,128]{2,1,0:T(8,128)(2,1)} %constant.12.clone.fit_ref) | copy-start | bytes 393220
  19.6 13.2 %copy-start.2 = (s32[1,2]{1,0:T(1,128)S(1)}, s32[1,2]{1,0:T(1,128)}, u32[]{:S(2)}) copy-start(s32[1,2]{1,0:T(1,128)} %margin_ref.3) | copy-start | bytes 28
  19.6 13.2 %collective-permute-start.5 = (bf16[10,16,256]{2,1,0:T(8,128)(2,1)S(1)}, bf16[10,16,256]{2,1,0:T(8,128)(2,1)S(1)}, u32[]{:S(2)}, u32[]{:S(2)}) collective-permute-start(bf16[10,16,256]{2,1,0:T(8,128)(2,1)S(1)} %get-tuple-element.34), channel_id=1, source_target_pairs={{0,15},{1,0},{2,1},{3,2},{4,3},{5,4},{6,5},{7,6},{8,7},{9,8},{10,9... | collective-permute-start | bytes 245768 | tf_op jit(solution)/shard_map/ppermute | solution.py:538
  57.1 8.7 %collective-permute-start.6 = (f32[16,2816]{1,0:T(8,128)S(1)}, f32[16,2816]{1,0:T(8,128)S(1)}, u32[]{:S(2)}, u32[]{:S(2)}) collective-permute-start(f32[16,2816]{1,0:T(8,128)S(1)} %get-tuple-element.49), channel_id=1, source_target_pairs={{0,16},{16,32},{32,48},{48,64},{64,80},{80,96},{96,112},{112,0},{1... | collective-permute-start | bytes 540680 | tf_op jit(solution)/shard_map/ppermute | solution.py:538
  57.1 8.7 %collective-permute-start.7 = (f32[16,2816]{1,0:T(8,128)S(1)}, f32[16,2816]{1,0:T(8,128)S(1)}, u32[]{:S(2)}, u32[]{:S(2)}) collective-permute-start(f32[16,2816]{1,0:T(8,128)S(1)} %get-tuple-element.50), channel_id=1, source_target_pairs={{0,112},{16,0},{32,16},{48,32},{64,48},{80,64},{96,80},{112,96},{1... | collective-permute-start | bytes 540680 | tf_op jit(solution)/shard_map/ppermute | solution.py:538
  60.1 5.7 %collective-permute-start.8 = (bf16[16,2816]{1,0:T(8,128)(2,1)S(1)}, bf16[16,2816]{1,0:T(8,128)(2,1)S(1)}, u32[]{:S(2)}, u32[]{:S(2)}) collective-permute-start(bf16[16,2816]{1,0:T(8,128)(2,1)S(1)} %get-tuple-element.51), channel_id=1, source_target_pairs={{0,32},{16,48},{32,64},{48,80},{64,96},{80,112},{96,0},{112,16},{1... | collective-permute-start | bytes 270344 | tf_op jit(solution)/shard_map/ppermute | solution.py:538
  60.3 5.5 %collective-permute-start.9 = (bf16[16,2816]{1,0:T(8,128)(2,1)S(1)}, bf16[16,2816]{1,0:T(8,128)(2,1)S(1)}, u32[]{:S(2)}, u32[]{:S(2)}) collective-permute-start(bf16[16,2816]{1,0:T(8,128)(2,1)S(1)} %get-tuple-element.52), channel_id=1, source_target_pairs={{0,96},{16,112},{32,0},{48,16},{64,32},{80,48},{96,64},{112,80},{1... | collective-permute-start | bytes 270344 | tf_op jit(solution)/shard_map/ppermute | solution.py:538

commit v4 on v3

--- a/solution.py
+++ b/solution.py
@@ -70,7 +70,8 @@
                 couple[t, :, q, :3] = left[i]
                 couple[t, :, q, 3] = left[i, :, 0]
     table = np.einsum("qry,xw->qrxwy", rows, np.eye(8)).reshape(count, YR * 8, 8 * BY)
-    return np.stack(split(table), axis=1), couple.reshape(count, own, count * 4).astype(np.float32)
+    spaced = np.einsum("qmtc,xw->qxmtwc", couple, np.eye(8)).reshape(count, own * 8, count * 32)
+    return np.stack(split(table), axis=1), np.stack(split(spaced), axis=1)
 
 
 def x_tables(count):
@@ -211,12 +212,13 @@
 
 
 def stencil_body(count_x, count_y, margin_ref, yl_ref, yh_ref, xl_ref, xh_ref, cl_ref, ch_ref, fit_ref, base_hbm, send_hbm,
-                 near_hbm, ytab_hbm, end_ref, *rest_refs):
+                 near_hbm, ytab_hbm, couple_hbm, end_ref,
+                 *rest_refs):
     f32 = jnp.float32
     outs = rest_refs[KEPT:]
-    adv_ref, zt_ref, lo_ref, hi_ref, lo2_ref, hi2_ref, full_ref = outs[:7]
-    u_s, v0_s, v1_s, v2_s, kx_s, ky_s, kyd_s, kz_s, kzd_s, c_s, edge_s = outs[7 : 7 + KEPT]
-    kh_s, kp_s, base_s, send_s, near_s, ytab_s, sems = outs[7 + KEPT :]
+    adv_hbm, zt_ref, lo_ref, hi_ref, lo2_ref, hi2_ref, full_ref, couple_ref = outs[:8]
+    u_s, v0_s, v1_s, v2_s, kx_s, ky_s, kyd_s, kz_s, kzd_s, c_s, edge_s = outs[8 : 8 + KEPT]
+    kh_s, kp_s, base_s, send_s, near_s, ytab_s, sems = outs[8 + KEPT :]
     p = lax.axis_index("px")
     q = lax.axis_index("py")
 
@@ -233,6 +235,7 @@
         pltpu.make_async_copy(near_hbm.at[low, 0], near_s.at[0], sems.at[2]),
         pltpu.make_async_copy(near_hbm.at[high, 1], near_s.at[1], sems.at[3]),
         pltpu.make_async_copy(ytab_hbm.at[q], ytab_s, sems.at[4]),
+        pltpu.make_async_copy(couple_hbm.at[q], couple_ref, sems.at[5]),
     ]
     for copy in copies:
         copy.start()
@@ -360,6 +363,8 @@
         first_up = first_u * (kx_s[lo] + v0_s[lo] * (0.025 * first_u))
         lax.fori_loop(lo + 1, hi + 1, one_plane, (jnp.zeros((EY, NZ), f32), first_up), unroll=4)
 
+    result = pltpu.make_async_copy(u_s.at[pl.ds(W, BX), pl.ds(0, BY)], adv_hbm, sems.at[6])
+    result.start()
     for copy in copies:
         copy.wait()
     fit = (fit_ref[0], fit_ref[1])
@@ -368,7 +373,6 @@
     def fit_planes(group, carry):
         at = pl.multiple_of(group * 8, 8)
         part = u_s[pl.ds(at + W, 8), 0:BY]
-        adv_ref[pl.ds(at, 8)] = part
         rows = dot3(ytab, halves(part.reshape(8 * BY, NZ)))
         rows = dot3(halves(rows), fit)
         for r in range(YR):
@@ -391,64 +395,70 @@
         full = full + base[:, 70 + j : 71 + j] * near_s[0, j : j + 1, :]
         full = full + base[:, 86 + j : 87 + j] * near_s[1, j : j + 1, :]
     full_ref[...] = full
+    result.wait()
 
 
 def combine_body(zt_ref, lo_ref, hi_ref, lo2_ref, hi2_ref, full_ref, own_ref, carry_ref):
     f32 = jnp.float32
     q = lax.axis_index("py")
     full = halves(full_ref[...])
-    carries = []
-    for r in range(0, YR, 2):
-        lines = slice(r * MZ, (r + 2) * MZ)
-        rows = jnp.concatenate(
-            [jnp.concatenate([zt_ref[r], zt_ref[r + 1]], axis=1), lo_ref[:, lines], hi_ref[:, lines]]
+
+    def stack(first, last):
+        lines = slice(first * MZ, last * MZ)
+        return jnp.concatenate(
+            [jnp.concatenate([zt_ref[r] for r in range(first, last)], axis=1), lo_ref[:, lines], hi_ref[:, lines]]
             + [ref[:, lines].astype(f32) for ref in (lo2_ref, hi2_ref)],
             axis=0,
         )
-        out = dot3(full, halves(rows))
+
+    own = BY // 2
+    for r in range(0, own, 2):
+        out = dot3(full, halves(stack(r, r + 2)))
         for i in range(2):
-            part = out[:, i * MZ : (i + 1) * MZ]
-            if r + i < BY // 2:
-                own_ref[r + i] = part
-            else:
-                carries.append(part)
-
-    def coded(part):
-        head = part[0].astype(jnp.bfloat16)
-        rest = (part[0] - head.astype(f32)).astype(jnp.bfloat16)
-        return jnp.concatenate([head, part[1].astype(jnp.bfloat16), part[2].astype(jnp.bfloat16), rest], axis=0)
-
-    up = coded(carries[:3])
-    down = coded(carries[3:])
+            own_ref[:, r + i, :] = out[:, i * MZ : (i + 1) * MZ]
+
+    block = BX // 2
+    part = lax.broadcasted_iota(jnp.int32, (4 * block, 128), 0) % 4
+    spread = lax.broadcasted_iota(jnp.int32, (4 * block, block), 0) // 4
+    spread = jnp.where(spread == lax.broadcasted_iota(jnp.int32, (4 * block, block), 1), 1.0, 0.0).astype(jnp.bfloat16)
+    spaced = []
+    for f in full:
+        rows = jnp.dot(spread, f, preferred_element_type=f32)
+        spaced.append(
+            jnp.concatenate(
+                [jnp.where(part % 3 == 0, rows, 0.0), jnp.where(part == 1, rows, 0.0), jnp.where(part == 2, rows, 0.0)],
+                axis=1,
+            ).astype(jnp.bfloat16)
+        )
+    carries = stack(own, YR)
+    carries = jnp.concatenate(
+        [jnp.concatenate([carries[:, n * MZ : (n + 1) * MZ], carries[:, (n + 3) * MZ : (n + 4) * MZ]], axis=1) for n in range(3)],
+        axis=0,
+    )
+    carries = dot3(spaced, halves(carries))
+    coded = []
+    for n in range(2):
+        value = carries[:, n * MZ : (n + 1) * MZ]
+        head = value.astype(jnp.bfloat16).astype(f32)
+        coded.append(jnp.where(part == 3, value - head, value).astype(jnp.bfloat16))
     for t in range(carry_ref.shape[0]):
 
         @pl.when(t > q)
         def _():
-            carry_ref[t] = up
+            carry_ref[t] = coded[0]
 
         @pl.when(t <= q)
         def _():
-            carry_ref[t] = down
-
-
-def couple_body(own_ref, got_ref, couple_hbm, out_ref, couple_s, sem):
-    f32 = jnp.float32
-    q = lax.axis_index("py")
-    copy = pltpu.make_async_copy(couple_hbm.at[q], couple_s, sem)
-    copy.start()
-    copy.wait()
-    block = BX // 2
-    for base in range(0, BY // 2, 8):
-
-        def one(t, acc, base=base):
-            for c in range(4):
-                part = got_ref[t, c * block : (c + 1) * block].astype(f32)
-                acc = tuple(a + couple_s[base + m, t * 4 + c] * part for m, a in enumerate(acc))
-            return acc
-
-        acc = lax.fori_loop(0, got_ref.shape[0], one, tuple(own_ref[base + m] for m in range(8)), unroll=2)
-        for m in range(8):
-            out_ref[:, base + m, :] = acc[m]
+            carry_ref[t] = coded[1]
+
+
+def couple_body(own_ref, got_ref, couple_ref, out_ref):
+    dot = functools.partial(jnp.dot, preferred_element_type=jnp.float32)
+    head = couple_ref[0]
+    rest = couple_ref[1]
+    for x in range(0, BX // 2, 8):
+        got = got_ref[:, 4 * x : 4 * x + 32].reshape(-1, MZ)
+        out_ref[x : x + 8] = own_ref[x : x + 8] + (dot(head, got) + dot(rest, got)).reshape(8, BY // 2, MZ)
 
 
 KEPT = 11
@@ -484,10 +494,12 @@
     shapes += [((BX // 2, 128), f32)]
     return pl.pallas_call(
         functools.partial(stencil_body, *counts),
-        out_shape=[jax.ShapeDtypeStruct(s, t) for s, t in shapes] + [pltpu.VMEM(a.shape, f32) for a in kept],
-        in_specs=[smem] + [vmem] * 7 + [hbm] * 4 + [vmem] * (1 + KEPT),
-        out_specs=[vmem] * (7 + KEPT),
-        input_output_aliases={13 + i: 7 + i for i in range(KEPT)},
+        out_shape=[jax.ShapeDtypeStruct(s, t) for s, t in shapes]
+        + [pltpu.VMEM(tables[-1].shape[1:], bf16)]
+        + [pltpu.VMEM(a.shape, f32) for a in kept],
+        in_specs=[smem] + [vmem] * 7 + [hbm] * 5 + [vmem] * (1 + KEPT),
+        out_specs=[hbm] + [vmem] * (7 + KEPT),
+        input_output_aliases={14 + i: 8 + i for i in range(KEPT)},
         scratch_shapes=[
             pltpu.VMEM((EX, 8, NZ), f32),
             pltpu.VMEM((2 * W, BY, NZ), f32),
@@ -495,11 +507,11 @@
             pltpu.VMEM((BX // 2, BX), f32),
             pltpu.VMEM((2, 8, 128), f32),
             pltpu.VMEM((2, YR * 8, 8 * BY), bf16),
-            pltpu.SemaphoreType.DMA((5,)),
+            pltpu.SemaphoreType.DMA((7,)),
         ],
         compiler_params=pltpu.CompilerParams(vmem_limit_bytes=STEP_VMEM * 1024 * 1024),
         name="time_steps",
-    )(margin, *halos, fit, *[in_hbm(t) for t in tables], end, *kept)[:7]
+    )(margin, *halos, fit, *[in_hbm(t) for t in tables], end, *kept)[:8]
 
 
 def combine(count_y, rows):
@@ -507,7 +519,7 @@
     return pl.pallas_call(
         combine_body,
         out_shape=[
-            jax.ShapeDtypeStruct((BY // 2, BX // 2, MZ), jnp.float32),
+            jax.ShapeDtypeStruct((BX // 2, BY // 2, MZ), jnp.float32),
             jax.ShapeDtypeStruct((count_y, 2 * BX, MZ), jnp.bfloat16),
         ],
         in_specs=[vmem] * 6,
@@ -522,12 +534,11 @@
     return pl.pallas_call(
         couple_body,
         out_shape=jax.ShapeDtypeStruct((BX // 2, BY // 2, MZ), jnp.float32),
-        in_specs=[vmem, vmem, pl.BlockSpec(memory_space=pltpu.HBM)],
+        in_specs=[vmem] * 3,
         out_specs=vmem,
-        scratch_shapes=[pltpu.SMEM(couple.shape[1:], jnp.float32), pltpu.SemaphoreType.DMA(())],
         compiler_params=pltpu.CompilerParams(vmem_limit_bytes=8 * 1024 * 1024),
         name="add_carries",
-    )(own, got, in_hbm(couple))
+    )(own, got, couple)
 
 
 def ring(n, d):
@@ -538,10 +549,13 @@
     return lax.ppermute(a, axis, ring(lax.axis_size(axis), d))
 
 
-def pack_body(margin_ref, f_hbm, k_hbm, v_hbm, ylo_ref, yhi_ref, xlo_ref, xhi_ref, f_ref, k_ref, v_ref, sems):
+def pack_body(margin_hbm, f_hbm, k_hbm, v_hbm, ylo_ref, yhi_ref, xlo_ref, xhi_ref, f_ref, k_ref, v_ref, margin_ref, sems,
+              margin_sem):
     f32 = jnp.float32
     bf16 = jnp.bfloat16
     t = BY - W
+    margin_copy = pltpu.make_async_copy(margin_hbm, margin_ref, margin_sem)
+    margin_copy.start()
     copies = load((f_hbm, k_hbm, v_hbm), (f_ref, k_ref, v_ref), sems)
 
     def rest(u):
@@ -581,6 +595,7 @@
         half = jnp.zeros((16, NZ), f32)
         out[5 * W] = jnp.concatenate([half + margin_ref[0, 0].astype(f32), half + margin_ref[0, 1].astype(f32)], axis=0).astype(bf16)
 
+    margin_copy.wait()
     for c in range(BX // PACK):
         for copy in copies[c]:
             copy.wait()
@@ -609,17 +624,19 @@
     ylo, yhi, xlo, xhi = pl.pallas_call(
         pack_body,
         out_shape=[jax.ShapeDtypeStruct(s, bf16) for s in [y_shape] * 2 + [x_shape] * 2],
-        in_specs=[pl.BlockSpec(memory_space=pltpu.SMEM), hbm, hbm, hbm],
+        in_specs=[hbm] * 4,
         out_specs=[vmem] * 4,
         scratch_shapes=[pltpu.VMEM(a.shape, a.dtype) for a in (field, diffusivity, velocity)]
-        + [pltpu.SemaphoreType.DMA((3, BX // PACK))],
+        + [pltpu.SMEM(margin.shape, jnp.int32), pltpu.SemaphoreType.DMA((3, BX // PACK)), pltpu.SemaphoreType.DMA(())],
         compiler_params=pltpu.CompilerParams(vmem_limit_bytes=PACK_VMEM * 1024 * 1024),
         name="pack_faces",
-    )(margin, *[in_hbm(a) for a in (field, diffusivity, velocity)])
+    )(*[in_hbm(a) for a in (margin, field, diffusivity, velocity)])
     xl = shift(xlo, "px", 1)
     xh = shift(xhi, "px", -1)
     yl = shift(ylo, "py", 1)
     yh = shift(yhi, "py", -1)
+    kept = own_coefficients(field, diffusivity, velocity, ylo)
+    xl, xh, kept = lax.optimization_barrier((xl, xh, kept))
     c_up, c_down = pl.pallas_call(
         corner_body,
         out_shape=[jax.ShapeDtypeStruct(c_shape, bf16)] * 2,
@@ -629,7 +646,7 @@
         name="pack_corners",
     )(xl, xh)
     halos = (yl, yh, xl, xh, shift(c_up, "py", 1), shift(c_down, "py", -1))
-    return halos, own_coefficients(field, diffusivity, velocity, ylo)
+    return halos, kept
 
 
 def per_device(field, diffusivity, velocity, margin):
@@ -637,15 +654,15 @@
     count_y = lax.axis_size("py")
     fit = jnp.asarray(np.stack(split(fit_matrix(NZ).T)))
     ytab, couple = y_tables(count_y)
-    tables = [jnp.asarray(t) for t in x_tables(count_x) + [ytab]]
+    tables = [jnp.asarray(t) for t in x_tables(count_x) + [ytab, couple]]
     halos, kept = halo_parts(field, diffusivity, velocity, margin)
-    advected, zt, lo, hi, lo2, hi2, full = time_steps(
+    advected, zt, lo, hi, lo2, hi2, full, couple = time_steps(
         (count_x, count_y), margin, halos, fit, tables, kept[KEPT], kept[:KEPT]
     )
     rows = (zt, shift(lo, "px", 1), shift(hi, "px", -1), shift(lo2, "px", 2), shift(hi2, "px", -2), full)
     own, carries = combine(count_y, rows)
     got = lax.all_to_all(carries, "py", split_axis=0, concat_axis=0, tiled=True)
-    return advected, add_carries(own, got, jnp.asarray(couple))
+    return advected, add_carries(own, got, couple)
 
 
 def solution(mesh):

time: 83.2 us -> 79.7 us (0.958)
  Pallas kernels: 36.8 us -> 34 us
    pallas_call x1, Pallas kernels: 3.15 us -> 1.13 us  [add_carries(): pl.pallas_call(couple_body, out_shape=jax.ShapeDtypeStruct((BX // 2, BY /...]
  transfers between devices with their start and end apart: 10 -> 10, of which waited for: 3 -> 2; matrix products, arithmetic and copies ran while one was open for 0% -> 0% of each run, Pallas kernels for 6% -> 7%
where the time goes in v4:
time: 79.7 us; the launch traced here: 79.4 us
  Pallas kernels  34 us (43%)
  starting transfers between devices  21.3 us (27%)
  blocking collectives  13.3 us (17%)
  waiting for transfers between devices  10.1 us (13%)
    pallas_call x1, Pallas kernels, time_steps(): pl.pallas_call(functools.partial(stencil_body, *counts), out_shape=[jax.S...  23.8 us
    ppermute x10, starting transfers between devices, shift(): return lax.ppermute(a, axis, ring(lax.axis_size(axis), d))  21.3 us
    all_to_all x1, blocking collectives, per_device(): got = lax.all_to_all(carries, 'py', split_axis=0, concat_axis=0, tiled=True)  13.3 us
    ppermute x10, waiting for transfers between devices, shift(): return lax.ppermute(a, axis, ring(lax.axis_size(axis), d))  10.1 us
    pallas_call x1, Pallas kernels, own_coefficients(): pl.pallas_call(own_body, out_shape=[pltpu.VMEM((EX, EY, NZ), f32)] * (KEP...  5.15 us
    pallas_call x1, Pallas kernels, halo_parts(): pl.pallas_call(pack_body, out_shape=[jax.ShapeDtypeStruct(s, bf16) for s...  3.09 us
  transfers between devices with their start and end apart: 10, of which 2 were waited for; matrix products, arithmetic and copies ran while one was open for 0% of the time, Pallas kernels for 7%

profile of v4, /device:TPU:0, one launch (start us, length us, event | category | flops | bytes accessed | tf_op | source)
XLA Modules:
  0.0 79.4 jit_solution(7734352157185108371)
XLA Ops:
  0.6 3.1 %pack_faces.1 = (bf16[16,5,16,256]{3,2,1,0:T(8,128)(2,1)S(1)}, bf16[16,5,16,256]{3,2,1,0:T(8,128)(2,1)S(1)}, bf16[21,32,256]{2,1,0:T(8,128)(2,1)S(1)}, bf16[21,32,256]{2,1,0:T(8,128)(2,1)S(1)}) custom-call(s32[1,2]{1,0:T(1,128)} %margin_ref.1, f32[64,32,256]{2,1,0:T(8,128)} %f_hbm.3, bf16[64,32,256]{2,1,0:T(8,128)(2,1)} %k_hbm.3, bf16[3,64,32,256]{3,2,1,0:T(8,128)(2,1)} %v_hbm.3), custom_call_target="tpu_custom_call" | custom-call | tf_op jit(solution)/shard_map/pack_faces/pallas_call | solution.py:624
  3.7 6.6 %collective-permute-start.1 = (bf16[16,5,16,256]{3,2,1,0:T(8,128)(2,1)S(1)}, bf16[16,5,16,256]{3,2,1,0:T(8,128)(2,1)S(1)}, u32[]{:S(2)}, u32[]{:S(2)}) collective-permute-start(bf16[16,5,16,256]{3,2,1,0:T(8,128)(2,1)S(1)} %get-tuple-element.45), channel_id=1, source_target_pairs={{0,15},{1,0},{2,1},{3,2},{4,3},{5,4},{6,5},{7,6},{8,7},{9,8},{10,9... | collective-permute-start | bytes 1966088 | tf_op jit(solution)/shard_map/ppermute | solution.py:549
  10.4 0.0 collective-permute-start
  10.4 0.0 collective-permute-start.2
  10.4 0.0 copy-start.1
  10.4 2.9 %collective-permute-start.3 = (bf16[21,32,256]{2,1,0:T(8,128)(2,1)S(1)}, bf16[21,32,256]{2,1,0:T(8,128)(2,1)S(1)}, u32[]{:S(2)}, u32[]{:S(2)}) collective-permute-start(bf16[21,32,256]{2,1,0:T(8,128)(2,1)S(1)} %get-tuple-element.47), channel_id=1, source_target_pairs={{0,112},{16,0},{32,16},{48,32},{64,48},{80,64},{96,80},{112,96},{1... | collective-permute-start | bytes 1032200 | tf_op jit(solution)/shard_map/ppermute | solution.py:549
  13.3 5.2 %own_coefficients.1 = (f32[72,40,256]{2,1,0:T(8,128)S(1)}, f32[72,40,256]{2,1,0:T(8,128)S(1)}, f32[72,40,256]{2,1,0:T(8,128)S(1)}, f32[72,40,256]{2,1,0:T(8,128)...) custom-call(f32[64,32,256]{2,1,0:T(8,128)} %f_hbm.3, ...), custom_call_target="tpu_custom_call" | custom-call | tf_op jit(solution)/shard_map/own_coefficients/pallas_call | solution.py:474
  18.5 0.0 collective-permute-done.2.xl_ref
  18.5 0.0 collective-permute-done.3.xh_ref
  18.5 0.1 pack_corners.1
  18.6 0.1 collective-permute-start.4
  18.7 5.4 %collective-permute-start.5 = (bf16[10,16,256]{2,1,0:T(8,128)(2,1)S(1)}, bf16[10,16,256]{2,1,0:T(8,128)(2,1)S(1)}, u32[]{:S(2)}, u32[]{:S(2)}) collective-permute-start(bf16[10,16,256]{2,1,0:T(8,128)(2,1)S(1)} %get-tuple-element.63), channel_id=1, source_target_pairs={{0,15},{1,0},{2,1},{3,2},{4,3},{5,4},{6,5},{7,6},{8,7},{9,8},{10,9... | collective-permute-start | bytes 245768 | tf_op jit(solution)/shard_map/ppermute | solution.py:549
  24.1 7.6 %collective-permute-done.4.cl_ref = bf16[10,16,256]{2,1,0:T(8,128)(2,1)S(1)} collective-permute-done((bf16[10,16,256]{2,1,0:T(8,128)(2,1)S(1)}, bf16[10,16,256]{2,1,0:T(8,128)(2,1)S(1)}, u32[]{:S(2)}, u32[]{:S(2)}) %collective-permute-start.4) | collective-permute-done | bytes 81952 | tf_op jit(solution)/shard_map/ppermute | solution.py:549
  31.6 0.0 collective-permute-done.5.ch_ref
  31.6 0.0 collective-permute-done.1.yh_ref
  31.7 23.8 %time_steps.1 = (f32[64,32,256]{2,1,0:T(8,128)}, f32[22,64,128]{2,1,0:T(8,128)S(1)}, f32[16,2816]{1,0:T(8,128)S(1)}, f32[16,2816]{1,0:T(8,128)S(1)}, bf16[16,281...) custom-call(s32[1,2]{1,0:T(1,128)S(1)} %copy-done.1, ...), custom_call_target="tpu_custom_call", output_to_operand_aliasing={{8}: (14, {}), {9}: (15, {}), {10}: (16, {}), {11}: (17, {}... | custom-call | tf_op jit(solution)/shard_map/time_steps/pallas_call | solution.py:495
  55.4 0.0 collective-permute-start.6
  55.5 2.9 %collective-permute-start.7 = (f32[16,2816]{1,0:T(8,128)S(1)}, f32[16,2816]{1,0:T(8,128)S(1)}, u32[]{:S(2)}, u32[]{:S(2)}) collective-permute-start(f32[16,2816]{1,0:T(8,128)S(1)} %get-tuple-element.79), channel_id=1, source_target_pairs={{0,112},{16,0},{32,16},{48,32},{64,48},{80,64},{96,80},{112,96},{1... | collective-permute-start | bytes 540680 | tf_op jit(solution)/shard_map/ppermute | solution.py:549
  58.4 0.3 collective-permute-start.8
  58.7 3.0 %collective-permute-start.9 = (bf16[16,2816]{1,0:T(8,128)(2,1)S(1)}, bf16[16,2816]{1,0:T(8,128)(2,1)S(1)}, u32[]{:S(2)}, u32[]{:S(2)}) collective-permute-start(bf16[16,2816]{1,0:T(8,128)(2,1)S(1)} %get-tuple-element.81), channel_id=1, source_target_pairs={{0,96},{16,112},{32,0},{48,16},{64,32},{80,48},{96,64},{112,80},{1... | collective-permute-start | bytes 270344 | tf_op jit(solution)/shard_map/ppermute | solution.py:549
  61.6 2.5 %collective-permute-done.8.lo2_ref = bf16[16,2816]{1,0:T(8,128)(2,1)S(1)} collective-permute-done((bf16[16,2816]{1,0:T(8,128)(2,1)S(1)}, bf16[16,2816]{1,0:T(8,128)(2,1)S(1)}, u32[]{:S(2)}, u32[]{:S(2)}) %collective-permute-start.8) | collective-permute-done | bytes 90144 | tf_op jit(solution)/shard_map/ppermute | solution.py:549
  64.2 0.8 %combine.1 = (f32[32,16,128]{2,1,0:T(8,128)S(1)}, bf16[16,128,128]{2,1,0:T(8,128)(2,1)S(1)}) custom-call(f32[22,64,128]{2,1,0:T(8,128)S(1)} %get-tuple-element.77.zt_ref, f32[16,2816]{1,0:T(8,128)S(1)} %collective-permute-done.6.lo_ref, f32[16,2816]{1,0:T(8,128)S(1)} %collective-permute-done.7.hi_ref, bf16[16,2816]{1,0:T(8,128)(2,1)S(1)} %collective-permute-done.8.lo2_ref, ...), custom_call_target="tpu_custom_call" | custom-call | tf_op jit(solution)/shard_map/combine/pallas_call | solution.py:519
  65.0 13.3 %all_to_all.5.got_ref = bf16[16,128,128]{2,1,0:T(8,128)(2,1)S(1)} all-to-all(bf16[16,128,128]{2,1,0:T(8,128)(2,1)S(1)} %get-tuple-element.84), channel_id=1, replica_groups=mesh['px'=8,'py'=16] {'py'}, dimensions={0} | all-to-all | bytes 1048576 | tf_op jit(solution)/shard_map/all_to_all | solution.py:664
  78.3 1.1 %add_carries.1 = f32[32,16,128]{2,1,0:T(8,128)} custom-call(f32[32,16,128]{2,1,0:T(8,128)S(1)} %get-tuple-element.83.own_ref, bf16[16,128,128]{2,1,0:T(8,128)(2,1)S(1)} %all_to_all.5.got_ref, bf16[2,128,512]{2,1,0:T(8,128)(2,1)S(1)} %get-tuple-element.85.couple_ref), custom_call_target="tpu_custom_call" | custom-call | tf_op jit(solution)/shard_map/add_carries/pallas_call | solution.py:534
  (7 shorter events, 0.0 us)
Async XLA Ops:
  3.7 27.9 %collective-permute-start.1 = (bf16[16,5,16,256]{3,2,1,0:T(8,128)(2,1)S(1)}, bf16[16,5,16,256]{3,2,1,0:T(8,128)(2,1)S(1)}, u32[]{:S(2)}, u32[]{:S(2)}) collective-permute-start(bf16[16,5,16,256]{3,2,1,0:T(8,128)(2,1)S(1)} %get-tuple-element.45), channel_id=1, source_target_pairs={{0,15},{1,0},{2,1},{3,2},{4,3},{5,4},{6,5},{7,6},{8,7},{9,8},{10,9... | collective-permute-start | bytes 1966088 | tf_op jit(solution)/shard_map/ppermute | solution.py:549
  10.4 21.3 %collective-permute-start = (bf16[16,5,16,256]{3,2,1,0:T(8,128)(2,1)S(1)}, bf16[16,5,16,256]{3,2,1,0:T(8,128)(2,1)S(1)}, u32[]{:S(2)}, u32[]{:S(2)}) collective-permute-start(bf16[16,5,16,256]{3,2,1,0:T(8,128)(2,1)S(1)} %get-tuple-element.44.after_ref), channel_id=1, source_target_pairs={{0,1},{1,2},{2,3},{3,4},{4,5},{5,6},{6,7},{7,8},{8,9},{9,10},{10,1... | collective-permute-start | bytes 1966088 | tf_op jit(solution)/shard_map/ppermute | solution.py:549
  10.4 8.1 %collective-permute-start.2 = (bf16[21,32,256]{2,1,0:T(8,128)(2,1)S(1)}, bf16[21,32,256]{2,1,0:T(8,128)(2,1)S(1)}, u32[]{:S(2)}, u32[]{:S(2)}) collective-permute-start(bf16[21,32,256]{2,1,0:T(8,128)(2,1)S(1)} %get-tuple-element.46), channel_id=1, source_target_pairs={{0,16},{16,32},{32,48},{48,64},{64,80},{80,96},{96,112},{112,0},{1... | collective-permute-start | bytes 1032200 | tf_op jit(solution)/shard_map/ppermute | solution.py:549
  10.4 21.3 %copy-start = (bf16[2,256,128]{2,1,0:T(8,128)(2,1)S(1)}, bf16[2,256,128]{2,1,0:T(8,128)(2,1)}, u32[]{:S(2)}) copy-start(bf16[2,256,128]{2,1,0:T(8,128)(2,1)} %constant.12.clone.fit_ref) | copy-start | bytes 393220
  10.4 21.3 %copy-start.1 = (s32[1,2]{1,0:T(1,128)S(1)}, s32[1,2]{1,0:T(1,128)}, u32[]{:S(2)}) copy-start(s32[1,2]{1,0:T(1,128)} %margin_ref.1) | copy-start | bytes 28
  10.4 8.1 %collective-permute-start.3 = (bf16[21,32,256]{2,1,0:T(8,128)(2,1)S(1)}, bf16[21,32,256]{2,1,0:T(8,128)(2,1)S(1)}, u32[]{:S(2)}, u32[]{:S(2)}) collective-permute-start(bf16[21,32,256]{2,1,0:T(8,128)(2,1)S(1)} %get-tuple-element.47), channel_id=1, source_target_pairs={{0,112},{16,0},{32,16},{48,32},{64,48},{80,64},{96,80},{112,96},{1... | collective-permute-start | bytes 1032200 | tf_op jit(solution)/shard_map/ppermute | solution.py:549
  18.6 13.1 %collective-permute-start.4 = (bf16[10,16,256]{2,1,0:T(8,128)(2,1)S(1)}, bf16[10,16,256]{2,1,0:T(8,128)(2,1)S(1)}, u32[]{:S(2)}, u32[]{:S(2)}) collective-permute-start(bf16[10,16,256]{2,1,0:T(8,128)(2,1)S(1)} %get-tuple-element.62), channel_id=1, source_target_pairs={{0,1},{1,2},{2,3},{3,4},{4,5},{5,6},{6,7},{7,8},{8,9},{9,10},{10,1... | collective-permute-start | bytes 245768 | tf_op jit(solution)/shard_map/ppermute | solution.py:549
  18.7 13.0 %collective-permute-start.5 = (bf16[10,16,256]{2,1,0:T(8,128)(2,1)S(1)}, bf16[10,16,256]{2,1,0:T(8,128)(2,1)S(1)}, u32[]{:S(2)}, u32[]{:S(2)}) collective-permute-start(bf16[10,16,256]{2,1,0:T(8,128)(2,1)S(1)} %get-tuple-element.63), channel_id=1, source_target_pairs={{0,15},{1,0},{2,1},{3,2},{4,3},{5,4},{6,5},{7,6},{8,7},{9,8},{10,9... | collective-permute-start | bytes 245768 | tf_op jit(solution)/shard_map/ppermute | solution.py:549
  55.4 8.7 %collective-permute-start.6 = (f32[16,2816]{1,0:T(8,128)S(1)}, f32[16,2816]{1,0:T(8,128)S(1)}, u32[]{:S(2)}, u32[]{:S(2)}) collective-permute-start(f32[16,2816]{1,0:T(8,128)S(1)} %get-tuple-element.78), channel_id=1, source_target_pairs={{0,16},{16,32},{32,48},{48,64},{64,80},{80,96},{96,112},{112,0},{1... | collective-permute-start | bytes 540680 | tf_op jit(solution)/shard_map/ppermute | solution.py:549
  55.5 8.7 %collective-permute-start.7 = (f32[16,2816]{1,0:T(8,128)S(1)}, f32[16,2816]{1,0:T(8,128)S(1)}, u32[]{:S(2)}, u32[]{:S(2)}) collective-permute-start(f32[16,2816]{1,0:T(8,128)S(1)} %get-tuple-element.79), channel_id=1, source_target_pairs={{0,112},{16,0},{32,16},{48,32},{64,48},{80,64},{96,80},{112,96},{1... | collective-permute-start | bytes 540680 | tf_op jit(solution)/shard_map/ppermute | solution.py:549
  58.4 5.7 %collective-permute-start.8 = (bf16[16,2816]{1,0:T(8,128)(2,1)S(1)}, bf16[16,2816]{1,0:T(8,128)(2,1)S(1)}, u32[]{:S(2)}, u32[]{:S(2)}) collective-permute-start(bf16[16,2816]{1,0:T(8,128)(2,1)S(1)} %get-tuple-element.80), channel_id=1, source_target_pairs={{0,32},{16,48},{32,64},{48,80},{64,96},{80,112},{96,0},{112,16},{1... | collective-permute-start | bytes 270344 | tf_op jit(solution)/shard_map/ppermute | solution.py:549
  58.7 5.5 %collective-permute-start.9 = (bf16[16,2816]{1,0:T(8,128)(2,1)S(1)}, bf16[16,2816]{1,0:T(8,128)(2,1)S(1)}, u32[]{:S(2)}, u32[]{:S(2)}) collective-permute-start(bf16[16,2816]{1,0:T(8,128)(2,1)S(1)} %get-tuple-element.81), channel_id=1, source_target_pairs={{0,96},{16,112},{32,0},{48,16},{64,32},{80,48},{96,64},{112,80},{1... | collective-permute-start | bytes 270344 | tf_op jit(solution)/shard_map/ppermute | solution.py:549

commit v5 on v4

--- a/solution.py
+++ b/solution.py
@@ -194,6 +194,49 @@
     end_ref[1] = k_ref[BX - 1].astype(f32)
 
 
+def x_planes_body(count_x, xl_ref, xh_ref, end_ref, *rest_refs):
+    f32 = jnp.float32
+    u_s, v0_s, v1_s, v2_s, kx_s, ky_s, kyd_s, kz_s, kzd_s, c_s, edge_s = rest_refs[KEPT : 2 * KEPT]
+    kp_s = rest_refs[2 * KEPT]
+    refs = (kx_s, ky_s, kyd_s, kz_s, kzd_s, c_s)
+    p = lax.axis_index("px")
+    from_low_x = jnp.where(p > 0, 1.0, 0.0)
+    from_high_x = jnp.where(p < count_x - 1, 1.0, 0.0)
+    dest = (u_s, None, v0_s, v1_s, v2_s)
+    for n in range(5):
+        for base, ref, scale, near, outer in (
+            (0, xl_ref, from_low_x, (W - 1, W - 2), 0),
+            (BX + W, xh_ref, from_high_x, (0, 1), W - 1),
+        ):
+            for i in range(W):
+                value = ref[n * W + i].astype(f32)
+                if n == 0 and i in near:
+                    value = value + ref[(3 + near.index(i)) * W + outer].astype(f32)
+                value = value * scale
+                if n == 1:
+                    kp_s[base % BX + i] = value
+                    edge_s[base + i, 0:8] = value[0:8]
+                    edge_s[base + i, 8:16] = value[BY - 8 :]
+                else:
+                    dest[n][base + i, 0:BY] = value
+
+    kx_low = jnp.zeros((BY, NZ), f32)
+    for i in range(W):
+        k = kp_s[i]
+        kx = 0.05 * (k + (kp_s[i + 1] if i < W - 1 else end_ref[0]))
+        own_rows(k, kx_low, kx, refs, i)
+        kx_low = kx
+    c_s[W, 0:BY] = c_s[W, 0:BY] - kx_low
+    kx_low = 0.05 * (end_ref[1] + kp_s[W])
+    kx_s[BX + W - 1, 0:BY] = kx_low
+    c_s[BX + W - 1, 0:BY] = c_s[BX + W - 1, 0:BY] - kx_low
+    for i in range(W):
+        k = kp_s[W + i]
+        kx = 0.05 * (k + kp_s[min(W + i + 1, 2 * W - 1)])
+        own_rows(k, kx_low, kx, refs, BX + W + i)
+        kx_low = kx
+
+
 def dot3(a, b):
     dot = functools.partial(jnp.dot, preferred_element_type=jnp.float32)
     return dot(a[0], b[0]) + (dot(a[0], b[1]) + dot(a[1], b[0]))
@@ -212,13 +255,13 @@
 
 
 def stencil_body(count_x, count_y, margin_ref, yl_ref, yh_ref, xl_ref, xh_ref, cl_ref, ch_ref, fit_ref, base_hbm, send_hbm,
-                 near_hbm, ytab_hbm, couple_hbm, end_ref,
+                 near_hbm, ytab_hbm, couple_hbm,
                  *rest_refs):
     f32 = jnp.float32
     outs = rest_refs[KEPT:]
     adv_hbm, zt_ref, lo_ref, hi_ref, lo2_ref, hi2_ref, full_ref, couple_ref = outs[:8]
     u_s, v0_s, v1_s, v2_s, kx_s, ky_s, kyd_s, kz_s, kzd_s, c_s, edge_s = outs[8 : 8 + KEPT]
-    kh_s, kp_s, base_s, send_s, near_s, ytab_s, sems = outs[8 + KEPT :]
+    kh_s, base_s, send_s, near_s, ytab_s, sems = outs[8 + KEPT :]
     p = lax.axis_index("px")
     q = lax.axis_index("py")
 
@@ -264,44 +307,15 @@
         return carry
 
     lax.fori_loop(0, BX // 4, halo_rows, 0)
-    dest = (u_s, None, v0_s, v1_s, v2_s)
+    dest = (u_s, kh_s, v0_s, v1_s, v2_s)
     for n in range(5):
-        for base, ref, corner, scale, near, outer in (
-            (0, xl_ref, 0, from_low_x, (W - 1, W - 2), 0),
-            (BX + W, xh_ref, 5, from_high_x, (0, 1), W - 1),
-        ):
+        at = slice(0, 8) if n == 1 else beyond
+        for base, corner, scale in ((0, 0, from_low_x), (BX + W, 5, from_high_x)):
             low = cl_ref[corner + n].astype(f32) * (scale * from_low_y)
             high = ch_ref[corner + n].astype(f32) * (scale * from_high_y)
             for i in range(W):
-                value = ref[n * W + i].astype(f32)
-                if n == 0 and i in near:
-                    value = value + ref[(3 + near.index(i)) * W + outer].astype(f32)
-                value = value * scale
                 tile = jnp.concatenate([high[4 * i : 4 * i + 4], low[4 * i : 4 * i + 4]], axis=0)
-                if n == 1:
-                    kp_s[base % BX + i] = value
-                    kh_s[base + i] = tile
-                    edge_s[base + i, 0:8] = value[0:8]
-                    edge_s[base + i, 8:16] = value[BY - 8 :]
-                else:
-                    dest[n][base + i, 0:BY] = value
-                    dest[n][base + i, beyond] = tile
-
-    kx_low = jnp.zeros((BY, NZ), f32)
-    for i in range(W):
-        k = kp_s[i]
-        kx = 0.05 * (k + (kp_s[i + 1] if i < W - 1 else end_ref[0]))
-        own_rows(k, kx_low, kx, refs, i)
-        kx_low = kx
-    c_s[W, 0:BY] = c_s[W, 0:BY] - kx_low
-    kx_low = 0.05 * (end_ref[1] + kp_s[W])
-    kx_s[BX + W - 1, 0:BY] = kx_low
-    c_s[BX + W - 1, 0:BY] = c_s[BX + W - 1, 0:BY] - kx_low
-    for i in range(W):
-        k = kp_s[W + i]
-        kx = 0.05 * (k + kp_s[min(W + i + 1, 2 * W - 1)])
-        own_rows(k, kx_low, kx, refs, BX + W + i)
-        kx_low = kx
+                dest[n][base + i, at] = tile
 
     sub = lax.broadcasted_iota(jnp.int32, (8, NZ), 0)
     zt_up, zt_down = z_shifts(8)
@@ -330,8 +344,7 @@
         c_s[x, BY - 8 : BY] = c_s[x, BY - 8 : BY] - up
         return k_next, kx
 
-    lax.fori_loop(0, EX, halo_coefficients, (kh_s[0], jnp.zeros((8, NZ), f32)), unroll=4)
-    z_up, z_down = z_shifts(EY)
+    lax.fori_loop(0, EX, halo_coefficients, (kh_s[0], jnp.zeros((8, NZ), f32)), unroll=8)
 
     row = lax.broadcasted_iota(jnp.int32, (EY, NZ), 0)
     row_mask = jnp.where(row < BY, 1.0, jnp.where(row < BY + W, from_high_y, from_low_y))
@@ -340,28 +353,33 @@
         lo = step
         hi = EX - 1 - step
 
-        def one_plane(x, carry, step=step):
+        rows = EY if step < STEPS - 1 else BY
+        z_up, z_down = z_shifts(rows)
+
+        def one_plane(x, carry, rows=rows, z_up=z_up, z_down=z_down):
             partial, up = carry
-            u = u_s[x]
-            w = 0.025 * u
-            g0 = v0_s[x] * w
+            full = u_s[x]
+            w = 0.025 * full
             g1 = v1_s[x] * w
-            g2 = v2_s[x] * w
-            done = partial + u * (kx_s[x - 1] - g0)
+            y_part = pltpu.roll(full * (ky_s[x] + g1), 1, 0) + pltpu.roll(full * (kyd_s[x] - g1), EY - 1, 0)
+            u = full[:rows]
+            g0 = v0_s[x, 0:rows] * w[:rows]
+            g2 = v2_s[x, 0:rows] * w[:rows]
             prev = x - 1
-            plane_mask = jnp.where(prev < W, from_low_x, jnp.where(prev >= BX + W, from_high_x, 1.0))
-            u_s[prev] = done * (row_mask * plane_mask)
-            up_next = u * (kx_s[x] + g0)
-            total = u * c_s[x] + up
-            total = total + pltpu.roll(u * (ky_s[x] + g1), 1, 0)
-            total = total + pltpu.roll(u * (kyd_s[x] - g1), EY - 1, 0)
-            total = total + z_up(u * (kz_s[x] + g2))
-            total = total + z_down(u * (kzd_s[x] - g2))
+            done = partial + u * (kx_s[prev, 0:rows] - g0)
+            if rows == EY:
+                plane_mask = jnp.where(prev < W, from_low_x, jnp.where(prev >= BX + W, from_high_x, 1.0))
+                done = done * (row_mask * plane_mask)
+            u_s[prev, 0:rows] = done
+            up_next = u * (kx_s[x, 0:rows] + g0)
+            total = u * c_s[x, 0:rows] + up + y_part[:rows]
+            total = total + z_up(u * (kz_s[x, 0:rows] + g2))
+            total = total + z_down(u * (kzd_s[x, 0:rows] - g2))
             return total, up_next
 
-        first_u = u_s[lo]
-        first_up = first_u * (kx_s[lo] + v0_s[lo] * (0.025 * first_u))
-        lax.fori_loop(lo + 1, hi + 1, one_plane, (jnp.zeros((EY, NZ), f32), first_up), unroll=4)
+        first_u = u_s[lo, 0:rows]
+        first_up = first_u * (kx_s[lo, 0:rows] + v0_s[lo, 0:rows] * (0.025 * first_u))
+        lax.fori_loop(lo + 1, hi + 1, one_plane, (jnp.zeros((rows, NZ), f32), first_up), unroll=4)
 
     result = pltpu.make_async_copy(u_s.at[pl.ds(W, BX), pl.ds(0, BY)], adv_hbm, sems.at[6])
     result.start()
@@ -379,7 +397,7 @@
             zt_ref[r, pl.ds(at, 8)] = rows[8 * r : 8 * r + 8]
         return carry
 
-    lax.fori_loop(0, BX // 8, fit_planes, 0, unroll=2)
+    lax.fori_loop(0, BX // 8, fit_planes, 0, unroll=8)
 
     send = halves(send_s[...])
     for r in range(0, YR, 2):
@@ -484,7 +502,22 @@
     )(*[in_hbm(a) for a in (field, diffusivity, velocity)], after)
 
 
-def time_steps(counts, margin, halos, fit, tables, end, kept):
+def x_planes(count_x, xl, xh, end, kept):
+    vmem = pl.BlockSpec(memory_space=pltpu.VMEM)
+    f32 = jnp.float32
+    return pl.pallas_call(
+        functools.partial(x_planes_body, count_x),
+        out_shape=[pltpu.VMEM(a.shape, f32) for a in kept],
+        in_specs=[vmem] * (3 + KEPT),
+        out_specs=[vmem] * KEPT,
+        input_output_aliases={3 + i: i for i in range(KEPT)},
+        scratch_shapes=[pltpu.VMEM((2 * W, BY, NZ), f32)],
+        compiler_params=pltpu.CompilerParams(vmem_limit_bytes=8 * 1024 * 1024),
+        name="x_planes",
+    )(xl, xh, end, *kept)
+
+
+def time_steps(counts, margin, halos, fit, tables, kept):
     vmem = pl.BlockSpec(memory_space=pltpu.VMEM)
     smem = pl.BlockSpec(memory_space=pltpu.SMEM)
     hbm = pl.BlockSpec(memory_space=pltpu.HBM)
@@ -497,12 +530,11 @@
         out_shape=[jax.ShapeDtypeStruct(s, t) for s, t in shapes]
         + [pltpu.VMEM(tables[-1].shape[1:], bf16)]
         + [pltpu.VMEM(a.shape, f32) for a in kept],
-        in_specs=[smem] + [vmem] * 7 + [hbm] * 5 + [vmem] * (1 + KEPT),
+        in_specs=[smem] + [vmem] * 7 + [hbm] * 5 + [vmem] * KEPT,
         out_specs=[hbm] + [vmem] * (7 + KEPT),
-        input_output_aliases={14 + i: 8 + i for i in range(KEPT)},
+        input_output_aliases={13 + i: 8 + i for i in range(KEPT)},
         scratch_shapes=[
             pltpu.VMEM((EX, 8, NZ), f32),
-            pltpu.VMEM((2 * W, BY, NZ), f32),
             pltpu.VMEM((BX // 2, 128), f32),
             pltpu.VMEM((BX // 2, BX), f32),
             pltpu.VMEM((2, 8, 128), f32),
@@ -511,7 +543,7 @@
         ],
         compiler_params=pltpu.CompilerParams(vmem_limit_bytes=STEP_VMEM * 1024 * 1024),
         name="time_steps",
-    )(margin, *halos, fit, *[in_hbm(t) for t in tables], end, *kept)[:8]
+    )(margin, *halos, fit, *[in_hbm(t) for t in tables], *kept)[:8]
 
 
 def combine(count_y, rows):
@@ -646,7 +678,8 @@
         name="pack_corners",
     )(xl, xh)
     halos = (yl, yh, xl, xh, shift(c_up, "py", 1), shift(c_down, "py", -1))
-    return halos, kept
+    _, kept = lax.optimization_barrier((c_up, kept))
+    return halos, x_planes(lax.axis_size("px"), xl, xh, kept[KEPT], kept[:KEPT])
 
 
 def per_device(field, diffusivity, velocity, margin):
@@ -657,7 +690,7 @@
     tables = [jnp.asarray(t) for t in x_tables(count_x) + [ytab, couple]]
     halos, kept = halo_parts(field, diffusivity, velocity, margin)
     advected, zt, lo, hi, lo2, hi2, full, couple = time_steps(
-        (count_x, count_y), margin, halos, fit, tables, kept[KEPT], kept[:KEPT]
+        (count_x, count_y), margin, halos, fit, tables, kept
     )
     rows = (zt, shift(lo, "px", 1), shift(hi, "px", -1), shift(lo2, "px", 2), shift(hi2, "px", -2), full)
     own, carries = combine(count_y, rows)

time: 79.7 us -> 76.4 us (0.959)
  Pallas kernels: 34 us -> 30.8 us
    pallas_call x1, Pallas kernels: 23.8 us -> 20.3 us  [time_steps(): pl.pallas_call(functools.partial(stencil_body, *counts), out_shape=[jax.S...]
  transfers between devices with their start and end apart: 10 -> 10, of which waited for: 2 -> 3; matrix products, arithmetic and copies ran while one was open for 0% -> 0% of each run, Pallas kernels for 7% -> 7%
where the time goes in v5:
time: 76.4 us; the launch traced here: 75.7 us
  Pallas kernels  30.8 us (40%)
  starting transfers between devices  21.2 us (28%)
  blocking collectives  12.9 us (17%)
  waiting for transfers between devices  10 us (13%)
    ppermute x10, starting transfers between devices, shift(): return lax.ppermute(a, axis, ring(lax.axis_size(axis), d))  21.2 us
    pallas_call x1, Pallas kernels, time_steps(): pl.pallas_call(functools.partial(stencil_body, *counts), out_shape=[jax.S...  20.3 us
    all_to_all x1, blocking collectives, per_device(): got = lax.all_to_all(carries, 'py', split_axis=0, concat_axis=0, tiled=True)  12.9 us
    ppermute x10, waiting for transfers between devices, shift(): return lax.ppermute(a, axis, ring(lax.axis_size(axis), d))  10 us
    pallas_call x1, Pallas kernels, own_coefficients(): pl.pallas_call(own_body, out_shape=[pltpu.VMEM((EX, EY, NZ), f32)] * (KEP...  5.16 us
    pallas_call x1, Pallas kernels, halo_parts(): pl.pallas_call(pack_body, out_shape=[jax.ShapeDtypeStruct(s, bf16) for s...  3.09 us
  transfers between devices with their start and end apart: 10, of which 3 were waited for; matrix products, arithmetic and copies ran while one was open for 0% of the time, Pallas kernels for 7%

profile of v5, /device:TPU:0, one launch (start us, length us, event | category | flops | bytes accessed | tf_op | source)
XLA Modules:
  0.0 75.7 jit_solution(9252429234990440765)
XLA Ops:
  0.6 3.1 %pack_faces.1 = (bf16[16,5,16,256]{3,2,1,0:T(8,128)(2,1)S(1)}, bf16[16,5,16,256]{3,2,1,0:T(8,128)(2,1)S(1)}, bf16[21,32,256]{2,1,0:T(8,128)(2,1)S(1)}, bf16[21,32,256]{2,1,0:T(8,128)(2,1)S(1)}) custom-call(s32[1,2]{1,0:T(1,128)} %margin_ref.1, f32[64,32,256]{2,1,0:T(8,128)} %f_hbm.3, bf16[64,32,256]{2,1,0:T(8,128)(2,1)} %k_hbm.3, bf16[3,64,32,256]{3,2,1,0:T(8,128)(2,1)} %v_hbm.3), custom_call_target="tpu_custom_call" | custom-call | tf_op jit(solution)/shard_map/pack_faces/pallas_call | solution.py:656
  3.7 6.6 %collective-permute-start.1 = (bf16[16,5,16,256]{3,2,1,0:T(8,128)(2,1)S(1)}, bf16[16,5,16,256]{3,2,1,0:T(8,128)(2,1)S(1)}, u32[]{:S(2)}, u32[]{:S(2)}) collective-permute-start(bf16[16,5,16,256]{3,2,1,0:T(8,128)(2,1)S(1)} %get-tuple-element.68), channel_id=1, source_target_pairs={{0,15},{1,0},{2,1},{3,2},{4,3},{5,4},{6,5},{7,6},{8,7},{9,8},{10,9... | collective-permute-start | bytes 1966088 | tf_op jit(solution)/shard_map/ppermute | solution.py:581
  10.4 0.0 collective-permute-start
  10.4 0.0 collective-permute-start.2
  10.4 3.0 %collective-permute-start.3 = (bf16[21,32,256]{2,1,0:T(8,128)(2,1)S(1)}, bf16[21,32,256]{2,1,0:T(8,128)(2,1)S(1)}, u32[]{:S(2)}, u32[]{:S(2)}) collective-permute-start(bf16[21,32,256]{2,1,0:T(8,128)(2,1)S(1)} %get-tuple-element.70), channel_id=1, source_target_pairs={{0,112},{16,0},{32,16},{48,32},{64,48},{80,64},{96,80},{112,96},{1... | collective-permute-start | bytes 1032200 | tf_op jit(solution)/shard_map/ppermute | solution.py:581
  13.3 5.2 %own_coefficients.1 = (f32[72,40,256]{2,1,0:T(8,128)S(1)}, f32[72,40,256]{2,1,0:T(8,128)S(1)}, f32[72,40,256]{2,1,0:T(8,128)S(1)}, f32[72,40,256]{2,1,0:T(8,128)...) custom-call(f32[64,32,256]{2,1,0:T(8,128)} %f_hbm.3, ...), custom_call_target="tpu_custom_call" | custom-call | tf_op jit(solution)/shard_map/own_coefficients/pallas_call | solution.py:492
  18.5 0.0 collective-permute-done.2.xl_ref
  18.5 0.0 collective-permute-done.3.xh_ref
  18.5 0.1 pack_corners.1
  18.6 5.4 %collective-permute-start.5 = (bf16[10,16,256]{2,1,0:T(8,128)(2,1)S(1)}, bf16[10,16,256]{2,1,0:T(8,128)(2,1)S(1)}, u32[]{:S(2)}, u32[]{:S(2)}) collective-permute-start(bf16[10,16,256]{2,1,0:T(8,128)(2,1)S(1)} %get-tuple-element.86), channel_id=1, source_target_pairs={{0,15},{1,0},{2,1},{3,2},{4,3},{5,4},{6,5},{7,6},{8,7},{9,8},{10,9... | collective-permute-start | bytes 245768 | tf_op jit(solution)/shard_map/ppermute | solution.py:581
  24.0 0.0 collective-permute-start.4
  24.0 0.3 x_planes.1
  24.3 2.0 %collective-permute-done.5.ch_ref = bf16[10,16,256]{2,1,0:T(8,128)(2,1)S(1)} collective-permute-done((bf16[10,16,256]{2,1,0:T(8,128)(2,1)S(1)}, bf16[10,16,256]{2,1,0:T(8,128)(2,1)S(1)}, u32[]{:S(2)}, u32[]{:S(2)}) %collective-permute-start.5) | collective-permute-done | bytes 81952 | tf_op jit(solution)/shard_map/ppermute | solution.py:581
  26.3 5.5 %collective-permute-done.4.cl_ref = bf16[10,16,256]{2,1,0:T(8,128)(2,1)S(1)} collective-permute-done((bf16[10,16,256]{2,1,0:T(8,128)(2,1)S(1)}, bf16[10,16,256]{2,1,0:T(8,128)(2,1)S(1)}, u32[]{:S(2)}, u32[]{:S(2)}) %collective-permute-start.4) | collective-permute-done | bytes 81952 | tf_op jit(solution)/shard_map/ppermute | solution.py:581
  31.8 0.0 collective-permute-done.1.yh_ref
  31.8 0.0 collective-permute-done.yl_ref
  31.8 20.3 %time_steps.1 = (f32[64,32,256]{2,1,0:T(8,128)}, f32[22,64,128]{2,1,0:T(8,128)S(1)}, f32[16,2816]{1,0:T(8,128)S(1)}, f32[16,2816]{1,0:T(8,128)S(1)}, bf16[16,281...) custom-call(s32[1,2]{1,0:T(1,128)S(1)} %copy-done.1, ...), custom_call_target="tpu_custom_call", output_to_operand_aliasing={{8}: (13, {}), {9}: (14, {}), {10}: (15, {}), {11}: (16, {}... | custom-call | tf_op jit(solution)/shard_map/time_steps/pallas_call | solution.py:528
  52.1 0.0 collective-permute-start.6
  52.2 2.9 %collective-permute-start.7 = (f32[16,2816]{1,0:T(8,128)S(1)}, f32[16,2816]{1,0:T(8,128)S(1)}, u32[]{:S(2)}, u32[]{:S(2)}) collective-permute-start(f32[16,2816]{1,0:T(8,128)S(1)} %get-tuple-element.125), channel_id=1, source_target_pairs={{0,112},{16,0},{32,16},{48,32},{64,48},{80,64},{96,80},{112,96},{1... | collective-permute-start | bytes 540680 | tf_op jit(solution)/shard_map/ppermute | solution.py:581
  55.1 3.2 %collective-permute-start.9 = (bf16[16,2816]{1,0:T(8,128)(2,1)S(1)}, bf16[16,2816]{1,0:T(8,128)(2,1)S(1)}, u32[]{:S(2)}, u32[]{:S(2)}) collective-permute-start(bf16[16,2816]{1,0:T(8,128)(2,1)S(1)} %get-tuple-element.127), channel_id=1, source_target_pairs={{0,96},{16,112},{32,0},{48,16},{64,32},{80,48},{96,64},{112,80},{1... | collective-permute-start | bytes 270344 | tf_op jit(solution)/shard_map/ppermute | solution.py:581
  58.3 2.5 %collective-permute-done.8.lo2_ref = bf16[16,2816]{1,0:T(8,128)(2,1)S(1)} collective-permute-done((bf16[16,2816]{1,0:T(8,128)(2,1)S(1)}, bf16[16,2816]{1,0:T(8,128)(2,1)S(1)}, u32[]{:S(2)}, u32[]{:S(2)}) %collective-permute-start.8) | collective-permute-done | bytes 90144 | tf_op jit(solution)/shard_map/ppermute | solution.py:581
  60.9 0.8 %combine.1 = (f32[32,16,128]{2,1,0:T(8,128)S(1)}, bf16[16,128,128]{2,1,0:T(8,128)(2,1)S(1)}) custom-call(f32[22,64,128]{2,1,0:T(8,128)S(1)} %get-tuple-element.123.zt_ref, f32[16,2816]{1,0:T(8,128)S(1)} %collective-permute-done.6.lo_ref, f32[16,2816]{1,0:T(8,128)S(1)} %collective-permute-done.7.hi_ref, bf16[16,2816]{1,0:T(8,128)(2,1)S(1)} %collective-permute-done.8.lo2_ref, ...), custom_call_target="tpu_custom_call" | custom-call | tf_op jit(solution)/shard_map/combine/pallas_call | solution.py:551
  61.7 12.9 %all_to_all.5.got_ref = bf16[16,128,128]{2,1,0:T(8,128)(2,1)S(1)} all-to-all(bf16[16,128,128]{2,1,0:T(8,128)(2,1)S(1)} %get-tuple-element.130), channel_id=1, replica_groups=mesh['px'=8,'py'=16] {'py'}, dimensions={0} | all-to-all | bytes 1048576 | tf_op jit(solution)/shard_map/all_to_all | solution.py:697
  74.6 1.1 %add_carries.1 = f32[32,16,128]{2,1,0:T(8,128)} custom-call(f32[32,16,128]{2,1,0:T(8,128)S(1)} %get-tuple-element.129.own_ref, bf16[16,128,128]{2,1,0:T(8,128)(2,1)S(1)} %all_to_all.5.got_ref, bf16[2,128,512]{2,1,0:T(8,128)(2,1)S(1)} %get-tuple-element.131.couple_ref), custom_call_target="tpu_custom_call" | custom-call | tf_op jit(solution)/shard_map/add_carries/pallas_call | solution.py:566
  (8 shorter events, 0.0 us)
Async XLA Ops:
  3.7 28.1 %collective-permute-start.1 = (bf16[16,5,16,256]{3,2,1,0:T(8,128)(2,1)S(1)}, bf16[16,5,16,256]{3,2,1,0:T(8,128)(2,1)S(1)}, u32[]{:S(2)}, u32[]{:S(2)}) collective-permute-start(bf16[16,5,16,256]{3,2,1,0:T(8,128)(2,1)S(1)} %get-tuple-element.68), channel_id=1, source_target_pairs={{0,15},{1,0},{2,1},{3,2},{4,3},{5,4},{6,5},{7,6},{8,7},{9,8},{10,9... | collective-permute-start | bytes 1966088 | tf_op jit(solution)/shard_map/ppermute | solution.py:581
  10.4 21.5 %collective-permute-start = (bf16[16,5,16,256]{3,2,1,0:T(8,128)(2,1)S(1)}, bf16[16,5,16,256]{3,2,1,0:T(8,128)(2,1)S(1)}, u32[]{:S(2)}, u32[]{:S(2)}) collective-permute-start(bf16[16,5,16,256]{3,2,1,0:T(8,128)(2,1)S(1)} %get-tuple-element.67.after_ref), channel_id=1, source_target_pairs={{0,1},{1,2},{2,3},{3,4},{4,5},{5,6},{6,7},{7,8},{8,9},{9,10},{10,1... | collective-permute-start | bytes 1966088 | tf_op jit(solution)/shard_map/ppermute | solution.py:581
  10.4 8.1 %collective-permute-start.2 = (bf16[21,32,256]{2,1,0:T(8,128)(2,1)S(1)}, bf16[21,32,256]{2,1,0:T(8,128)(2,1)S(1)}, u32[]{:S(2)}, u32[]{:S(2)}) collective-permute-start(bf16[21,32,256]{2,1,0:T(8,128)(2,1)S(1)} %get-tuple-element.69), channel_id=1, source_target_pairs={{0,16},{16,32},{32,48},{48,64},{64,80},{80,96},{96,112},{112,0},{1... | collective-permute-start | bytes 1032200 | tf_op jit(solution)/shard_map/ppermute | solution.py:581
  10.4 8.1 %collective-permute-start.3 = (bf16[21,32,256]{2,1,0:T(8,128)(2,1)S(1)}, bf16[21,32,256]{2,1,0:T(8,128)(2,1)S(1)}, u32[]{:S(2)}, u32[]{:S(2)}) collective-permute-start(bf16[21,32,256]{2,1,0:T(8,128)(2,1)S(1)} %get-tuple-element.70), channel_id=1, source_target_pairs={{0,112},{16,0},{32,16},{48,32},{64,48},{80,64},{96,80},{112,96},{1... | collective-permute-start | bytes 1032200 | tf_op jit(solution)/shard_map/ppermute | solution.py:581
  18.6 7.7 %collective-permute-start.5 = (bf16[10,16,256]{2,1,0:T(8,128)(2,1)S(1)}, bf16[10,16,256]{2,1,0:T(8,128)(2,1)S(1)}, u32[]{:S(2)}, u32[]{:S(2)}) collective-permute-start(bf16[10,16,256]{2,1,0:T(8,128)(2,1)S(1)} %get-tuple-element.86), channel_id=1, source_target_pairs={{0,15},{1,0},{2,1},{3,2},{4,3},{5,4},{6,5},{7,6},{8,7},{9,8},{10,9... | collective-permute-start | bytes 245768 | tf_op jit(solution)/shard_map/ppermute | solution.py:581
  24.0 7.8 %copy-start = (bf16[2,256,128]{2,1,0:T(8,128)(2,1)S(1)}, bf16[2,256,128]{2,1,0:T(8,128)(2,1)}, u32[]{:S(2)}) copy-start(bf16[2,256,128]{2,1,0:T(8,128)(2,1)} %constant.12.clone.fit_ref) | copy-start | bytes 393220
  24.0 7.8 %copy-start.1 = (s32[1,2]{1,0:T(1,128)S(1)}, s32[1,2]{1,0:T(1,128)}, u32[]{:S(2)}) copy-start(s32[1,2]{1,0:T(1,128)} %margin_ref.1) | copy-start | bytes 28
  24.0 7.8 %collective-permute-start.4 = (bf16[10,16,256]{2,1,0:T(8,128)(2,1)S(1)}, bf16[10,16,256]{2,1,0:T(8,128)(2,1)S(1)}, u32[]{:S(2)}, u32[]{:S(2)}) collective-permute-start(bf16[10,16,256]{2,1,0:T(8,128)(2,1)S(1)} %get-tuple-element.85), channel_id=1, source_target_pairs={{0,1},{1,2},{2,3},{3,4},{4,5},{5,6},{6,7},{7,8},{8,9},{9,10},{10,1... | collective-permute-start | bytes 245768 | tf_op jit(solution)/shard_map/ppermute | solution.py:581
  52.1 8.7 %collective-permute-start.6 = (f32[16,2816]{1,0:T(8,128)S(1)}, f32[16,2816]{1,0:T(8,128)S(1)}, u32[]{:S(2)}, u32[]{:S(2)}) collective-permute-start(f32[16,2816]{1,0:T(8,128)S(1)} %get-tuple-element.124), channel_id=1, source_target_pairs={{0,16},{16,32},{32,48},{48,64},{64,80},{80,96},{96,112},{112,0},{1... | collective-permute-start | bytes 540680 | tf_op jit(solution)/shard_map/ppermute | solution.py:581
  52.2 8.7 %collective-permute-start.7 = (f32[16,2816]{1,0:T(8,128)S(1)}, f32[16,2816]{1,0:T(8,128)S(1)}, u32[]{:S(2)}, u32[]{:S(2)}) collective-permute-start(f32[16,2816]{1,0:T(8,128)S(1)} %get-tuple-element.125), channel_id=1, source_target_pairs={{0,112},{16,0},{32,16},{48,32},{64,48},{80,64},{96,80},{112,96},{1... | collective-permute-start | bytes 540680 | tf_op jit(solution)/shard_map/ppermute | solution.py:581
  55.1 5.7 %collective-permute-start.8 = (bf16[16,2816]{1,0:T(8,128)(2,1)S(1)}, bf16[16,2816]{1,0:T(8,128)(2,1)S(1)}, u32[]{:S(2)}, u32[]{:S(2)}) collective-permute-start(bf16[16,2816]{1,0:T(8,128)(2,1)S(1)} %get-tuple-element.126), channel_id=1, source_target_pairs={{0,32},{16,48},{32,64},{48,80},{64,96},{80,112},{96,0},{112,16},{1... | collective-permute-start | bytes 270344 | tf_op jit(solution)/shard_map/ppermute | solution.py:581
  55.1 5.7 %collective-permute-start.9 = (bf16[16,2816]{1,0:T(8,128)(2,1)S(1)}, bf16[16,2816]{1,0:T(8,128)(2,1)S(1)}, u32[]{:S(2)}, u32[]{:S(2)}) collective-permute-start(bf16[16,2816]{1,0:T(8,128)(2,1)S(1)} %get-tuple-element.127), channel_id=1, source_target_pairs={{0,96},{16,112},{32,0},{48,16},{64,32},{80,48},{96,64},{112,80},{1... | collective-permute-start | bytes 270344 | tf_op jit(solution)/shard_map/ppermute | solution.py:581

commit v6 on v5

--- a/solution.py
+++ b/solution.py
@@ -308,13 +308,18 @@
 
     lax.fori_loop(0, BX // 4, halo_rows, 0)
     dest = (u_s, kh_s, v0_s, v1_s, v2_s)
-    for n in range(5):
-        at = slice(0, 8) if n == 1 else beyond
-        for base, corner, scale in ((0, 0, from_low_x), (BX + W, 5, from_high_x)):
-            low = cl_ref[corner + n].astype(f32) * (scale * from_low_y)
-            high = ch_ref[corner + n].astype(f32) * (scale * from_high_y)
+    none = jnp.zeros((1, NZ), f32)
+    for base, corner, scale, near in ((0, 0, from_low_x, range(1, W)), (BX + W, 3, from_high_x, range(W - 1))):
+        low = cl_ref[corner : corner + 3].astype(f32).reshape(48, NZ) * (scale * from_low_y)
+        high = ch_ref[corner : corner + 3].astype(f32).reshape(48, NZ) * (scale * from_high_y)
+        for n in range(5):
+            at = slice(0, 8) if n == 1 else beyond
             for i in range(W):
-                tile = jnp.concatenate([high[4 * i : 4 * i + 4], low[4 * i : 4 * i + 4]], axis=0)
+                if i in near:
+                    row = (n * 3 + near.index(i)) * 3
+                    tile = jnp.concatenate([high[row : row + 3], none, none, low[row : row + 3]], axis=0)
+                else:
+                    tile = jnp.zeros((8, NZ), f32)
                 dest[n][base + i, at] = tile
 
     sub = lax.broadcasted_iota(jnp.int32, (8, NZ), 0)
@@ -639,18 +644,19 @@
 
 def corner_body(xl_ref, xh_ref, up_ref, down_ref):
     f32 = jnp.float32
-    for side, ref in enumerate((xl_ref, xh_ref)):
-        for n in range(5):
-            planes = [ref[n * W + i].astype(f32) for i in range(W)]
-            up_ref[side * 5 + n] = jnp.concatenate([a[BY - W :] for a in planes], axis=0).astype(jnp.bfloat16)
-            down_ref[side * 5 + n] = jnp.concatenate([a[:W] for a in planes], axis=0).astype(jnp.bfloat16)
+    for side, ref, near in ((0, xl_ref, range(1, W)), (1, xh_ref, range(W - 1))):
+        planes = [ref[n * W + i].astype(f32) for n in range(5) for i in near]
+        gap = [jnp.zeros((3, NZ), f32)]
+        part = slice(side * 3, side * 3 + 3)
+        for out, rows in ((up_ref, slice(BY - 3, BY)), (down_ref, slice(0, 3))):
+            out[part] = jnp.concatenate([a[rows] for a in planes] + gap, axis=0).reshape(3, 16, NZ).astype(jnp.bfloat16)
 
 
 def halo_parts(field, diffusivity, velocity, margin):
     bf16 = jnp.bfloat16
     y_shape = (BX // 4, 5, 16, NZ)
     x_shape = (5 * W + 1, BY, NZ)
-    c_shape = (10, 16, NZ)
+    c_shape = (6, 16, NZ)
     vmem = pl.BlockSpec(memory_space=pltpu.VMEM)
     hbm = pl.BlockSpec(memory_space=pltpu.HBM)
     ylo, yhi, xlo, xhi = pl.pallas_call(

time: 76.4 us -> 75.9 us (level)
  no operation moved by 1% of the time
where the time goes in v6:
time: 75.9 us; the launch traced here: 75.2 us
  Pallas kernels  30.8 us (41%)
  starting transfers between devices  21.2 us (28%)
  blocking collectives  12.8 us (17%)
  waiting for transfers between devices  9.63 us (13%)
    ppermute x10, starting transfers between devices, shift(): return lax.ppermute(a, axis, ring(lax.axis_size(axis), d))  21.2 us
    pallas_call x1, Pallas kernels, time_steps(): pl.pallas_call(functools.partial(stencil_body, *counts), out_shape=[jax.S...  20.3 us
    all_to_all x1, blocking collectives, per_device(): got = lax.all_to_all(carries, 'py', split_axis=0, concat_axis=0, tiled=True)  12.8 us
    ppermute x10, waiting for transfers between devices, shift(): return lax.ppermute(a, axis, ring(lax.axis_size(axis), d))  9.63 us
    pallas_call x1, Pallas kernels, own_coefficients(): pl.pallas_call(own_body, out_shape=[pltpu.VMEM((EX, EY, NZ), f32)] * (KEP...  5.16 us
    pallas_call x1, Pallas kernels, halo_parts(): pl.pallas_call(pack_body, out_shape=[jax.ShapeDtypeStruct(s, bf16) for s...  3.09 us
  transfers between devices with their start and end apart: 10, of which 3 were waited for; matrix products, arithmetic and copies ran while one was open for 0% of the time, Pallas kernels for 7%

profile of v6, /device:TPU:0, one launch (start us, length us, event | category | flops | bytes accessed | tf_op | source)
XLA Modules:
  0.0 75.2 jit_solution(14942656286119388222)
XLA Ops:
  0.6 3.1 %pack_faces.1 = (bf16[16,5,16,256]{3,2,1,0:T(8,128)(2,1)S(1)}, bf16[16,5,16,256]{3,2,1,0:T(8,128)(2,1)S(1)}, bf16[21,32,256]{2,1,0:T(8,128)(2,1)S(1)}, bf16[21,32,256]{2,1,0:T(8,128)(2,1)S(1)}) custom-call(s32[1,2]{1,0:T(1,128)} %margin_ref.1, f32[64,32,256]{2,1,0:T(8,128)} %f_hbm.3, bf16[64,32,256]{2,1,0:T(8,128)(2,1)} %k_hbm.3, bf16[3,64,32,256]{3,2,1,0:T(8,128)(2,1)} %v_hbm.3), custom_call_target="tpu_custom_call" | custom-call | tf_op jit(solution)/shard_map/pack_faces/pallas_call | solution.py:662
  3.7 6.6 %collective-permute-start.1 = (bf16[16,5,16,256]{3,2,1,0:T(8,128)(2,1)S(1)}, bf16[16,5,16,256]{3,2,1,0:T(8,128)(2,1)S(1)}, u32[]{:S(2)}, u32[]{:S(2)}) collective-permute-start(bf16[16,5,16,256]{3,2,1,0:T(8,128)(2,1)S(1)} %get-tuple-element.68), channel_id=1, source_target_pairs={{0,15},{1,0},{2,1},{3,2},{4,3},{5,4},{6,5},{7,6},{8,7},{9,8},{10,9... | collective-permute-start | bytes 1966088 | tf_op jit(solution)/shard_map/ppermute | solution.py:586
  10.4 0.0 collective-permute-start
  10.4 0.0 collective-permute-start.2
  10.4 3.0 %collective-permute-start.3 = (bf16[21,32,256]{2,1,0:T(8,128)(2,1)S(1)}, bf16[21,32,256]{2,1,0:T(8,128)(2,1)S(1)}, u32[]{:S(2)}, u32[]{:S(2)}) collective-permute-start(bf16[21,32,256]{2,1,0:T(8,128)(2,1)S(1)} %get-tuple-element.70), channel_id=1, source_target_pairs={{0,112},{16,0},{32,16},{48,32},{64,48},{80,64},{96,80},{112,96},{1... | collective-permute-start | bytes 1032200 | tf_op jit(solution)/shard_map/ppermute | solution.py:586
  13.3 5.2 %own_coefficients.1 = (f32[72,40,256]{2,1,0:T(8,128)S(1)}, f32[72,40,256]{2,1,0:T(8,128)S(1)}, f32[72,40,256]{2,1,0:T(8,128)S(1)}, f32[72,40,256]{2,1,0:T(8,128)...) custom-call(f32[64,32,256]{2,1,0:T(8,128)} %f_hbm.3, ...), custom_call_target="tpu_custom_call" | custom-call | tf_op jit(solution)/shard_map/own_coefficients/pallas_call | solution.py:497
  18.5 0.0 collective-permute-done.3.xh_ref
  18.5 0.1 pack_corners.1
  18.6 5.4 %collective-permute-start.5 = (bf16[6,16,256]{2,1,0:T(8,128)(2,1)S(1)}, bf16[6,16,256]{2,1,0:T(8,128)(2,1)S(1)}, u32[]{:S(2)}, u32[]{:S(2)}) collective-permute-start(bf16[6,16,256]{2,1,0:T(8,128)(2,1)S(1)} %get-tuple-element.86), channel_id=1, source_target_pairs={{0,15},{1,0},{2,1},{3,2},{4,3},{5,4},{6,5},{7,6},{8,7},{9,8},{10,9... | collective-permute-start | bytes 147464 | tf_op jit(solution)/shard_map/ppermute | solution.py:586
  24.0 0.3 x_planes.1
  24.3 1.4 %collective-permute-done.5.ch_ref = bf16[6,16,256]{2,1,0:T(8,128)(2,1)S(1)} collective-permute-done((bf16[6,16,256]{2,1,0:T(8,128)(2,1)S(1)}, bf16[6,16,256]{2,1,0:T(8,128)(2,1)S(1)}, u32[]{:S(2)}, u32[]{:S(2)}) %collective-permute-start.5) | collective-permute-done | bytes 49184 | tf_op jit(solution)/shard_map/ppermute | solution.py:586
  25.7 5.7 %collective-permute-done.4.cl_ref = bf16[6,16,256]{2,1,0:T(8,128)(2,1)S(1)} collective-permute-done((bf16[6,16,256]{2,1,0:T(8,128)(2,1)S(1)}, bf16[6,16,256]{2,1,0:T(8,128)(2,1)S(1)}, u32[]{:S(2)}, u32[]{:S(2)}) %collective-permute-start.4) | collective-permute-done | bytes 49184 | tf_op jit(solution)/shard_map/ppermute | solution.py:586
  31.4 0.0 collective-permute-done.1.yh_ref
  31.4 0.0 collective-permute-done.yl_ref
  31.4 20.3 %time_steps.1 = (f32[64,32,256]{2,1,0:T(8,128)}, f32[22,64,128]{2,1,0:T(8,128)S(1)}, f32[16,2816]{1,0:T(8,128)S(1)}, f32[16,2816]{1,0:T(8,128)S(1)}, bf16[16,281...) custom-call(s32[1,2]{1,0:T(1,128)S(1)} %copy-done.1, ...), custom_call_target="tpu_custom_call", output_to_operand_aliasing={{8}: (13, {}), {9}: (14, {}), {10}: (15, {}), {11}: (16, {}... | custom-call | tf_op jit(solution)/shard_map/time_steps/pallas_call | solution.py:533
  51.7 0.0 collective-permute-start.6
  51.8 2.9 %collective-permute-start.7 = (f32[16,2816]{1,0:T(8,128)S(1)}, f32[16,2816]{1,0:T(8,128)S(1)}, u32[]{:S(2)}, u32[]{:S(2)}) collective-permute-start(f32[16,2816]{1,0:T(8,128)S(1)} %get-tuple-element.125), channel_id=1, source_target_pairs={{0,112},{16,0},{32,16},{48,32},{64,48},{80,64},{96,80},{112,96},{1... | collective-permute-start | bytes 540680 | tf_op jit(solution)/shard_map/ppermute | solution.py:586
  54.7 3.2 %collective-permute-start.9 = (bf16[16,2816]{1,0:T(8,128)(2,1)S(1)}, bf16[16,2816]{1,0:T(8,128)(2,1)S(1)}, u32[]{:S(2)}, u32[]{:S(2)}) collective-permute-start(bf16[16,2816]{1,0:T(8,128)(2,1)S(1)} %get-tuple-element.127), channel_id=1, source_target_pairs={{0,96},{16,112},{32,0},{48,16},{64,32},{80,48},{96,64},{112,80},{1... | collective-permute-start | bytes 270344 | tf_op jit(solution)/shard_map/ppermute | solution.py:586
  57.9 2.5 %collective-permute-done.8.lo2_ref = bf16[16,2816]{1,0:T(8,128)(2,1)S(1)} collective-permute-done((bf16[16,2816]{1,0:T(8,128)(2,1)S(1)}, bf16[16,2816]{1,0:T(8,128)(2,1)S(1)}, u32[]{:S(2)}, u32[]{:S(2)}) %collective-permute-start.8) | collective-permute-done | bytes 90144 | tf_op jit(solution)/shard_map/ppermute | solution.py:586
  60.4 0.0 collective-permute-done.6.lo_ref
  60.4 0.0 collective-permute-done.7.hi_ref
  60.4 0.8 %combine.1 = (f32[32,16,128]{2,1,0:T(8,128)S(1)}, bf16[16,128,128]{2,1,0:T(8,128)(2,1)S(1)}) custom-call(f32[22,64,128]{2,1,0:T(8,128)S(1)} %get-tuple-element.123.zt_ref, f32[16,2816]{1,0:T(8,128)S(1)} %collective-permute-done.6.lo_ref, f32[16,2816]{1,0:T(8,128)S(1)} %collective-permute-done.7.hi_ref, bf16[16,2816]{1,0:T(8,128)(2,1)S(1)} %collective-permute-done.8.lo2_ref, ...), custom_call_target="tpu_custom_call" | custom-call | tf_op jit(solution)/shard_map/combine/pallas_call | solution.py:556
  61.3 12.8 %all_to_all.5.got_ref = bf16[16,128,128]{2,1,0:T(8,128)(2,1)S(1)} all-to-all(bf16[16,128,128]{2,1,0:T(8,128)(2,1)S(1)} %get-tuple-element.130), channel_id=1, replica_groups=mesh['px'=8,'py'=16] {'py'}, dimensions={0} | all-to-all | bytes 1048576 | tf_op jit(solution)/shard_map/all_to_all | solution.py:703
  74.0 1.1 %add_carries.1 = f32[32,16,128]{2,1,0:T(8,128)} custom-call(f32[32,16,128]{2,1,0:T(8,128)S(1)} %get-tuple-element.129.own_ref, bf16[16,128,128]{2,1,0:T(8,128)(2,1)S(1)} %all_to_all.5.got_ref, bf16[2,128,512]{2,1,0:T(8,128)(2,1)S(1)} %get-tuple-element.131.couple_ref), custom_call_target="tpu_custom_call" | custom-call | tf_op jit(solution)/shard_map/add_carries/pallas_call | solution.py:571
  (8 shorter events, 0.0 us)
Async XLA Ops:
  3.7 27.7 %collective-permute-start.1 = (bf16[16,5,16,256]{3,2,1,0:T(8,128)(2,1)S(1)}, bf16[16,5,16,256]{3,2,1,0:T(8,128)(2,1)S(1)}, u32[]{:S(2)}, u32[]{:S(2)}) collective-permute-start(bf16[16,5,16,256]{3,2,1,0:T(8,128)(2,1)S(1)} %get-tuple-element.68), channel_id=1, source_target_pairs={{0,15},{1,0},{2,1},{3,2},{4,3},{5,4},{6,5},{7,6},{8,7},{9,8},{10,9... | collective-permute-start | bytes 1966088 | tf_op jit(solution)/shard_map/ppermute | solution.py:586
  10.4 21.0 %collective-permute-start = (bf16[16,5,16,256]{3,2,1,0:T(8,128)(2,1)S(1)}, bf16[16,5,16,256]{3,2,1,0:T(8,128)(2,1)S(1)}, u32[]{:S(2)}, u32[]{:S(2)}) collective-permute-start(bf16[16,5,16,256]{3,2,1,0:T(8,128)(2,1)S(1)} %get-tuple-element.67.after_ref), channel_id=1, source_target_pairs={{0,1},{1,2},{2,3},{3,4},{4,5},{5,6},{6,7},{7,8},{8,9},{9,10},{10,1... | collective-permute-start | bytes 1966088 | tf_op jit(solution)/shard_map/ppermute | solution.py:586
  10.4 8.1 %collective-permute-start.2 = (bf16[21,32,256]{2,1,0:T(8,128)(2,1)S(1)}, bf16[21,32,256]{2,1,0:T(8,128)(2,1)S(1)}, u32[]{:S(2)}, u32[]{:S(2)}) collective-permute-start(bf16[21,32,256]{2,1,0:T(8,128)(2,1)S(1)} %get-tuple-element.69), channel_id=1, source_target_pairs={{0,16},{16,32},{32,48},{48,64},{64,80},{80,96},{96,112},{112,0},{1... | collective-permute-start | bytes 1032200 | tf_op jit(solution)/shard_map/ppermute | solution.py:586
  10.4 8.1 %collective-permute-start.3 = (bf16[21,32,256]{2,1,0:T(8,128)(2,1)S(1)}, bf16[21,32,256]{2,1,0:T(8,128)(2,1)S(1)}, u32[]{:S(2)}, u32[]{:S(2)}) collective-permute-start(bf16[21,32,256]{2,1,0:T(8,128)(2,1)S(1)} %get-tuple-element.70), channel_id=1, source_target_pairs={{0,112},{16,0},{32,16},{48,32},{64,48},{80,64},{96,80},{112,96},{1... | collective-permute-start | bytes 1032200 | tf_op jit(solution)/shard_map/ppermute | solution.py:586
  18.6 7.2 %collective-permute-start.5 = (bf16[6,16,256]{2,1,0:T(8,128)(2,1)S(1)}, bf16[6,16,256]{2,1,0:T(8,128)(2,1)S(1)}, u32[]{:S(2)}, u32[]{:S(2)}) collective-permute-start(bf16[6,16,256]{2,1,0:T(8,128)(2,1)S(1)} %get-tuple-element.86), channel_id=1, source_target_pairs={{0,15},{1,0},{2,1},{3,2},{4,3},{5,4},{6,5},{7,6},{8,7},{9,8},{10,9... | collective-permute-start | bytes 147464 | tf_op jit(solution)/shard_map/ppermute | solution.py:586
  24.0 7.4 %copy-start = (bf16[2,256,128]{2,1,0:T(8,128)(2,1)S(1)}, bf16[2,256,128]{2,1,0:T(8,128)(2,1)}, u32[]{:S(2)}) copy-start(bf16[2,256,128]{2,1,0:T(8,128)(2,1)} %constant.12.clone.fit_ref) | copy-start | bytes 393220
  24.0 7.4 %copy-start.1 = (s32[1,2]{1,0:T(1,128)S(1)}, s32[1,2]{1,0:T(1,128)}, u32[]{:S(2)}) copy-start(s32[1,2]{1,0:T(1,128)} %margin_ref.1) | copy-start | bytes 28
  24.0 7.4 %collective-permute-start.4 = (bf16[6,16,256]{2,1,0:T(8,128)(2,1)S(1)}, bf16[6,16,256]{2,1,0:T(8,128)(2,1)S(1)}, u32[]{:S(2)}, u32[]{:S(2)}) collective-permute-start(bf16[6,16,256]{2,1,0:T(8,128)(2,1)S(1)} %get-tuple-element.85), channel_id=1, source_target_pairs={{0,1},{1,2},{2,3},{3,4},{4,5},{5,6},{6,7},{7,8},{8,9},{9,10},{10,1... | collective-permute-start | bytes 147464 | tf_op jit(solution)/shard_map/ppermute | solution.py:586
  51.7 8.7 %collective-permute-start.6 = (f32[16,2816]{1,0:T(8,128)S(1)}, f32[16,2816]{1,0:T(8,128)S(1)}, u32[]{:S(2)}, u32[]{:S(2)}) collective-permute-start(f32[16,2816]{1,0:T(8,128)S(1)} %get-tuple-element.124), channel_id=1, source_target_pairs={{0,16},{16,32},{32,48},{48,64},{64,80},{80,96},{96,112},{112,0},{1... | collective-permute-start | bytes 540680 | tf_op jit(solution)/shard_map/ppermute | solution.py:586
  51.8 8.7 %collective-permute-start.7 = (f32[16,2816]{1,0:T(8,128)S(1)}, f32[16,2816]{1,0:T(8,128)S(1)}, u32[]{:S(2)}, u32[]{:S(2)}) collective-permute-start(f32[16,2816]{1,0:T(8,128)S(1)} %get-tuple-element.125), channel_id=1, source_target_pairs={{0,112},{16,0},{32,16},{48,32},{64,48},{80,64},{96,80},{112,96},{1... | collective-permute-start | bytes 540680 | tf_op jit(solution)/shard_map/ppermute | solution.py:586
  54.7 5.7 %collective-permute-start.8 = (bf16[16,2816]{1,0:T(8,128)(2,1)S(1)}, bf16[16,2816]{1,0:T(8,128)(2,1)S(1)}, u32[]{:S(2)}, u32[]{:S(2)}) collective-permute-start(bf16[16,2816]{1,0:T(8,128)(2,1)S(1)} %get-tuple-element.126), channel_id=1, source_target_pairs={{0,32},{16,48},{32,64},{48,80},{64,96},{80,112},{96,0},{112,16},{1... | collective-permute-start | bytes 270344 | tf_op jit(solution)/shard_map/ppermute | solution.py:586
  54.7 5.7 %collective-permute-start.9 = (bf16[16,2816]{1,0:T(8,128)(2,1)S(1)}, bf16[16,2816]{1,0:T(8,128)(2,1)S(1)}, u32[]{:S(2)}, u32[]{:S(2)}) collective-permute-start(bf16[16,2816]{1,0:T(8,128)(2,1)S(1)} %get-tuple-element.127), channel_id=1, source_target_pairs={{0,96},{16,112},{32,0},{48,16},{64,32},{80,48},{96,64},{112,80},{1... | collective-permute-start | bytes 270344 | tf_op jit(solution)/shard_map/ppermute | solution.py:586

commit v7 on v6

--- a/solution.py
+++ b/solution.py
@@ -306,7 +306,7 @@
                 ref[x, beyond] = jnp.concatenate([kh[m : m + 4], kl[m : m + 4]], axis=0)
         return carry
 
-    lax.fori_loop(0, BX // 4, halo_rows, 0)
+    lax.fori_loop(0, BX // 4, halo_rows, 0, unroll=2)
     dest = (u_s, kh_s, v0_s, v1_s, v2_s)
     none = jnp.zeros((1, NZ), f32)
     for base, corner, scale, near in ((0, 0, from_low_x, range(1, W)), (BX + W, 3, from_high_x, range(W - 1))):
@@ -349,7 +349,7 @@
         c_s[x, BY - 8 : BY] = c_s[x, BY - 8 : BY] - up
         return k_next, kx
 
-    lax.fori_loop(0, EX, halo_coefficients, (kh_s[0], jnp.zeros((8, NZ), f32)), unroll=8)
+    lax.fori_loop(0, EX, halo_coefficients, (kh_s[0], jnp.zeros((8, NZ), f32)), unroll=12)
 
     row = lax.broadcasted_iota(jnp.int32, (EY, NZ), 0)
     row_mask = jnp.where(row < BY, 1.0, jnp.where(row < BY + W, from_high_y, from_low_y))

time: 75.9 us -> 75.6 us (level)
  no operation moved by 1% of the time
where the time goes in v7:
time: 75.6 us; the launch traced here: 74.9 us
  Pallas kernels  30.5 us (40%)
  starting transfers between devices  21.2 us (28%)
  blocking collectives  12.8 us (17%)
  waiting for transfers between devices  9.63 us (13%)
    ppermute x10, starting transfers between devices, shift(): return lax.ppermute(a, axis, ring(lax.axis_size(axis), d))  21.2 us
    pallas_call x1, Pallas kernels, time_steps(): pl.pallas_call(functools.partial(stencil_body, *counts), out_shape=[jax.S...  20 us
    all_to_all x1, blocking collectives, per_device(): got = lax.all_to_all(carries, 'py', split_axis=0, concat_axis=0, tiled=True)  12.8 us
    ppermute x10, waiting for transfers between devices, shift(): return lax.ppermute(a, axis, ring(lax.axis_size(axis), d))  9.63 us
    pallas_call x1, Pallas kernels, own_coefficients(): pl.pallas_call(own_body, out_shape=[pltpu.VMEM((EX, EY, NZ), f32)] * (KEP...  5.16 us
    pallas_call x1, Pallas kernels, halo_parts(): pl.pallas_call(pack_body, out_shape=[jax.ShapeDtypeStruct(s, bf16) for s...  3.09 us
  transfers between devices with their start and end apart: 10, of which 3 were waited for; matrix products, arithmetic and copies ran while one was open for 0% of the time, Pallas kernels for 7%

profile of v7, /device:TPU:0, one launch (start us, length us, event | category | flops | bytes accessed | tf_op | source)
XLA Modules:
  0.0 74.9 jit_solution(3734049782319243292)
XLA Ops:
  0.6 3.1 %pack_faces.1 = (bf16[16,5,16,256]{3,2,1,0:T(8,128)(2,1)S(1)}, bf16[16,5,16,256]{3,2,1,0:T(8,128)(2,1)S(1)}, bf16[21,32,256]{2,1,0:T(8,128)(2,1)S(1)}, bf16[21,32,256]{2,1,0:T(8,128)(2,1)S(1)}) custom-call(s32[1,2]{1,0:T(1,128)} %margin_ref.1, f32[64,32,256]{2,1,0:T(8,128)} %f_hbm.3, bf16[64,32,256]{2,1,0:T(8,128)(2,1)} %k_hbm.3, bf16[3,64,32,256]{3,2,1,0:T(8,128)(2,1)} %v_hbm.3), custom_call_target="tpu_custom_call" | custom-call | tf_op jit(solution)/shard_map/pack_faces/pallas_call | solution.py:662
  3.7 6.6 %collective-permute-start.1 = (bf16[16,5,16,256]{3,2,1,0:T(8,128)(2,1)S(1)}, bf16[16,5,16,256]{3,2,1,0:T(8,128)(2,1)S(1)}, u32[]{:S(2)}, u32[]{:S(2)}) collective-permute-start(bf16[16,5,16,256]{3,2,1,0:T(8,128)(2,1)S(1)} %get-tuple-element.68), channel_id=1, source_target_pairs={{0,15},{1,0},{2,1},{3,2},{4,3},{5,4},{6,5},{7,6},{8,7},{9,8},{10,9... | collective-permute-start | bytes 1966088 | tf_op jit(solution)/shard_map/ppermute | solution.py:586
  10.4 0.0 collective-permute-start
  10.4 0.0 collective-permute-start.2
  10.4 3.0 %collective-permute-start.3 = (bf16[21,32,256]{2,1,0:T(8,128)(2,1)S(1)}, bf16[21,32,256]{2,1,0:T(8,128)(2,1)S(1)}, u32[]{:S(2)}, u32[]{:S(2)}) collective-permute-start(bf16[21,32,256]{2,1,0:T(8,128)(2,1)S(1)} %get-tuple-element.70), channel_id=1, source_target_pairs={{0,112},{16,0},{32,16},{48,32},{64,48},{80,64},{96,80},{112,96},{1... | collective-permute-start | bytes 1032200 | tf_op jit(solution)/shard_map/ppermute | solution.py:586
  13.3 5.2 %own_coefficients.1 = (f32[72,40,256]{2,1,0:T(8,128)S(1)}, f32[72,40,256]{2,1,0:T(8,128)S(1)}, f32[72,40,256]{2,1,0:T(8,128)S(1)}, f32[72,40,256]{2,1,0:T(8,128)...) custom-call(f32[64,32,256]{2,1,0:T(8,128)} %f_hbm.3, ...), custom_call_target="tpu_custom_call" | custom-call | tf_op jit(solution)/shard_map/own_coefficients/pallas_call | solution.py:497
  18.5 0.0 collective-permute-done.2.xl_ref
  18.5 0.0 collective-permute-done.3.xh_ref
  18.5 0.1 pack_corners.1
  18.6 5.4 %collective-permute-start.5 = (bf16[6,16,256]{2,1,0:T(8,128)(2,1)S(1)}, bf16[6,16,256]{2,1,0:T(8,128)(2,1)S(1)}, u32[]{:S(2)}, u32[]{:S(2)}) collective-permute-start(bf16[6,16,256]{2,1,0:T(8,128)(2,1)S(1)} %get-tuple-element.86), channel_id=1, source_target_pairs={{0,15},{1,0},{2,1},{3,2},{4,3},{5,4},{6,5},{7,6},{8,7},{9,8},{10,9... | collective-permute-start | bytes 147464 | tf_op jit(solution)/shard_map/ppermute | solution.py:586
  24.0 0.3 x_planes.1
  24.3 1.4 %collective-permute-done.5.ch_ref = bf16[6,16,256]{2,1,0:T(8,128)(2,1)S(1)} collective-permute-done((bf16[6,16,256]{2,1,0:T(8,128)(2,1)S(1)}, bf16[6,16,256]{2,1,0:T(8,128)(2,1)S(1)}, u32[]{:S(2)}, u32[]{:S(2)}) %collective-permute-start.5) | collective-permute-done | bytes 49184 | tf_op jit(solution)/shard_map/ppermute | solution.py:586
  25.7 5.7 %collective-permute-done.4.cl_ref = bf16[6,16,256]{2,1,0:T(8,128)(2,1)S(1)} collective-permute-done((bf16[6,16,256]{2,1,0:T(8,128)(2,1)S(1)}, bf16[6,16,256]{2,1,0:T(8,128)(2,1)S(1)}, u32[]{:S(2)}, u32[]{:S(2)}) %collective-permute-start.4) | collective-permute-done | bytes 49184 | tf_op jit(solution)/shard_map/ppermute | solution.py:586
  31.4 0.0 collective-permute-done.1.yh_ref
  31.4 20.0 %time_steps.1 = (f32[64,32,256]{2,1,0:T(8,128)}, f32[22,64,128]{2,1,0:T(8,128)S(1)}, f32[16,2816]{1,0:T(8,128)S(1)}, f32[16,2816]{1,0:T(8,128)S(1)}, bf16[16,281...) custom-call(s32[1,2]{1,0:T(1,128)S(1)} %copy-done.1, ...), custom_call_target="tpu_custom_call", output_to_operand_aliasing={{8}: (13, {}), {9}: (14, {}), {10}: (15, {}), {11}: (16, {}... | custom-call | tf_op jit(solution)/shard_map/time_steps/pallas_call | solution.py:533
  51.4 0.0 collective-permute-start.6
  51.5 2.9 %collective-permute-start.7 = (f32[16,2816]{1,0:T(8,128)S(1)}, f32[16,2816]{1,0:T(8,128)S(1)}, u32[]{:S(2)}, u32[]{:S(2)}) collective-permute-start(f32[16,2816]{1,0:T(8,128)S(1)} %get-tuple-element.125), channel_id=1, source_target_pairs={{0,112},{16,0},{32,16},{48,32},{64,48},{80,64},{96,80},{112,96},{1... | collective-permute-start | bytes 540680 | tf_op jit(solution)/shard_map/ppermute | solution.py:586
  54.4 3.2 %collective-permute-start.9 = (bf16[16,2816]{1,0:T(8,128)(2,1)S(1)}, bf16[16,2816]{1,0:T(8,128)(2,1)S(1)}, u32[]{:S(2)}, u32[]{:S(2)}) collective-permute-start(bf16[16,2816]{1,0:T(8,128)(2,1)S(1)} %get-tuple-element.127), channel_id=1, source_target_pairs={{0,96},{16,112},{32,0},{48,16},{64,32},{80,48},{96,64},{112,80},{1... | collective-permute-start | bytes 270344 | tf_op jit(solution)/shard_map/ppermute | solution.py:586
  57.6 2.5 %collective-permute-done.8.lo2_ref = bf16[16,2816]{1,0:T(8,128)(2,1)S(1)} collective-permute-done((bf16[16,2816]{1,0:T(8,128)(2,1)S(1)}, bf16[16,2816]{1,0:T(8,128)(2,1)S(1)}, u32[]{:S(2)}, u32[]{:S(2)}) %collective-permute-start.8) | collective-permute-done | bytes 90144 | tf_op jit(solution)/shard_map/ppermute | solution.py:586
  60.2 0.0 collective-permute-done.6.lo_ref
  60.2 0.0 collective-permute-done.7.hi_ref
  60.2 0.8 %combine.1 = (f32[32,16,128]{2,1,0:T(8,128)S(1)}, bf16[16,128,128]{2,1,0:T(8,128)(2,1)S(1)}) custom-call(f32[22,64,128]{2,1,0:T(8,128)S(1)} %get-tuple-element.123.zt_ref, f32[16,2816]{1,0:T(8,128)S(1)} %collective-permute-done.6.lo_ref, f32[16,2816]{1,0:T(8,128)S(1)} %collective-permute-done.7.hi_ref, bf16[16,2816]{1,0:T(8,128)(2,1)S(1)} %collective-permute-done.8.lo2_ref, ...), custom_call_target="tpu_custom_call" | custom-call | tf_op jit(solution)/shard_map/combine/pallas_call | solution.py:556
  61.0 12.8 %all_to_all.5.got_ref = bf16[16,128,128]{2,1,0:T(8,128)(2,1)S(1)} all-to-all(bf16[16,128,128]{2,1,0:T(8,128)(2,1)S(1)} %get-tuple-element.130), channel_id=1, replica_groups=mesh['px'=8,'py'=16] {'py'}, dimensions={0} | all-to-all | bytes 1048576 | tf_op jit(solution)/shard_map/all_to_all | solution.py:703
  73.7 1.1 %add_carries.1 = f32[32,16,128]{2,1,0:T(8,128)} custom-call(f32[32,16,128]{2,1,0:T(8,128)S(1)} %get-tuple-element.129.own_ref, bf16[16,128,128]{2,1,0:T(8,128)(2,1)S(1)} %all_to_all.5.got_ref, bf16[2,128,512]{2,1,0:T(8,128)(2,1)S(1)} %get-tuple-element.131.couple_ref), custom_call_target="tpu_custom_call" | custom-call | tf_op jit(solution)/shard_map/add_carries/pallas_call | solution.py:571
  (8 shorter events, 0.0 us)
Async XLA Ops:
  3.7 27.7 %collective-permute-start.1 = (bf16[16,5,16,256]{3,2,1,0:T(8,128)(2,1)S(1)}, bf16[16,5,16,256]{3,2,1,0:T(8,128)(2,1)S(1)}, u32[]{:S(2)}, u32[]{:S(2)}) collective-permute-start(bf16[16,5,16,256]{3,2,1,0:T(8,128)(2,1)S(1)} %get-tuple-element.68), channel_id=1, source_target_pairs={{0,15},{1,0},{2,1},{3,2},{4,3},{5,4},{6,5},{7,6},{8,7},{9,8},{10,9... | collective-permute-start | bytes 1966088 | tf_op jit(solution)/shard_map/ppermute | solution.py:586
  10.4 21.0 %collective-permute-start = (bf16[16,5,16,256]{3,2,1,0:T(8,128)(2,1)S(1)}, bf16[16,5,16,256]{3,2,1,0:T(8,128)(2,1)S(1)}, u32[]{:S(2)}, u32[]{:S(2)}) collective-permute-start(bf16[16,5,16,256]{3,2,1,0:T(8,128)(2,1)S(1)} %get-tuple-element.67.after_ref), channel_id=1, source_target_pairs={{0,1},{1,2},{2,3},{3,4},{4,5},{5,6},{6,7},{7,8},{8,9},{9,10},{10,1... | collective-permute-start | bytes 1966088 | tf_op jit(solution)/shard_map/ppermute | solution.py:586
  10.4 8.1 %collective-permute-start.2 = (bf16[21,32,256]{2,1,0:T(8,128)(2,1)S(1)}, bf16[21,32,256]{2,1,0:T(8,128)(2,1)S(1)}, u32[]{:S(2)}, u32[]{:S(2)}) collective-permute-start(bf16[21,32,256]{2,1,0:T(8,128)(2,1)S(1)} %get-tuple-element.69), channel_id=1, source_target_pairs={{0,16},{16,32},{32,48},{48,64},{64,80},{80,96},{96,112},{112,0},{1... | collective-permute-start | bytes 1032200 | tf_op jit(solution)/shard_map/ppermute | solution.py:586
  10.4 8.1 %collective-permute-start.3 = (bf16[21,32,256]{2,1,0:T(8,128)(2,1)S(1)}, bf16[21,32,256]{2,1,0:T(8,128)(2,1)S(1)}, u32[]{:S(2)}, u32[]{:S(2)}) collective-permute-start(bf16[21,32,256]{2,1,0:T(8,128)(2,1)S(1)} %get-tuple-element.70), channel_id=1, source_target_pairs={{0,112},{16,0},{32,16},{48,32},{64,48},{80,64},{96,80},{112,96},{1... | collective-permute-start | bytes 1032200 | tf_op jit(solution)/shard_map/ppermute | solution.py:586
  18.6 7.2 %collective-permute-start.5 = (bf16[6,16,256]{2,1,0:T(8,128)(2,1)S(1)}, bf16[6,16,256]{2,1,0:T(8,128)(2,1)S(1)}, u32[]{:S(2)}, u32[]{:S(2)}) collective-permute-start(bf16[6,16,256]{2,1,0:T(8,128)(2,1)S(1)} %get-tuple-element.86), channel_id=1, source_target_pairs={{0,15},{1,0},{2,1},{3,2},{4,3},{5,4},{6,5},{7,6},{8,7},{9,8},{10,9... | collective-permute-start | bytes 147464 | tf_op jit(solution)/shard_map/ppermute | solution.py:586
  24.0 7.4 %copy-start = (bf16[2,256,128]{2,1,0:T(8,128)(2,1)S(1)}, bf16[2,256,128]{2,1,0:T(8,128)(2,1)}, u32[]{:S(2)}) copy-start(bf16[2,256,128]{2,1,0:T(8,128)(2,1)} %constant.12.clone.fit_ref) | copy-start | bytes 393220
  24.0 7.4 %copy-start.1 = (s32[1,2]{1,0:T(1,128)S(1)}, s32[1,2]{1,0:T(1,128)}, u32[]{:S(2)}) copy-start(s32[1,2]{1,0:T(1,128)} %margin_ref.1) | copy-start | bytes 28
  24.0 7.4 %collective-permute-start.4 = (bf16[6,16,256]{2,1,0:T(8,128)(2,1)S(1)}, bf16[6,16,256]{2,1,0:T(8,128)(2,1)S(1)}, u32[]{:S(2)}, u32[]{:S(2)}) collective-permute-start(bf16[6,16,256]{2,1,0:T(8,128)(2,1)S(1)} %get-tuple-element.85), channel_id=1, source_target_pairs={{0,1},{1,2},{2,3},{3,4},{4,5},{5,6},{6,7},{7,8},{8,9},{9,10},{10,1... | collective-permute-start | bytes 147464 | tf_op jit(solution)/shard_map/ppermute | solution.py:586
  51.4 8.7 %collective-permute-start.6 = (f32[16,2816]{1,0:T(8,128)S(1)}, f32[16,2816]{1,0:T(8,128)S(1)}, u32[]{:S(2)}, u32[]{:S(2)}) collective-permute-start(f32[16,2816]{1,0:T(8,128)S(1)} %get-tuple-element.124), channel_id=1, source_target_pairs={{0,16},{16,32},{32,48},{48,64},{64,80},{80,96},{96,112},{112,0},{1... | collective-permute-start | bytes 540680 | tf_op jit(solution)/shard_map/ppermute | solution.py:586
  51.5 8.7 %collective-permute-start.7 = (f32[16,2816]{1,0:T(8,128)S(1)}, f32[16,2816]{1,0:T(8,128)S(1)}, u32[]{:S(2)}, u32[]{:S(2)}) collective-permute-start(f32[16,2816]{1,0:T(8,128)S(1)} %get-tuple-element.125), channel_id=1, source_target_pairs={{0,112},{16,0},{32,16},{48,32},{64,48},{80,64},{96,80},{112,96},{1... | collective-permute-start | bytes 540680 | tf_op jit(solution)/shard_map/ppermute | solution.py:586
  54.4 5.7 %collective-permute-start.8 = (bf16[16,2816]{1,0:T(8,128)(2,1)S(1)}, bf16[16,2816]{1,0:T(8,128)(2,1)S(1)}, u32[]{:S(2)}, u32[]{:S(2)}) collective-permute-start(bf16[16,2816]{1,0:T(8,128)(2,1)S(1)} %get-tuple-element.126), channel_id=1, source_target_pairs={{0,32},{16,48},{32,64},{48,80},{64,96},{80,112},{96,0},{112,16},{1... | collective-permute-start | bytes 270344 | tf_op jit(solution)/shard_map/ppermute | solution.py:586
  54.4 5.7 %collective-permute-start.9 = (bf16[16,2816]{1,0:T(8,128)(2,1)S(1)}, bf16[16,2816]{1,0:T(8,128)(2,1)S(1)}, u32[]{:S(2)}, u32[]{:S(2)}) collective-permute-start(bf16[16,2816]{1,0:T(8,128)(2,1)S(1)} %get-tuple-element.127), channel_id=1, source_target_pairs={{0,96},{16,112},{32,0},{48,16},{64,32},{80,48},{96,64},{112,80},{1... | collective-permute-start | bytes 270344 | tf_op jit(solution)/shard_map/ppermute | solution.py:586
